TPU v7x, 32 devices: a whole 2x2x4 slice. The times are simulated.
32 devices in a mesh: gen: 16 (over z, y, core), tp: 2 (over x).
Axes of the slice: x: 2, y: 2, z: 4, core: 2. Of those that a mesh axis runs over, the one named last changes fastest.
Arguments:
- tokens_in: bfloat16 [2048, 5120], P('gen', 'tp'), may hold values from -6 to 6
- w_kv: bfloat16 [5120, 2048], P('tp'), may hold values from -0.078125 to 0.078125
- queries: bfloat16 [1024, 2, 40, 128], P('gen', None, 'tp'), may hold values from -8 to 8
- k_cache: bfloat16 [896, 8, 64, 128], P('gen', 'tp'), may hold values from -8 to 8
- v_cache: bfloat16 [896, 8, 64, 128], P('gen', 'tp'), may hold values from -5 to 5
- page_table: int32 [1024, 32], P('gen'), may hold values from 0 to 55, as said below
- lengths: int32 [1024], P('gen'), may hold values from 1 to 2048, as said below
- move_dest: int32 [256, 1], replicated, may hold values from 0 to 15; in each aligned block of 16 rows (0 to 15, 16 to 31, ...) at most 2 rows name the same one
- move_page: int32 [256], replicated, may hold values from 0 to 55
- move_seq: int32 [256], replicated, may hold values from 0 to 63
Outputs:
- attended: bfloat16 [1024, 2, 40, 128], P('gen', None, 'tp')
- new_kv: bfloat16 [2048, 2048], P('gen', 'tp')
Inputs may be any that keep to these rules, and one draw needn't show every extreme that they name: `page_table`: each row names 32 different pages. `lengths`: some sequence has exactly 2048 positions in every draw. `move_dest`: rows r * 16 to (r + 1) * 16 - 1 are the moves of source device r; among one source's rows no destination appears more than 2 times, a bound that some block reaches.
All inputs are finite; a program needn't handle non-finite values.
Results may differ from a plain program's by a relative error of at most 0.0043.
Values may be sent and summed in bfloat16 or wider, within the bound.
No kernel may reach another device: no remote copies, remote signals or barrier semaphores. Data moves between devices by JAX's collectives and lax.ppermute only.
A program may use at most 192 MiB of HBM per device.

v0:
```python
import math

import jax
import jax.numpy as jnp
from jax import lax
from jax.sharding import PartitionSpec as P

MAXP = 32
CAP = 2


NEGATIVE = -1e30


def move_rank(destinations):
    position = jnp.arange(destinations.shape[-1])
    earlier = position[None, :] < position[:, None]
    same_dest = destinations[..., :, None] == destinations[..., None, :]
    return jnp.sum(jnp.where(same_dest & earlier, 1, 0), axis=-1).astype(jnp.int32)


def attend_partial(slot_query, slot_keys, slot_values, score_scale):
    scores = (
        jnp.einsum(
            "...crd,...cpd->...crp", slot_query, slot_keys, preferred_element_type=jnp.float32
        )
        * score_scale
    )
    slot_max = jnp.max(scores, axis=-1)
    weights = jnp.exp(scores - slot_max[..., None]).astype(jnp.bfloat16)
    weight_sum = jnp.sum(weights.astype(jnp.float32), axis=-1)
    summed = jnp.einsum(
        "...crp,...cpd->...crd", weights, slot_values, preferred_element_type=jnp.float32
    )
    return (slot_max, weight_sum, summed)


def per_device(
    tokens_in, w_kv, queries, k_cache, v_cache, page_table, lengths, move_dest, move_page, move_seq
):
    groups = lax.axis_size("gen")
    own_index = lax.axis_index("gen")
    seq_dev, step_count, heads_dev, head_dim = queries.shape
    pool_size, kv_dev, page_len, _ = k_cache.shape
    per_group = heads_dev // kv_dev
    query_count = step_count * per_group
    per_source = move_dest.shape[0] // groups
    slot_count = groups * CAP
    score_scale = 1.0 / math.sqrt(head_dim)
    fresh_kv = lax.psum_scatter(
        lax.dot_general(
            w_kv, tokens_in, (((0,), (1,)), ((), ())), preferred_element_type=jnp.float32
        ),
        "tp",
        scatter_dimension=0,
        tiled=True,
    ).T
    new_kv = fresh_kv.astype(jnp.bfloat16)
    new_parts = new_kv.reshape(seq_dev, step_count, kv_dev, 2, head_dim)
    new_keys = new_parts[:, :, :, 0]
    new_values = new_parts[:, :, :, 1]
    query_rows = queries.reshape(seq_dev, step_count, kv_dev, per_group, head_dim).transpose(
        0, 2, 1, 3, 4
    )
    query_rows = query_rows.reshape(seq_dev, kv_dev, query_count, head_dim)
    destinations = move_dest.reshape(groups, per_source)
    page_ids = move_page.reshape(groups, per_source)
    owner_ids = move_seq.reshape(groups, per_source)
    move_ranks = move_rank(destinations)
    capacity = jnp.arange(CAP)
    matches = (
        (destinations[:, :, None] == own_index)
        & (move_ranks[:, :, None] == capacity[None, None, :])
    ).astype(jnp.int32)
    arrived = jnp.sum(matches, axis=1).reshape(slot_count)
    owner_seq = jnp.sum(matches * owner_ids[:, :, None], axis=1).reshape(slot_count)
    slot_query = query_rows[owner_seq]
    my_dests = lax.dynamic_index_in_dim(destinations, own_index, 0, keepdims=False)
    my_ranks = lax.dynamic_index_in_dim(move_ranks, own_index, 0, keepdims=False)
    my_pages = lax.dynamic_index_in_dim(page_ids, own_index, 0, keepdims=False)
    targets = jnp.arange(groups)
    outgoing = (
        (my_dests[:, None, None] == targets[None, :, None])
        & (my_ranks[:, None, None] == capacity[None, None, :])
    ).astype(jnp.int32)
    sent_flag = jnp.sum(outgoing, axis=0).reshape(slot_count)
    send_page = jnp.sum(outgoing * my_pages[:, None, None], axis=0).reshape(slot_count)
    sent_mask = (sent_flag > 0)[:, None, None, None]
    send_keys = jnp.where(sent_mask, k_cache[send_page], jnp.zeros((), k_cache.dtype))
    send_values = jnp.where(sent_mask, v_cache[send_page], jnp.zeros((), v_cache.dtype))
    moved_keys, moved_values = (
        lax.all_to_all(send_keys, "gen", split_axis=0, concat_axis=0, tiled=True),
        lax.all_to_all(send_values, "gen", split_axis=0, concat_axis=0, tiled=True),
    )
    slot_max, slot_total, slot_sum = attend_partial(
        slot_query, moved_keys, moved_values, score_scale
    )
    landed = arrived > 0
    slot_max = jnp.where(landed[:, None, None], slot_max, NEGATIVE)
    member = (owner_seq[None, :] == jnp.arange(seq_dev)[:, None]) & landed[None, :]
    moved_max = jnp.max(jnp.where(member[:, :, None, None], slot_max[None], NEGATIVE), axis=1)
    positions = jnp.arange(MAXP)[:, None] * page_len + jnp.arange(page_len)[None, :]
    inside = (positions[None] < lengths[:, None, None]).astype(jnp.float32)
    chosen = (page_table[:, :, None] == jnp.arange(pool_size)[None, None, :]).astype(jnp.float32)
    usage_count = jnp.einsum("smp,smq->spq", chosen, inside)
    visible = (usage_count > 0.5)[:, None, None]
    local_scores = (
        jnp.einsum("scrd,pcqd->scrpq", query_rows, k_cache, preferred_element_type=jnp.float32)
        * score_scale
    )
    local_max = jnp.max(jnp.where(visible, local_scores, NEGATIVE), axis=(3, 4))
    new_scores = (
        jnp.einsum("scrd,sicd->scri", query_rows, new_keys, preferred_element_type=jnp.float32)
        * score_scale
    )
    row_step = jnp.arange(query_count) // per_group
    causal = jnp.arange(step_count)[None, :] <= row_step[:, None]
    new_max = jnp.max(jnp.where(causal, new_scores, NEGATIVE), axis=-1)
    biggest = jnp.maximum(jnp.maximum(local_max, new_max), moved_max)
    local_weights = jnp.where(
        visible, jnp.exp(local_scores - biggest[..., None, None]), 0.0
    ).astype(jnp.bfloat16)
    local_total = jnp.sum(local_weights.astype(jnp.float32), axis=(3, 4))
    local_sum = jnp.einsum(
        "scrpq,pcqd->scrd", local_weights, v_cache, preferred_element_type=jnp.float32
    )
    new_weights = jnp.where(causal, jnp.exp(new_scores - biggest[..., None]), 0.0)
    new_total = jnp.sum(new_weights, axis=-1)
    new_sum = jnp.einsum(
        "scri,sicd->scrd",
        new_weights,
        new_values.astype(jnp.float32),
        precision=lax.Precision.HIGHEST,
    )
    factor = jnp.exp(slot_max - biggest[owner_seq])
    member_f = member.astype(jnp.float32)
    moved_total = jnp.einsum(
        "sn,ncr->scr", member_f, factor * slot_total, precision=lax.Precision.HIGHEST
    )
    moved_sum = jnp.einsum(
        "sn,ncrd->scrd", member_f, factor[..., None] * slot_sum, precision=lax.Precision.HIGHEST
    )
    combined = (local_sum + moved_sum + new_sum) / (local_total + moved_total + new_total)[
        ..., None
    ]
    attended = combined.reshape(seq_dev, kv_dev, step_count, per_group, head_dim).transpose(
        0, 2, 1, 3, 4
    )
    attended = attended.reshape(seq_dev, step_count, heads_dev, head_dim).astype(jnp.bfloat16)
    return (attended, new_kv)


def solution(mesh):
    return jax.shard_map(
        per_device,
        mesh=mesh,
        in_specs=(
            P("gen", "tp"),
            P("tp", None),
            P("gen", None, "tp", None),
            P("gen", "tp", None, None),
            P("gen", "tp", None, None),
            P("gen", None),
            P("gen"),
            P(),
            P(),
            P(),
        ),
        out_specs=(P("gen", None, "tp", None), P("gen", "tp")),
        check_vma=False,
    )
```

profile of v0, /device:TPU:0, one launch (start us, length us, event | category | flops | bytes accessed | tf_op | source)
XLA Modules:
  0.0 175.1 jit_solution(12613292075043482657)
XLA Ops:
  7.2 0.0 reduce-scatter.2.cloned.1.call-start
  7.3 1.0 copy-done
  8.3 7.9 %fusion.47 = f32[2048,128]{1,0:T(8,128)} fusion(bf16[2560,2048]{1,0:T(8,128)(2,1)} %param.11, bf16[128,2560]{1,0:T(8,128)(2,1)S(1)} %copy-done), kind=kOutput, calls=%fused_computation.97 | convolution fusion | flops 1342177280 | bytes 12189696 | tf_op jit(solution)/shard_map/dot_general | solution.py:51
  16.1 0.0 reduce-scatter.2.cloned.1.call-update
  16.2 0.5 broadcast.203
  16.7 0.7 reduce.3
  17.4 0.1 broadcast_in_dim_reshape.2
  17.5 0.1 iota_compare_fusion.4
  17.5 0.4 select_reduce_fusion.2
  18.0 0.1 reshape.286
  18.1 0.1 fusion.27
  18.2 0.1 copy.160
  18.3 0.1 reshape.287
  18.4 0.1 mul.76
  18.5 0.2 convert_reduce_fusion.2
  18.6 0.1 copy.159
  18.7 0.1 gt.35
  18.8 0.1 copy.155
  18.9 0.1 reshape.285
  19.0 3.0 %gather_fusion.3 = bf16[32,4,64,128]{3,2,1,0:T(8,128)(2,1)S(1)} fusion(bf16[56,4,64,128]{3,2,1,0:T(8,128)(2,1)} %param.14, s32[1024]{0:T(1024)S(1)} %pad_clamp_fusion), kind=kCustom, calls=%fused_computation.3 | custom fusion | bytes 4194432 | tf_op jit(solution)/shard_map/gather | solution.py:90
  22.0 4.2 %gather_fusion.1 = bf16[32,4,64,128]{3,2,1,0:T(8,128)(2,1)} fusion(bf16[56,4,64,128]{3,2,1,0:T(8,128)(2,1)} %param.13, s32[1024]{0:T(1024)S(1)} %pad_clamp_fusion), kind=kCustom, calls=%fused_computation.1 | custom fusion | bytes 4194432 | tf_op jit(solution)/shard_map/gather | solution.py:89
  26.3 3.9 %broadcast_select_fusion = (bf16[32,4,64,128]{3,2,1,0:T(8,128)(2,1)}, bf16[32,4,64,128]{3,2,1,0:T(8,128)(2,1)}) fusion(bf16[32,4,64,128]{3,2,1,0:T(8,128)(2,1)S(1)} %gather_fusion.3, pred[32]{0:T(512)(128)(4,1)S(1)} %gt.35, bf16[32,4,64,128]{3,2,1,0:T(8,128)(2,1)} %gather_fusion.1), kind=kLoop, calls=%fused_computation.16 | loop fusion | flops 2097152 | bytes 8388640 | tf_op jit(solution)/shard_map/jit(_where)/select_n | solution.py:90
  30.2 7.9 %all-to-all-start = ((bf16[32,4,64,128]{3,2,1,0:T(8,128)(2,1)}), bf16[32,4,64,128]{3,2,1,0:T(8,128)(2,1)S(1)}, u32[]{:S(2)}, u32[]{:S(2)}) async-start(bf16[32,4,64,128]{3,2,1,0:T(8,128)(2,1)} %get-tuple-element.25), calls=%async_computation.1 | async-start | bytes 4194304 | tf_op jit(solution)/shard_map/all_to_all | solution.py:92
  38.1 0.6 iota_compare_fusion.7
  38.7 0.1 iota_add_fusion
  38.8 0.1 copy.145
  38.9 2.1 %convolution_compare_fusion = pred[64,56,64]{2,1,0:T(8,128)(4,1)} fusion(s32[32,64]{1,0:T(8,128)S(1)} %iota_add_fusion, s32[64,32]{1,0:T(8,128)S(1)} %copy.145, s32[64]{0:T(128)S(1)} %copy-done.13), kind=kOutput, calls=%fused_computation.22 | convolution fusion | flops 15155200 | bytes 246016 | tf_op jit(solution)/shard_map/smp,smq->spq/dot_general | solution.py:105
  40.9 0.1 eq.120
  41.0 0.1 copy.156
  41.1 0.1 gt.33
  41.2 2.6 %copy.146 = pred[64,56,64]{0,2,1:T(8,128)(4,1)S(1)} copy(pred[64,56,64]{2,1,0:T(8,128)(4,1)} %convolution_compare_fusion) | data formatting | bytes 458752 | tf_op jit(solution)/shard_map/gt | solution.py:106
  43.8 1.2 copy.147
  45.1 0.1 copy.148
  45.1 0.8 copy-done.1
  46.0 1.3 copy.158
  47.3 1.9 %gather_fusion = bf16[32,4,10,128]{3,1,2,0:T(4,128)(2,1)S(1)} fusion(bf16[64,4,10,128]{3,1,2,0:T(4,128)(2,1)} %copy.158, s32[1024]{0:T(1024)S(1)} %pad_clamp_fusion.1), kind=kCustom, calls=%fused_computation | custom fusion | bytes 655488 | tf_op jit(solution)/shard_map/gather | solution.py:77
  49.2 0.1 fusion.30
  49.3 30.1 %fusion = (f32[64,4,10]{0,2,1:T(8,128)}, f32[4,56,64,64,10]{3,2,4,1,0:T(8,128)}) fusion(pred[64,56,64]{0,2,1:T(8,128)(4,1)S(1)} %copy.146, bf16[64,4,10,128,1]{3,0,2,4,1:T(8,128)(2,1)} %bitcast.83, bf16[56,4,64,128]{3,2,1,0:T(8,128)(2,1)} %param.13), kind=kOutput, calls=%fused_computation.6 | convolution fusion | flops 2376332800 | bytes 41265152 | tf_op jit(solution)/shard_map/scrd,pcqd->scrpq/dot_general | solution.py:108
  79.4 1.8 %convert_bitcast_fusion = bf16[128,1024]{0,1:T(8,128)(2,1)} fusion(f32[1024,128]{1,0:T(8,128)} %reduce-scatter.2.cloned.1.call-done), kind=kLoop, calls=%fused_computation.43 | loop fusion | flops 131072 | bytes 786432 | tf_op jit(solution)/shard_map/convert_element_type | solution.py:58
  81.2 1.8 %copy.150 = bf16[128,1024]{1,0:T(8,128)(2,1)} copy(bf16[128,1024]{0,1:T(8,128)(2,1)} %convert_bitcast_fusion) | data formatting | bytes 524288 | tf_op jit(solution)/shard_map/convert_element_type | solution.py:58
  83.0 1.8 %reshape.284 = bf16[64,2,4,2,128]{4,3,2,1,0:T(2,128)(2,1)} reshape(bf16[128,1024]{1,0:T(8,128)(2,1)} %copy.150) | data formatting | bytes 524288 | tf_op jit(solution)/shard_map/reshape | solution.py:59
  84.8 2.2 %fusion.45 = (bf16[64,2,4,1,128]{4,3,2,1,0:T(2,128)(2,1)}, bf16[64,2,4,1,128]{4,3,2,1,0:T(2,128)(2,1)S(1)}) fusion(bf16[64,2,4,2,128]{4,3,2,1,0:T(2,128)(2,1)} %reshape.284), kind=kLoop, calls=%fused_computation.95 | loop fusion | bytes 524288 | tf_op jit(solution)/shard_map/slice | solution.py:61
  87.0 3.4 %select_reduce_fusion.1 = (f32[64,4,10]{2,1,0:T(4,128)}, f32[64,4,10,2]{2,3,1,0:T(2,128)}) fusion(pred[10,2]{0,1:T(4,128)(4,1)} %iota_compare_fusion.7, bf16[64,4,10,128]{3,0,2,1:T(8,128)(2,1)} %bitcast.84, bf16[64,2,4,1,128]{4,3,2,1,0:T(2,128)(2,1)S(1)} %get-tuple-element.23), kind=kOutput, calls=%fused_computation.42 | convolution fusion | flops 1323520 | bytes 817172 | tf_op jit(solution)/shard_map/scrd,sicd->scri/dot_general | solution.py:113
  90.4 1.6 copy.154
  92.0 6.1 %all-to-all-start.1 = ((bf16[32,4,64,128]{3,2,1,0:T(8,128)(2,1)}), bf16[32,4,64,128]{3,2,1,0:T(8,128)(2,1)}, u32[]{:S(2)}, u32[]{:S(2)}) async-start(bf16[32,4,64,128]{3,2,1,0:T(8,128)(2,1)} %get-tuple-element.24), calls=%async_computation.2 | async-start | bytes 4194304 | tf_op jit(solution)/shard_map/all_to_all | solution.py:93
  98.1 2.2 %fusion.46 = (f32[32,4,10]{2,1,0:T(4,128)S(1)}, f32[32,4,10,64]{3,2,1,0:T(8,128)}) fusion(bf16[32,4,64,128]{3,2,1,0:T(8,128)(2,1)S(1)} %all-to-all-done, bf16[32,4,10,128]{3,1,2,0:T(4,128)(2,1)S(1)} %gather_fusion), kind=kOutput, calls=%fused_computation.96 | convolution fusion | flops 21134080 | bytes 2757632 | tf_op jit(solution)/shard_map/...crd,...cpd->...crp/dot_general | solution.py:24
  100.3 0.6 copy-done.4
  100.9 0.1 broadcast_select_fusion.2
  101.0 0.1 copy.162
  101.1 0.3 select_reduce_fusion
  101.4 0.8 copy_maximum_fusion
  102.2 0.1 copy.167
  102.3 1.9 %convert_reduce_fusion.1 = f32[32,4,10]{2,1,0:T(4,128)S(1)} fusion(f32[32,4,10,64]{3,2,1,0:T(8,128)} %get-tuple-element.27, f32[32,4,10]{2,1,0:T(4,128)} %copy-done.4), kind=kLoop, calls=%fused_computation.31 | loop fusion | flops 326400 | bytes 337920 | tf_op jit(solution)/shard_map/reduce_sum | solution.py:31
  104.2 0.6 gather_fusion.2
  104.8 1.5 fusion.33
  106.3 0.1 copy.173
  106.4 23.5 %convert_reduce_fusion = f32[64,4,10]{0,2,1:T(8,128)S(1)} fusion(f32[64,4,10]{0,2,1:T(8,128)S(1)} %copy.164, f32[4,56,64,64,10]{3,2,4,1,0:T(8,128)} %get-tuple-element.31, pred[64,56,64]{0,2,1:T(8,128)(4,1)S(1)} %copy.146), kind=kLoop, calls=%fused_computation.10 | loop fusion | flops 55047680 | bytes 36950016 | tf_op jit(solution)/shard_map/reduce_sum | solution.py:123
  129.9 0.1 fusion.44
  130.1 0.3 fusion.16
  130.4 3.3 %fusion.25 = f32[64,4,10,128]{3,2,1,0:T(8,128)} fusion(bf16[64,2,4,1,128]{4,3,2,1,0:T(2,128)(2,1)S(1)} %copy-done.7, f32[64,4,10,2]{2,3,1,0:T(2,128)S(1)} %copy-done.6, pred[10,2]{0,1:T(4,128)(4,1)S(1)} %copy-done.9, f32[64,4,10]{2,1,0:T(4,128)S(1)} %copy.167), kind=kOutput, calls=%fused_computation.45 | convolution fusion | flops 7874560 | bytes 1472532 | tf_op jit(solution)/shard_map/scri,sicd->scrd/dot_general | solution.py:129
  133.6 28.5 %fusion.9 = f32[64,4,10,128]{3,0,2,1:T(8,128)} fusion(f32[4,56,64,64,10]{3,2,4,1,0:T(8,128)} %get-tuple-element.31, f32[64,4,10]{0,2,1:T(8,128)S(1)} %copy.164, pred[64,56,64]{0,2,1:T(8,128)(4,1)S(1)} %copy.146, bf16[56,4,64,128]{3,2,1,0:T(8,128)(2,1)} %param.14), kind=kOutput, calls=%fused_computation.18 | convolution fusion | flops 2385510400 | bytes 41920512 | tf_op jit(solution)/shard_map/scrpq,pcqd->scrd/dot_general | solution.py:124
  162.1 2.6 %convolution_multiply_fusion = f32[32,4,10,128]{3,2,1,0:T(8,128)S(1)} fusion(bf16[32,4,64,128]{3,2,1,0:T(8,128)(2,1)} %all-to-all-done.1, f32[32,4,10]{2,1,0:T(4,128)S(1)} %get-tuple-element.21, f32[32,4,10,64]{3,2,1,0:T(8,128)S(1)} %copy-done.2, f32[32,4,10]{2,1,0:T(4,128)S(1)} %copy-done.5), kind=kOutput, calls=%fused_computation.23 | convolution fusion | flops 21299200 | bytes 3090432 | tf_op jit(solution)/shard_map/...crp,...cpd->...crd/dot_general | solution.py:32
  164.7 2.0 %fusion.14 = bf16[64,4,10,128]{3,0,2,1:T(8,128)(2,1)S(1)} fusion(f32[64,4,10,128]{3,0,2,1:T(8,128)S(1)} %copy-done.14, f32[64,4,10,128]{3,2,1,0:T(8,128)S(1)} %copy-done.3, f32[32,4,10,128]{3,2,1,0:T(8,128)S(1)} %convolution_multiply_fusion, f32[64,4,10]{0,2,1:T(8,128)S(1)} %fusion.16, s32[32]{0:T(128)S(1)} %eq.120, pred[32]{0:T(512)(128)(4,1)S(1)} %gt.33), kind=kOutput, calls=%fused_computation.25 | convolution fusion | flops 127143936 | bytes 3942560 | tf_op jit(solution)/shard_map/sn,ncrd->scrd/dot_general | solution.py:140
  166.7 1.5 copy.174
  (43 shorter events, 0.2 us)
Async XLA Ops:
  7.2 1.1 copy-start
  7.2 9.5 %copy-start.12 = (s32[256,1]{0,1:T(1,128)S(1)}, s32[256,1]{0,1:T(1,128)}, u32[]{:S(2)}) copy-start(s32[256,1]{0,1:T(1,128)} %param.17) | copy-start | bytes 3076
  7.2 10.8 %copy-start.10 = (s32[256]{0:T(256)S(1)}, s32[256]{0:T(256)}, u32[]{:S(2)}) copy-start(s32[256]{0:T(256)} %param.18) | copy-start | bytes 3076
  7.2 11.2 %copy-start.11 = (s32[256]{0:T(256)S(1)}, s32[256]{0:T(256)}, u32[]{:S(2)}) copy-start(s32[256]{0:T(256)} %param.19) | copy-start | bytes 3076
  7.2 72.2 %reduce-scatter.2.cloned.1.call-start = ((), (), s32[]{:S(2)}) async-start(), calls=%async_computation.3 | async-start | bytes 1572864 | tf_op jit(solution)/shard_map/reduce_scatter | solution.py:50
  30.2 8.6 %copy-start.8 = (s32[64,32]{0,1:T(8,128)S(1)}, s32[64,32]{0,1:T(8,128)}, u32[]{:S(2)}) copy-start(s32[64,32]{0,1:T(8,128)} %param.15) | copy-start | bytes 24580
  30.2 8.7 %copy-start.13 = (s32[64]{0:T(128)S(1)}, s32[64]{0:T(128)}, u32[]{:S(2)}) copy-start(s32[64]{0:T(128)} %param.16) | copy-start | bytes 772
  30.2 61.8 %all-to-all-start = ((bf16[32,4,64,128]{3,2,1,0:T(8,128)(2,1)}), bf16[32,4,64,128]{3,2,1,0:T(8,128)(2,1)S(1)}, u32[]{:S(2)}, u32[]{:S(2)}) async-start(bf16[32,4,64,128]{3,2,1,0:T(8,128)(2,1)} %get-tuple-element.25), calls=%async_computation.1 | async-start | bytes 4194304 | tf_op jit(solution)/shard_map/all_to_all | solution.py:92
  45.1 0.8 copy-start.1
  92.0 70.1 %all-to-all-start.1 = ((bf16[32,4,64,128]{3,2,1,0:T(8,128)(2,1)}), bf16[32,4,64,128]{3,2,1,0:T(8,128)(2,1)}, u32[]{:S(2)}, u32[]{:S(2)}) async-start(bf16[32,4,64,128]{3,2,1,0:T(8,128)(2,1)} %get-tuple-element.24), calls=%async_computation.2 | async-start | bytes 4194304 | tf_op jit(solution)/shard_map/all_to_all | solution.py:93
  100.3 0.6 copy-start.4
  106.4 23.5 %copy-start.5 = (f32[32,4,10]{2,1,0:T(4,128)S(1)}, f32[32,4,10]{2,1,0:T(4,128)}, u32[]{:S(2)}) copy-start(f32[32,4,10]{2,1,0:T(4,128)} %copy-done.4) | copy-start | bytes 15364
  106.4 23.9 %copy-start.6 = (f32[64,4,10,2]{2,3,1,0:T(2,128)S(1)}, f32[64,4,10,2]{2,3,1,0:T(2,128)}, u32[]{:S(2)}) copy-start(f32[64,4,10,2]{2,3,1,0:T(2,128)} %get-tuple-element.29) | copy-start | bytes 61444
  106.4 23.9 %copy-start.7 = (bf16[64,2,4,1,128]{4,3,2,1,0:T(2,128)(2,1)S(1)}, bf16[64,2,4,1,128]{4,3,2,1,0:T(2,128)(2,1)}, u32[]{:S(2)}) copy-start(bf16[64,2,4,1,128]{4,3,2,1,0:T(2,128)(2,1)} %get-tuple-element.22) | copy-start | bytes 393220
  106.4 23.9 %copy-start.9 = (pred[10,2]{0,1:T(4,128)(4,1)S(1)}, pred[10,2]{0,1:T(4,128)(4,1)}, u32[]{:S(2)}) copy-start(pred[10,2]{0,1:T(4,128)(4,1)} %iota_compare_fusion.7) | copy-start | bytes 64
  133.6 28.5 %copy-start.2 = (f32[32,4,10,64]{3,2,1,0:T(8,128)S(1)}, f32[32,4,10,64]{3,2,1,0:T(8,128)}, u32[]{:S(2)}) copy-start(f32[32,4,10,64]{3,2,1,0:T(8,128)} %get-tuple-element.27) | copy-start | bytes 983044
  162.1 2.6 %copy-start.3 = (f32[64,4,10,128]{3,2,1,0:T(8,128)S(1)}, f32[64,4,10,128]{3,2,1,0:T(8,128)}, u32[]{:S(2)}) copy-start(f32[64,4,10,128]{3,2,1,0:T(8,128)} %fusion.25) | copy-start | bytes 3932164
  162.1 2.6 %copy-start.14 = (f32[64,4,10,128]{3,0,2,1:T(8,128)S(1)}, f32[64,4,10,128]{3,0,2,1:T(8,128)}, u32[]{:S(2)}) copy-start(f32[64,4,10,128]{3,0,2,1:T(8,128)} %fusion.9) | copy-start | bytes 3932164
Sparse Core Ops, SparseCore 0:
  16.3 22.9 reduce-scatter.1
where the time goes:
time: 176 us; the launch traced here: 175 us
  matrix products  82.2 us (47%)
  other arithmetic  36 us (20%)
  local copies, waits for them, and re-layouts  28.4 us (16%)
  between operations  14.4 us (8%)
  starting transfers between devices  14 us (8%)
    dot_general x1, matrix products, per_device(): jnp.einsum('scrd,pcqd->scrpq', query_rows, k_cache, preferred_element_typ...  30.1 us
    dot_general x1, matrix products, per_device(): jnp.einsum('scrpq,pcqd->scrd', local_weights, v_cache, preferred_element_...  28.5 us
    reduce_sum x1, other arithmetic, per_device(): local_total = jnp.sum(local_weights.astype(jnp.float32), axis=(3, 4))  23.5 us
    all_to_all x1, starting transfers between devices, per_device(): lax.all_to_all(send_keys, 'gen', split_axis=0, concat_axis=0, tiled=True)  7.91 us
    dot_general x1, matrix products, per_device(): lax.dot_general(w_kv, tokens_in, (((0,), (1,)), ((), ())), preferred_elem...  7.89 us
    all_to_all x1, starting transfers between devices, per_device(): lax.all_to_all(send_values, 'gen', split_axis=0, concat_axis=0, tiled=True)  6.08 us
    unnamed x33, local copies, waits for them, and re-layouts  4.34 us
    gather x1, local copies, waits for them, and re-layouts, per_device(): k_cache[send_page]  4.21 us
  transfers between devices with their start and end apart: 3, of which 0 were waited for; matrix products, arithmetic and copies ran while one was open for 74% of the time, Pallas kernels for 0%

commit v1 on v0

v1 whole, which is shorter than its diff:
```python
import functools
import math

import jax
import jax.numpy as jnp
from jax import lax
from jax.experimental import pallas as pl
from jax.experimental.pallas import tpu as pltpu
from jax.sharding import PartitionSpec as P

CAP = 2
NEGATIVE = -1e30
LOG2E = 1.4426950408889634
LANES = 128
VMEM_LIMIT = 56 * 1024 * 1024


def whole(array):
    return pl.BlockSpec(array.shape, lambda *_: (0,) * array.ndim)


def smem():
    return pl.BlockSpec(memory_space=pltpu.SMEM)


def padded(rows):
    return (rows + 7) // 8 * 8


def slot_rows(steps, heads):
    step_rows = padded(heads + 3)
    return step_rows, (steps * step_rows + 15) // 16 * 16


def gather_kernel(
    dest_ref, seq_ref, me_ref, q_ref, owner_ref, landed_ref, slot_ref, out_ref, *, groups, per_source
):
    me = me_ref[0]
    slots = groups * CAP
    seqs, steps, heads, head_dim = q_ref.shape
    step_rows, rows = slot_rows(steps, heads)

    def clear(n, _):
        owner_ref[n] = 0
        landed_ref[n] = 0
        return 0

    lax.fori_loop(0, slots, clear, 0, unroll=8)
    owner_ref[slots] = 0
    landed_ref[slots] = 0

    def one_source(src, _):
        count = jnp.int32(0)
        for k in range(per_source):
            row = src * per_source + k
            hit = dest_ref[row] == me
            place = jnp.where(hit, src * CAP + count, slots)
            owner_ref[place] = seq_ref[row]
            landed_ref[place] = 1
            count = count + hit.astype(jnp.int32)
        return 0

    lax.fori_loop(0, groups, one_source, 0)

    for k in range(per_source):
        mine = dest_ref[me * per_source + k]
        rank = jnp.int32(0)
        for j in range(k):
            rank = rank + (dest_ref[me * per_source + j] == mine).astype(jnp.int32)
        slot_ref[k] = mine * CAP + rank

    zeros = jnp.zeros((step_rows - heads, head_dim), jnp.float32)

    def one_slot(n, _):
        block = q_ref[owner_ref[n]].astype(jnp.float32)
        parts = []
        for i in range(steps):
            parts += [block[i], zeros]
        if rows > steps * step_rows:
            parts.append(jnp.zeros((rows - steps * step_rows, head_dim), jnp.float32))
        out_ref[n] = jnp.concatenate(parts, axis=0).astype(jnp.bfloat16)
        return 0

    lax.fori_loop(0, slots, one_slot, 0, unroll=4)


def gather(dest, seq, me, queries, groups):
    per_source = dest.shape[0] // groups
    slots = groups * CAP
    seqs, steps, heads, head_dim = queries.shape
    _, rows = slot_rows(steps, heads)
    return pl.pallas_call(
        functools.partial(gather_kernel, groups=groups, per_source=per_source),
        in_specs=[smem(), smem(), smem(), pl.BlockSpec(memory_space=pltpu.VMEM)],
        out_specs=[smem(), smem(), smem(), pl.BlockSpec(memory_space=pltpu.VMEM)],
        out_shape=[
            jax.ShapeDtypeStruct((slots + 1,), jnp.int32),
            jax.ShapeDtypeStruct((slots + 1,), jnp.int32),
            jax.ShapeDtypeStruct((per_source,), jnp.int32),
            jax.ShapeDtypeStruct((slots, rows, head_dim), jnp.bfloat16),
        ],
        compiler_params=pltpu.CompilerParams(vmem_limit_bytes=VMEM_LIMIT),
        cost_estimate=pl.CostEstimate(flops=0, bytes_accessed=4 * queries.size, transcendentals=0),
        name="gather_queries",
    )(dest, seq, me, queries)


def project_kernel(shift_ref, x_ref, w_ref, own_ref, send_ref, *, blocks):
    product = jnp.dot(x_ref[...], w_ref[...], preferred_element_type=jnp.float32)
    step = pl.program_id(0)

    @pl.when(step < blocks)
    def _():
        own_ref[...] = product

    @pl.when(step >= blocks)
    def _():
        send_ref[0] = product


def project(tokens, w_kv, tp, tp_index):
    rows, depth = tokens.shape
    columns = w_kv.shape[1] // tp
    width = min(256, columns)
    blocks = columns // width
    shift = jnp.reshape(tp_index, (1,)).astype(jnp.int32)

    def w_map(step, shift_ref):
        owner = lax.rem(shift_ref[0] + step // blocks, tp)
        return (0, owner * blocks + lax.rem(step, blocks))

    def send_map(step, shift_ref):
        after = jnp.maximum(step - blocks, 0)
        return (after // blocks, 0, lax.rem(after, blocks))

    return pl.pallas_call(
        functools.partial(project_kernel, blocks=blocks),
        grid_spec=pltpu.PrefetchScalarGridSpec(
            num_scalar_prefetch=1,
            grid=(tp * blocks,),
            in_specs=[
                pl.BlockSpec((rows, depth), lambda step, shift_ref: (0, 0)),
                pl.BlockSpec((depth, width), w_map),
            ],
            out_specs=[
                pl.BlockSpec(
                    (rows, width), lambda step, shift_ref: (0, jnp.minimum(step, blocks - 1))
                ),
                pl.BlockSpec((1, rows, width), send_map),
            ],
        ),
        out_shape=[
            jax.ShapeDtypeStruct((rows, columns), jnp.float32),
            jax.ShapeDtypeStruct((tp - 1, rows, columns), jnp.float32),
        ],
        compiler_params=pltpu.CompilerParams(vmem_limit_bytes=VMEM_LIMIT),
        cost_estimate=pl.CostEstimate(
            flops=2 * rows * depth * columns * tp,
            bytes_accessed=2 * w_kv.size + 2 * tokens.size + 4 * rows * columns * tp,
            transcendentals=0,
        ),
        name="project_kv",
    )(shift, tokens, w_kv)


def local_kernel(
    q_ref, k_ref, v_ref, table_ref, length_ref, out_ref, lse_ref, query, bias, scores, top, total,
    *, width, first_head, per_group, scale
):
    seqs, steps, heads, head_dim = q_ref.shape
    page = k_ref.shape[2]
    blocks = scores.shape[0]
    step_rows = padded(heads)
    groups = steps * per_group
    rows = groups * seqs
    pages = width // page
    tiles = width // LANES
    head = pl.program_id(0)

    @pl.when(head == 0)
    def _():
        spread = query.reshape(seqs * steps, step_rows, head_dim)
        spread[:, :heads, :] = q_ref[...].reshape(seqs * steps, heads, head_dim).astype(jnp.float32)
        across = lax.broadcasted_iota(jnp.int32, (seqs, seqs), 1)
        down = lax.broadcasted_iota(jnp.int32, (seqs, seqs), 0)
        lengths = jnp.broadcast_to(length_ref[...].astype(jnp.float32), (seqs, seqs))
        lengths = jnp.sum(jnp.where(down == across, lengths, 0.0), axis=1, keepdims=True)
        lane = lax.broadcasted_iota(jnp.int32, (seqs, LANES), 1)
        used = jnp.zeros((seqs, LANES), jnp.float32)
        table = table_ref[...]
        for j in range(table.shape[1]):
            inside = jnp.clip(lengths - float(page * j), 0.0, float(page))
            used = used + jnp.where(table[:, j : j + 1] == lane, inside, 0.0)
        used = used.astype(jnp.bfloat16)

        def one_block(b, _):
            key = lax.broadcasted_iota(jnp.int32, (LANES, width), 1) + b * width
            owner = lax.broadcasted_iota(jnp.int32, (LANES, width), 0)
            expand = jnp.where(key // page == owner, 1.0, 0.0).astype(jnp.bfloat16)
            count = jnp.dot(used, expand, preferred_element_type=jnp.float32)
            position = lax.broadcasted_iota(jnp.int32, (seqs, width), 1) % page
            bias[b] = jnp.where(position.astype(jnp.float32) < count, 0.0, NEGATIVE)
            return 0

        lax.fori_loop(0, blocks, one_block, 0)

    parts = []
    for i in range(steps):
        for g in range(per_group):
            start = i * step_rows + (first_head + head) * per_group + g
            parts.append(query[pl.ds(start, seqs, stride=steps * step_rows), :])
    head_query = jnp.concatenate(parts, axis=0).astype(jnp.bfloat16)
    top[...] = jnp.full(top.shape, NEGATIVE, jnp.float32)
    total[...] = jnp.zeros(total.shape, jnp.float32)

    def score_block(b, _):
        keys = k_ref[pl.ds(b * pages, pages), 0].reshape(width, head_dim)
        s = lax.dot_general(
            head_query, keys, (((1,), (1,)), ((), ())), preferred_element_type=jnp.float32
        )
        s = (s.reshape(groups, seqs, width) + bias[b][None]).reshape(rows, width)
        scores[b] = s
        largest = s[:, :LANES]
        for t in range(1, tiles):
            largest = jnp.maximum(largest, s[:, t * LANES : (t + 1) * LANES])
        top[...] = jnp.maximum(top[...], largest)
        return 0

    lax.fori_loop(0, blocks, score_block, 0)
    top[...] = jnp.broadcast_to(jnp.max(top[...], axis=1, keepdims=True), top.shape)
    ones = jnp.ones((width, head_dim), jnp.bfloat16)

    def value_block(b, _):
        values = v_ref[pl.ds(b * pages, pages), 0].reshape(width, head_dim)
        values = jnp.concatenate([values, ones], axis=1)
        biggest = top[...]
        weights = jnp.concatenate(
            [
                jnp.exp2((scores[b, :, t * LANES : (t + 1) * LANES] - biggest) * scale).astype(
                    jnp.bfloat16
                )
                for t in range(tiles)
            ],
            axis=1,
        )
        total[...] += jnp.dot(weights, values, preferred_element_type=jnp.float32)
        return 0

    lax.fori_loop(0, blocks, value_block, 0)
    weight_sum = total[:, head_dim:]
    out_ref[0] = total[:, :head_dim] / weight_sum
    lse_ref[0] = top[...] * scale + jnp.log2(weight_sum)


def local_attention(queries, k_cache, v_cache, page_table, lengths, first_head, count, scale):
    seqs, steps, heads, head_dim = queries.shape
    pool, kv_heads, page, _ = k_cache.shape
    per_group = heads // kv_heads
    rows = steps * per_group * seqs
    keys = pool * page
    width = keys // 4
    cache_spec = pl.BlockSpec((pool, 1, page, head_dim), lambda h: (0, first_head + h, 0, 0))
    out_spec = pl.BlockSpec((1, rows, head_dim), lambda h: (h, 0, 0))
    out_shape = jax.ShapeDtypeStruct((count, rows, head_dim), jnp.float32)
    return pl.pallas_call(
        functools.partial(
            local_kernel, width=width, first_head=first_head, per_group=per_group, scale=scale
        ),
        grid=(count,),
        in_specs=[whole(queries), cache_spec, cache_spec, whole(page_table), whole(lengths)],
        out_specs=[out_spec, out_spec],
        out_shape=[out_shape, out_shape],
        scratch_shapes=[
            pltpu.VMEM((seqs * steps * padded(heads), head_dim), jnp.float32),
            pltpu.VMEM((keys // width, seqs, width), jnp.float32),
            pltpu.VMEM((keys // width, rows, width), jnp.float32),
            pltpu.VMEM((rows, LANES), jnp.float32),
            pltpu.VMEM((rows, 2 * head_dim), jnp.float32),
        ],
        compiler_params=pltpu.CompilerParams(vmem_limit_bytes=VMEM_LIMIT),
        cost_estimate=pl.CostEstimate(
            flops=6 * count * rows * keys * head_dim,
            bytes_accessed=4 * count * keys * head_dim + 8 * count * rows * head_dim,
            transcendentals=count * rows * keys,
        ),
        name="local_attention",
    )(queries, k_cache, v_cache, page_table, lengths)


def moved_kernel(
    slot_ref, page_ref, q_ref, k_hbm, v_hbm, out_ref, keys, values, sems, *, steps, heads, scale
):
    moves, kv_heads, page, head_dim = keys.shape
    per_group = heads // kv_heads
    step_rows, rows = slot_rows(steps, heads)
    columns = kv_heads * page

    def copies(k):
        source = page_ref[k]
        return (
            pltpu.make_async_copy(k_hbm.at[source], keys.at[k], sems.at[0, k]),
            pltpu.make_async_copy(v_hbm.at[source], values.at[k], sems.at[1, k]),
        )

    def start(k, _):
        for copy in copies(k):
            copy.start()
        return 0

    lax.fori_loop(0, moves, start, 0)
    out_ref[...] = jnp.zeros(out_ref.shape, jnp.bfloat16)
    row = lax.broadcasted_iota(jnp.int32, (rows, columns), 0)
    column = lax.broadcasted_iota(jnp.int32, (rows, columns), 1)
    same_head = (lax.rem(row, step_rows) // per_group) == column // page
    tall = lax.broadcasted_iota(jnp.int32, (rows, LANES), 0)
    lane = lax.broadcasted_iota(jnp.int32, (rows, LANES), 1)
    ones = jnp.ones((columns, head_dim), jnp.bfloat16)

    def one_move(k):
        s = lax.dot_general(
            q_ref[slot_ref[k]],
            keys[k].reshape(columns, head_dim),
            (((1,), (1,)), ((), ())),
            preferred_element_type=jnp.float32,
        )
        s = jnp.where(same_head, s, NEGATIVE)
        biggest = jnp.max(s, axis=1, keepdims=True)
        weights = jnp.exp2((s - biggest) * scale).astype(jnp.bfloat16)
        both = jnp.concatenate([values[k].reshape(columns, head_dim), ones], axis=1)
        summed = jnp.dot(weights, both, preferred_element_type=jnp.float32)
        weight_sum = summed[:, head_dim:]
        lse = biggest * scale + jnp.log2(weight_sum)
        lse = jnp.sum(jnp.where(tall == lane, lse, 0.0), axis=0, keepdims=True)
        high = lse.astype(jnp.bfloat16).astype(jnp.float32)
        middle = (lse - high).astype(jnp.bfloat16).astype(jnp.float32)
        low = lse - high - middle
        result = summed[:, :head_dim] / weight_sum
        for offset, piece in enumerate((high, middle, low)):
            result = jnp.where(tall == heads + offset, piece, result)
        out_ref[slot_ref[k]] = result.astype(jnp.bfloat16)

    def wait(k, _):
        for copy in copies(k):
            copy.wait()
        return 0

    lax.fori_loop(0, moves, wait, 0)
    batch = min(8, moves)

    def some_moves(b, _):
        for k in range(batch):
            one_move(b * batch + k)
        return 0

    lax.fori_loop(0, moves // batch, some_moves, 0)


def moved_attention(slots, pages, received, k_cache, v_cache, steps, heads, scale):
    moves = slots.shape[0]
    _, kv_heads, page, head_dim = k_cache.shape
    return pl.pallas_call(
        functools.partial(moved_kernel, steps=steps, heads=heads, scale=scale),
        in_specs=[
            smem(),
            smem(),
            pl.BlockSpec(memory_space=pltpu.VMEM),
            pl.BlockSpec(memory_space=pl.ANY),
            pl.BlockSpec(memory_space=pl.ANY),
        ],
        out_specs=pl.BlockSpec(memory_space=pltpu.VMEM),
        out_shape=jax.ShapeDtypeStruct(received.shape, jnp.bfloat16),
        scratch_shapes=[
            pltpu.VMEM((moves, kv_heads, page, head_dim), jnp.bfloat16),
            pltpu.VMEM((moves, kv_heads, page, head_dim), jnp.bfloat16),
            pltpu.SemaphoreType.DMA((2, moves)),
        ],
        compiler_params=pltpu.CompilerParams(vmem_limit_bytes=VMEM_LIMIT),
        cost_estimate=pl.CostEstimate(
            flops=4 * moves * 48 * 256 * 256,
            bytes_accessed=4 * moves * kv_heads * page * head_dim + 4 * received.size,
            transcendentals=moves * 48 * 256,
        ),
        name="moved_attention",
    )(slots, pages, received, k_cache, v_cache)


def final_kernel(
    owner_ref, landed_ref, q_ref, own_ref, other_ref, *refs, scale, local_count, per_group
):
    local = refs[: 2 * local_count]
    slot_ref, out_ref, new_ref, query, fresh, state, state_lse = refs[2 * local_count :]
    seqs, steps, heads, head_dim = q_ref.shape
    step_rows = padded(heads)
    slot_step, slot_size = slot_rows(steps, heads)
    stride = steps * step_rows
    spread = query.reshape(seqs * steps, step_rows, head_dim)
    spread[:, :heads, :] = q_ref[...].reshape(seqs * steps, heads, head_dim).astype(jnp.float32)
    new = own_ref[...]
    for k in range(other_ref.shape[0]):
        new = new + other_ref[k]
    new = new.astype(jnp.bfloat16)
    new_ref[...] = new
    for column in range(fresh.shape[0]):
        fresh[column] = new[:, column * head_dim : (column + 1) * head_dim].astype(jnp.float32)

    head = 0
    for part in range(local_count):
        out_part, lse_part = local[2 * part], local[2 * part + 1]
        for h in range(out_part.shape[0]):
            keys, values = [], []
            for j in range(steps):
                every = pl.ds(j, seqs, stride=steps)
                keys.append(fresh[2 * head, every, :])
                values.append(fresh[2 * head + 1, every, :])
            for i in range(steps):
                for g in range(per_group):
                    place = pl.ds(i * step_rows + head * per_group + g, seqs, stride=stride)
                    block = (i * per_group + g) * seqs
                    q = query[place, :]
                    lse = lse_part[h, block : block + seqs, :]
                    new_scores = [
                        jnp.sum(q * keys[j], axis=1, keepdims=True) * scale for j in range(i + 1)
                    ]
                    biggest = lse
                    for s in new_scores:
                        biggest = jnp.maximum(biggest, s)
                    weight = jnp.exp2(lse - biggest)
                    summed = weight * out_part[h, block : block + seqs, :]
                    for j, s in enumerate(new_scores):
                        w = jnp.exp2(s - biggest)
                        weight = weight + w
                        summed = summed + w * values[j]
                    state[place, :] = summed / weight
                    state_lse[place, :] = biggest + jnp.log2(weight)
            head += 1

    tall = lax.broadcasted_iota(jnp.int32, (slot_size, LANES), 0)
    lane = lax.broadcasted_iota(jnp.int32, (slot_size, LANES), 1)

    def one_slot(n, _):
        @pl.when(landed_ref[n] > 0)
        def _():
            block = slot_ref[n].astype(jnp.float32)
            packed = block[heads : heads + 1] + block[heads + 1 : heads + 2]
            packed = packed + block[heads + 2 : heads + 3]
            slot_lse = jnp.sum(jnp.where(tall == lane, packed, 0.0), axis=1, keepdims=True)
            for i in range(steps):
                place = pl.ds(owner_ref[n] * stride + i * step_rows, step_rows)
                rows = slice(i * slot_step, i * slot_step + step_rows)
                lse = state_lse[place, :]
                biggest = jnp.maximum(lse, slot_lse[rows])
                old = jnp.exp2(lse - biggest)
                come = jnp.exp2(slot_lse[rows] - biggest)
                weight = old + come
                state[place, :] = (old * state[place, :] + come * block[rows]) / weight
                state_lse[place, :] = biggest + jnp.log2(weight)

        return 0

    lax.fori_loop(0, slot_ref.shape[0], one_slot, 0)
    done = state.reshape(seqs * steps, step_rows, head_dim)[:, :heads, :]
    out_ref[...] = done.astype(jnp.bfloat16).reshape(out_ref.shape)


def finish(owner, landed, queries, own, other, local, slots, per_group, scale):
    seqs, steps, heads, head_dim = queries.shape
    flat = (seqs * steps * padded(heads), head_dim)
    vmem = pl.BlockSpec(memory_space=pltpu.VMEM)
    return pl.pallas_call(
        functools.partial(
            final_kernel, scale=scale, local_count=len(local) // 2, per_group=per_group
        ),
        in_specs=[smem(), smem()] + [vmem] * (4 + len(local)),
        out_specs=[vmem, vmem],
        out_shape=[
            jax.ShapeDtypeStruct(queries.shape, jnp.bfloat16),
            jax.ShapeDtypeStruct(own.shape, jnp.bfloat16),
        ],
        scratch_shapes=[
            pltpu.VMEM(flat, jnp.float32),
            pltpu.VMEM((own.shape[1] // head_dim, own.shape[0], head_dim), jnp.float32),
            pltpu.VMEM(flat, jnp.float32),
            pltpu.VMEM(flat, jnp.float32),
        ],
        compiler_params=pltpu.CompilerParams(vmem_limit_bytes=VMEM_LIMIT),
        cost_estimate=pl.CostEstimate(
            flops=40 * queries.size, bytes_accessed=16 * queries.size, transcendentals=0
        ),
        name="combine",
    )(owner, landed, queries, own, other, *local, slots)


def per_device(
    tokens_in, w_kv, queries, k_cache, v_cache, page_table, lengths, move_dest, move_page, move_seq
):
    groups = lax.axis_size("gen")
    me = lax.axis_index("gen").astype(jnp.int32)
    tp = lax.axis_size("tp")
    tp_index = lax.axis_index("tp")
    seqs, steps, heads, head_dim = queries.shape
    kv_heads = k_cache.shape[1]
    per_group = heads // kv_heads
    per_source = move_dest.shape[0] // groups
    scale = LOG2E / math.sqrt(head_dim)

    def exchange(array):
        return lax.all_to_all(array, "gen", split_axis=0, concat_axis=0, tiled=True)

    owner, landed, slots, to_send = gather(
        move_dest.reshape(-1), move_seq, me.reshape(1), queries, groups
    )
    received = exchange(to_send)
    own, partial = project(tokens_in, w_kv, tp, tp_index)
    pieces = []
    for k in range(1, tp):
        pairs = [(i, (i + k) % tp) for i in range(tp)]
        pieces.append(lax.ppermute(partial[k - 1], "tp", pairs))
    other = jnp.stack(pieces)

    lengths_row = lengths.reshape(1, seqs)
    early = max(1, kv_heads // 2)
    local = list(
        local_attention(queries, k_cache, v_cache, page_table, lengths_row, 0, early, scale)
    )
    pages = lax.dynamic_slice_in_dim(move_page, me * per_source, per_source, 0)
    received, local[0] = lax.optimization_barrier((received, local[0]))
    answers = moved_attention(slots, pages, received, k_cache, v_cache, steps, heads, scale)
    if early < kv_heads:
        late_queries, answers = lax.optimization_barrier((queries, answers))
        local += list(
            local_attention(
                late_queries, k_cache, v_cache, page_table, lengths_row, early, kv_heads - early,
                scale,
            )
        )
    returned = exchange(answers)
    attended, new_kv = finish(owner, landed, queries, own, other, local, returned, per_group, scale)
    return (attended, new_kv)


def solution(mesh):
    return jax.shard_map(
        per_device,
        mesh=mesh,
        in_specs=(
            P("gen", "tp"),
            P("tp", None),
            P("gen", None, "tp", None),
            P("gen", "tp", None, None),
            P("gen", "tp", None, None),
            P("gen", None),
            P("gen"),
            P(),
            P(),
            P(),
        ),
        out_specs=(P("gen", None, "tp", None), P("gen", "tp")),
        check_vma=False,
    )
```

time: 176 us -> 77 us (0.44)
  matrix products: 82.2 us -> 0 us
  Pallas kernels: 0 us -> 49.8 us
  other arithmetic: 36 us -> 0 us
  local copies, waits for them, and re-layouts: 28.4 us -> 10 us
  between operations: 14.4 us -> 0.71 us
    dot_general x10 -> x0, matrix products: 82.2 us -> none  [the longest x1 30.1 us: per_device(): jnp.einsum('scrd,pcqd->scrpq', query_rows, k_cache, preferred_element_typ...]
    pallas_call x0 -> x6, Pallas kernels: none -> 49.8 us  [the longest x2 25.2 us: local_attention(): pl.pallas_call(functools.partial(local_kernel, width=width, first_head=fi...]
    reduce_sum x6 -> x0, other arithmetic: 27.5 us -> none  [the longest x1 23.5 us: per_device(): local_total = jnp.sum(local_weights.astype(jnp.float32), axis=(3, 4))]
    gather x4 -> x0, local copies, waits for them, and re-layouts: 9.73 us -> none  [the longest x1 4.21 us: per_device(): k_cache[send_page]]
    select_n x4 -> x0, other arithmetic: 4.05 us -> none  [the longest x1 3.93 us: per_device(): jnp.where(sent_mask, v_cache[send_page], jnp.zeros((), v_cache.dtype))]
    reshape x5 -> x0, local copies, waits for them, and re-layouts: 3.43 us -> none  [the longest x1 1.83 us: per_device(): new_parts = new_kv.reshape(seq_dev, step_count, kv_dev, 2, head_dim)]
    convert_element_type x2 -> x0, local copies, waits for them, and re-layouts: 3.3 us -> none  [the longest x1 1.79 us: per_device(): new_kv = fresh_kv.astype(jnp.bfloat16)]
    gt x5 -> x0, local copies, waits for them, and re-layouts: 2.98 us -> none  [the longest x1 2.58 us: per_device(): visible = (usage_count > 0.5)[:, None, None]]
  transfers between devices with their start and end apart: 3 -> 3, of which waited for: 0 -> 0; matrix products, arithmetic and copies ran while one was open for 74% -> 5% of each run, Pallas kernels for 0% -> 45%
where the time goes in v1:
time: 77 us; the launch traced here: 75.5 us
  Pallas kernels  49.8 us (65%)
  starting transfers between devices  15 us (19%)
  local copies, waits for them, and re-layouts  10 us (13%)
    pallas_call x2, Pallas kernels, local_attention(): pl.pallas_call(functools.partial(local_kernel, width=width, first_head=fi...  25.2 us
    all_to_all x2, starting transfers between devices, exchange(): return lax.all_to_all(array, 'gen', split_axis=0, concat_axis=0, tiled=True)  13.4 us
    pallas_call x1, Pallas kernels, project(): pl.pallas_call(functools.partial(project_kernel, blocks=blocks), grid_spe...  8.77 us
    pallas_call x1, Pallas kernels, finish(): pl.pallas_call(functools.partial(final_kernel, scale=scale, local_count=l...  7.64 us
    unnamed x10, local copies, waits for them, and re-layouts  5.17 us
    pallas_call x1, Pallas kernels, moved_attention(): pl.pallas_call(functools.partial(moved_kernel, steps=steps, heads=heads,...  4.92 us
    pallas_call x1, Pallas kernels, gather(): pl.pallas_call(functools.partial(gather_kernel, groups=groups, per_source...  3.2 us
    pallas_call x1, local copies, waits for them, and re-layouts, finish(): pl.pallas_call(functools.partial(final_kernel, scale=scale, local_count=l...  2.48 us
  transfers between devices with their start and end apart: 3, of which 0 were waited for; matrix products, arithmetic and copies ran while one was open for 5% of the time, Pallas kernels for 45%

profile of v1, /device:TPU:0, one launch (start us, length us, event | category | flops | bytes accessed | tf_op | source)
XLA Modules:
  0.0 75.5 jit_solution(5856370720520738812)
XLA Ops:
  0.6 2.1 %copy.12.q_ref = bf16[64,2,20,128]{3,2,1,0:T(8,128)(2,1)} copy(bf16[64,2,20,128]{3,1,2,0:T(2,128)(2,1)} %param.12) | data formatting | bytes 1310720 | tf_op args[2]
  2.7 3.2 %gather_queries.1 = (s32[33]{0:T(128)}, s32[33]{0:T(128)}, s32[16]{0:T(128)}, bf16[32,48,128]{2,1,0:T(8,128)(2,1)}) custom-call(s32[256]{0:T(256)} %bitcast.7, s32[256]{0:T(256)} %seq_ref.1, s32[1]{0:T(128)} %bitcast.1.me_ref, bf16[64,2,20,128]{3,2,1,0:T(8,128)(2,1)} %copy.12.q_ref), custom_call_target="tpu_custom_call" | custom-call | bytes 1310720 | tf_op jit(solution)/shard_map/gather_queries/pallas_call | solution.py:92
  5.9 7.4 %all-to-all-start = ((bf16[32,48,128]{2,1,0:T(8,128)(2,1)}), bf16[32,48,128]{2,1,0:T(8,128)(2,1)S(1)}, u32[]{:S(2)}, u32[]{:S(2)}) async-start(bf16[32,48,128]{2,1,0:T(8,128)(2,1)} %get-tuple-element.20), calls=%async_computation | async-start | bytes 786432 | tf_op jit(solution)/shard_map/all_to_all | solution.py:507
  13.3 1.4 %copy.14.table_ref = s32[64,32]{1,0:T(8,128)} copy(s32[64,32]{0,1:T(8,128)} %param.15) | data formatting | bytes 16384 | tf_op args[5]
  14.8 1.3 %dynamic_slice.3.page_ref = s32[16]{0:T(128)} dynamic-slice(s32[256]{0:T(256)} %param.18, s32[]{:T(128)S(6)} %select_n.3), dynamic_slice_sizes={16} | dynamic-slice | bytes 132 | tf_op jit(solution)/shard_map/dynamic_slice | solution.py:525
  16.1 12.6 %local_attention.2 = (f32[2,640,128]{2,1,0:T(8,128)}, f32[2,640,128]{2,1,0:T(8,128)}) custom-call(bf16[64,2,20,128]{3,2,1,0:T(8,128)(2,1)} %copy.12.q_ref, bf16[56,4,64,128]{3,2,1,0:T(8,128)(2,1)} %k_ref.3, bf16[56,4,64,128]{3,2,1,0:T(8,128)(2,1)} %v_ref.3, s32[64,32]{1,0:T(8,128)} %copy.14.table_ref, s32[1,64]{1,0:T(1,128)} %bitcast.9), custom_call_target="tpu_custom_call" | custom-call | flops 3523215360 | bytes 4980736 | tf_op jit(solution)/shard_map/local_attention/pallas_call | solution.py:265
  28.7 0.0 all-to-all-done.q_ref
  28.7 0.0 copy-start.1
  28.7 0.7 copy-done.1
  29.5 4.9 %moved_attention.1 = bf16[32,48,128]{2,1,0:T(8,128)(2,1)} custom-call(s32[16]{0:T(128)} %get-tuple-element.24.slot_ref, s32[16]{0:T(128)} %dynamic_slice.3.page_ref, bf16[32,48,128]{2,1,0:T(8,128)(2,1)} %copy-done.1, bf16[56,4,64,128]{3,2,1,0:T(8,128)(2,1)} %k_ref.3, bf16[56,4,64,128]{3,2,1,0:T(8,128)(2,1)} %v_ref.3), custom_call_target="tpu_custom_call" | custom-call | flops 201326592 | bytes 2883584 | tf_op jit(solution)/shard_map/moved_attention/pallas_call | solution.py:361
  34.4 6.0 %all-to-all-start.1 = ((bf16[32,48,128]{2,1,0:T(8,128)(2,1)}), bf16[32,48,128]{2,1,0:T(8,128)(2,1)S(1)}, u32[]{:S(2)}, u32[]{:S(2)}) async-start(bf16[32,48,128]{2,1,0:T(8,128)(2,1)} %moved_attention.1), calls=%async_computation.1 | async-start | bytes 786432 | tf_op jit(solution)/shard_map/all_to_all | solution.py:507
  40.4 0.0 copy-start
  40.4 8.8 %project_kv.1 = (f32[128,1024]{1,0:T(8,128)}, f32[1,128,1024]{2,1,0:T(8,128)}) custom-call(s32[1]{0:T(128)} %bitcast.2.shift_ref, bf16[128,2560]{1,0:T(8,128)(2,1)} %x_ref.1, bf16[2560,2048]{1,0:T(8,128)(2,1)} %w_ref.1), custom_call_target="tpu_custom_call" | custom-call | flops 1342177280 | bytes 12189696 | tf_op jit(solution)/shard_map/project_kv/pallas_call | solution.py:136
  49.2 1.5 %collective-permute-start = (f32[128,1024]{1,0:T(8,128)}, f32[128,1024]{1,0:T(8,128)S(1)}, u32[]{:S(2)}, u32[]{:S(2)}) collective-permute-start(f32[128,1024]{1,0:T(8,128)} %bitcast.8), channel_id=1, source_target_pairs={{0,1},{1,0},{2,3},{3,2},{4,5},{5,4},{6,7},{7,6},{8,9},{9,8},{10,11... | collective-permute-start | bytes 1572872 | tf_op jit(solution)/shard_map/ppermute | solution.py:517
  50.7 0.0 copy-done
  50.7 1.0 %copy.15.q_ref = bf16[64,2,20,128]{3,2,1,0:T(8,128)(2,1)} copy(bf16[64,2,20,128]{3,1,2,0:T(2,128)(2,1)S(1)} %copy-done) | data formatting | bytes 1310720 | tf_op jit(solution)/shard_map/optimization_barrier | solution.py:529
  51.8 12.6 %local_attention.3 = (f32[2,640,128]{2,1,0:T(8,128)}, f32[2,640,128]{2,1,0:T(8,128)}) custom-call(bf16[64,2,20,128]{3,2,1,0:T(8,128)(2,1)} %copy.15.q_ref, bf16[56,4,64,128]{3,2,1,0:T(8,128)(2,1)} %k_ref.3, bf16[56,4,64,128]{3,2,1,0:T(8,128)(2,1)} %v_ref.3, s32[64,32]{1,0:T(8,128)} %copy.14.table_ref, s32[1,64]{1,0:T(1,128)} %bitcast.10), custom_call_target="tpu_custom_call" | custom-call | flops 3523215360 | bytes 4980736 | tf_op jit(solution)/shard_map/local_attention/pallas_call | solution.py:265
  64.4 0.0 collective-permute-done
  64.4 0.0 copy-start.3
  64.4 0.0 all-to-all-done.1.refs_4_
  64.4 0.0 copy-start.2
  64.4 0.8 %copy-done.3 = f32[128,1024]{1,0:T(8,128)} copy-done((f32[128,1024]{1,0:T(8,128)}, f32[128,1024]{1,0:T(8,128)S(1)}, u32[]{:S(2)}) %copy-start.3) | copy-done | bytes 524312
  65.2 0.1 copy-done.2
  65.3 7.6 %combine.1 = (bf16[64,2,20,128]{3,2,1,0:T(8,128)(2,1)}, bf16[128,1024]{1,0:T(8,128)(2,1)}) custom-call(s32[33]{0:T(128)} %get-tuple-element.16.owner_ref, s32[33]{0:T(128)} %get-tuple-element.17.landed_ref, bf16[64,2,20,128]{3,2,1,0:T(8,128)(2,1)} %copy.12.q_ref, f32[128,1024]{1,0:T(8,128)} %get-tuple-element.18.own_ref, f32[1,128,1024]{2,1,0:T(8,128)} %bitcast.6, ...), custom_call_target="tpu_custom_call" | custom-call | flops 13107200 | bytes 5242880 | tf_op jit(solution)/shard_map/combine/pallas_call | solution.py:469
  73.0 2.5 %copy.18 = bf16[64,2,20,128]{3,1,2,0:T(2,128)(2,1)} copy(bf16[64,2,20,128]{3,2,1,0:T(8,128)(2,1)} %get-tuple-element.30) | data formatting | bytes 1310720 | tf_op jit(solution)/shard_map/combine/pallas_call | solution.py:469
Async XLA Ops:
  5.9 22.8 %all-to-all-start = ((bf16[32,48,128]{2,1,0:T(8,128)(2,1)}), bf16[32,48,128]{2,1,0:T(8,128)(2,1)S(1)}, u32[]{:S(2)}, u32[]{:S(2)}) async-start(bf16[32,48,128]{2,1,0:T(8,128)(2,1)} %get-tuple-element.20), calls=%async_computation | async-start | bytes 786432 | tf_op jit(solution)/shard_map/all_to_all | solution.py:507
  28.7 0.7 copy-start.1
  34.4 30.0 %all-to-all-start.1 = ((bf16[32,48,128]{2,1,0:T(8,128)(2,1)}), bf16[32,48,128]{2,1,0:T(8,128)(2,1)S(1)}, u32[]{:S(2)}, u32[]{:S(2)}) async-start(bf16[32,48,128]{2,1,0:T(8,128)(2,1)} %moved_attention.1), calls=%async_computation.1 | async-start | bytes 786432 | tf_op jit(solution)/shard_map/all_to_all | solution.py:507
  40.4 10.3 %copy-start = (bf16[64,2,20,128]{3,1,2,0:T(2,128)(2,1)S(1)}, bf16[64,2,20,128]{3,1,2,0:T(2,128)(2,1)}, u32[]{:S(2)}) copy-start(bf16[64,2,20,128]{3,1,2,0:T(2,128)(2,1)} %param.12) | copy-start | bytes 1966084
  49.2 15.2 %collective-permute-start = (f32[128,1024]{1,0:T(8,128)}, f32[128,1024]{1,0:T(8,128)S(1)}, u32[]{:S(2)}, u32[]{:S(2)}) collective-permute-start(f32[128,1024]{1,0:T(8,128)} %bitcast.8), channel_id=1, source_target_pairs={{0,1},{1,0},{2,3},{3,2},{4,5},{5,4},{6,7},{7,6},{8,9},{9,8},{10,11... | collective-permute-start | bytes 1572872 | tf_op jit(solution)/shard_map/ppermute | solution.py:517
  64.4 0.8 %copy-start.3 = (f32[128,1024]{1,0:T(8,128)}, f32[128,1024]{1,0:T(8,128)S(1)}, u32[]{:S(2)}) copy-start(f32[128,1024]{1,0:T(8,128)S(1)} %collective-permute-done) | copy-start | bytes 1572868
  64.4 0.9 %copy-start.2 = (bf16[32,48,128]{2,1,0:T(8,128)(2,1)}, bf16[32,48,128]{2,1,0:T(8,128)(2,1)S(1)}, u32[]{:S(2)}) copy-start(bf16[32,48,128]{2,1,0:T(8,128)(2,1)S(1)} %all-to-all-done.1.refs_4_) | copy-start | bytes 1179652

commit v2 on v0

v2 whole, which is shorter than its diff:
```python
import functools
import math

import jax
import jax.numpy as jnp
from jax import lax
from jax.experimental import pallas as pl
from jax.experimental.pallas import tpu as pltpu
from jax.sharding import PartitionSpec as P

CAP = 2
NEGATIVE = -1e30
LOG2E = 1.4426950408889634
LANES = 128
VMEM_LIMIT = 56 * 1024 * 1024


def smem():
    return pl.BlockSpec(memory_space=pltpu.SMEM)


def vmem():
    return pl.BlockSpec(memory_space=pltpu.VMEM)


def hbm():
    return pl.BlockSpec(memory_space=pl.ANY)


def answer_rows(rows):
    return (rows + 3 + 15) // 16 * 16


def gather_kernel(dest_ref, seq_ref, me_ref, q_ref, owner_ref, slot_ref, out_ref, *, groups):
    me = me_ref[0]
    slots = groups * CAP
    per_source = slot_ref.shape[0]

    def clear(n, _):
        owner_ref[n] = -1
        return 0

    lax.fori_loop(0, slots, clear, 0, unroll=8)

    def one_source(src, _):
        count = jnp.int32(0)
        for k in range(per_source):
            row = src * per_source + k
            hit = dest_ref[row] == me
            owner_ref[jnp.where(hit, src * CAP + count, slots)] = seq_ref[row]
            count = count + hit.astype(jnp.int32)
        return 0

    lax.fori_loop(0, groups, one_source, 0)

    def one_slot(n, _):
        out_ref[n] = q_ref[jnp.maximum(owner_ref[n], 0)]
        return 0

    lax.fori_loop(0, slots, one_slot, 0, unroll=8)

    for k in range(per_source):
        mine = dest_ref[me * per_source + k]
        rank = jnp.int32(0)
        for j in range(k):
            rank = rank + (dest_ref[me * per_source + j] == mine).astype(jnp.int32)
        slot_ref[k] = mine * CAP + rank


def gather(dest, seq, me, queries, groups):
    per_source = dest.shape[0] // groups
    slots = groups * CAP
    seqs, rows, head_dim = queries.shape
    return pl.pallas_call(
        functools.partial(gather_kernel, groups=groups),
        in_specs=[smem(), smem(), smem(), vmem()],
        out_specs=[smem(), smem(), vmem()],
        out_shape=[
            jax.ShapeDtypeStruct((slots + 1,), jnp.int32),
            jax.ShapeDtypeStruct((per_source,), jnp.int32),
            jax.ShapeDtypeStruct((slots, rows, head_dim), jnp.bfloat16),
        ],
        compiler_params=pltpu.CompilerParams(vmem_limit_bytes=VMEM_LIMIT),
        cost_estimate=pl.CostEstimate(flops=0, bytes_accessed=4 * queries.size, transcendentals=0),
        name="gather_queries",
    )(dest, seq, me, queries)


def make_bias(table_ref, length_ref, bias, page):
    blocks, seqs, width = bias.shape
    pool = 64
    lengths = length_ref[...].astype(jnp.float32)
    page_id = lax.broadcasted_iota(jnp.int32, (pool, seqs), 0)
    used = jnp.zeros((pool, seqs), jnp.float32)
    for j in range(table_ref.shape[0]):
        inside = jnp.clip(lengths - float(page * j), 0.0, float(page))
        used = used + jnp.where(table_ref[j : j + 1, :] == page_id, inside, 0.0)
    used = used.T.astype(jnp.bfloat16)

    def one_block(b, _):
        key = lax.broadcasted_iota(jnp.int32, (pool, width), 1) + b * width
        owner = lax.broadcasted_iota(jnp.int32, (pool, width), 0)
        expand = jnp.where(key // page == owner, 1.0, 0.0).astype(jnp.bfloat16)
        count = jnp.dot(used, expand, preferred_element_type=jnp.float32)
        position = lax.broadcasted_iota(jnp.int32, (seqs, width), 1) % page
        bias[b] = jnp.where(position.astype(jnp.float32) < count, 0.0, NEGATIVE)
        return 0

    lax.fori_loop(0, blocks, one_block, 0)


class Attend:
    def __init__(self, query, bias, keys, values, scores, tops, packed, total, scale, per_head):
        self.query, self.bias, self.keys, self.values = query, bias, keys, values
        self.scores, self.tops, self.packed, self.total = scores, tops, packed, total
        self.scale, self.per_head = scale, per_head
        self.blocks, self.seqs, self.width = bias.shape
        self.head_dim = query.shape[1]
        self.stride = query.shape[0] // self.seqs
        self.rows = per_head * self.seqs
        self.pages = self.width // keys.shape[2]

    def start_scores(self, h, head):
        for r in range(self.per_head):
            rows = self.query[pl.ds(head * self.per_head + r, self.seqs, stride=self.stride), :]
            self.packed[pl.ds(r * self.seqs, self.seqs), :] = rows.astype(jnp.bfloat16)
        self.tops[h % 2][...] = jnp.full(self.tops[0].shape, NEGATIVE, jnp.float32)

    def score_block(self, h, b):
        top = self.tops[h % 2]
        keys = self.keys[h, pl.ds(b * self.pages, self.pages)].reshape(self.width, self.head_dim)
        s = lax.dot_general(
            self.packed[...], keys, (((1,), (1,)), ((), ())), preferred_element_type=jnp.float32
        )
        s = s.reshape(self.per_head, self.seqs, self.width) + self.bias[b][None]
        s = s.reshape(self.rows, self.width)
        self.scores[h % 2][b] = s
        largest = s[:, :LANES]
        for t in range(1, self.width // LANES):
            largest = jnp.maximum(largest, s[:, t * LANES : (t + 1) * LANES])
        top[...] = jnp.maximum(top[...], largest)

    def start_values(self, h):
        top = self.tops[h % 2]
        top[...] = jnp.broadcast_to(jnp.max(top[...], axis=1, keepdims=True), top.shape)
        self.total[...] = jnp.zeros(self.total.shape, jnp.float32)

    def value_block(self, h, b):
        scores, biggest = self.scores[h % 2], self.tops[h % 2][...]
        values = self.values[h, pl.ds(b * self.pages, self.pages)]
        values = values.reshape(self.width, self.head_dim)
        ones = jnp.ones((self.width, self.head_dim), jnp.bfloat16)
        weights = []
        for t in range(self.width // LANES):
            s = scores[b, :, t * LANES : (t + 1) * LANES]
            weights.append(jnp.exp2((s - biggest) * self.scale).astype(jnp.bfloat16))
        self.total[...] += jnp.dot(
            jnp.concatenate(weights, axis=1),
            jnp.concatenate([values, ones], axis=1),
            preferred_element_type=jnp.float32,
        )

    def run(self, first, count, ready, take):
        for h in range(count + 1):
            if h < count:
                ready(h)
                self.start_scores(h, first + h)
            if h > 0:
                self.start_values(h - 1)

            def one_block(b, _, h=h):
                if h < count:
                    self.score_block(h, b)
                if h > 0:
                    self.value_block(h - 1, b)
                return 0

            lax.fori_loop(0, self.blocks, one_block, 0)
            if h > 0:
                take(h - 1)


def cache_copies(k_hbm, v_hbm, keys, values, sems, first):
    def copies(h):
        return (
            pltpu.make_async_copy(k_hbm.at[:, first + h], keys.at[h], sems.at[0, h]),
            pltpu.make_async_copy(v_hbm.at[:, first + h], values.at[h], sems.at[1, h]),
        )

    return copies


def attend_scratch(count, pool, page, head_dim, seqs, per_head, stride):
    keys = pool * page
    width = keys // 2
    rows = per_head * seqs
    slots = max(count, 1)
    return [
        pltpu.VMEM((seqs * stride, head_dim), jnp.bfloat16),
        pltpu.VMEM((seqs * stride, head_dim), jnp.float32),
        pltpu.VMEM((keys // width, seqs, width), jnp.float32),
        pltpu.VMEM((slots, pool, page, head_dim), jnp.bfloat16),
        pltpu.VMEM((slots, pool, page, head_dim), jnp.bfloat16),
        pltpu.VMEM((keys // width, rows, width), jnp.float32),
        pltpu.VMEM((keys // width, rows, width), jnp.float32),
        pltpu.VMEM((rows, LANES), jnp.float32),
        pltpu.VMEM((rows, LANES), jnp.float32),
        pltpu.VMEM((rows, head_dim), jnp.bfloat16),
        pltpu.VMEM((rows, 2 * head_dim), jnp.float32),
        pltpu.SemaphoreType.DMA((2, slots)),
        pltpu.SemaphoreType.DMA((1,)),
    ]


def early_kernel(
    place_ref, table_ref, length_ref, q_hbm, k_hbm, v_hbm, x_hbm, w_hbm, *refs,
    tp, scale, count, per_head,
):
    outs = 2 if count else 0
    local, (own_ref, send_ref) = refs[:outs], refs[outs : outs + 2]
    (x, w, x_sem, w_sems, raw, query, bias, keys, values, s0, s1, t0, t1, packed, total,
     sems, q_sem) = refs[outs + 2 :]
    blocks, _, width = w.shape
    copies = cache_copies(k_hbm, v_hbm, keys, values, sems, 0)
    x_copy = pltpu.make_async_copy(x_hbm, x, x_sem.at[0])
    per_owner = blocks // tp

    def w_copy(b):
        owner = lax.rem(place_ref[0] + b // per_owner, tp)
        first = pl.multiple_of((owner * per_owner + b % per_owner) * width, width)
        return pltpu.make_async_copy(w_hbm.at[:, pl.ds(first, width)], w.at[b], w_sems.at[b])

    if count:
        q_copy = pltpu.make_async_copy(q_hbm, raw, q_sem.at[0])
        q_copy.start()
        for h in range(count):
            for copy in copies(h):
                copy.start()
    x_copy.start()
    for b in range(blocks):
        w_copy(b).start()
    if count:
        make_bias(table_ref, length_ref, bias, keys.shape[2])
        q_copy.wait()
        query[...] = raw[...].astype(jnp.float32)
        attend = Attend(
            query, bias, keys, values, (s0, s1), (t0, t1), packed, total, scale, per_head
        )

        def ready(h):
            for copy in copies(h):
                copy.wait()

        def take(h):
            weight_sum = total[:, keys.shape[3] :]
            local[0][h] = total[:, : keys.shape[3]] / weight_sum
            local[1][h] = attend.tops[h % 2][...] * scale + jnp.log2(weight_sum)

        attend.run(0, count, ready, take)
    x_copy.wait()
    for b in range(blocks):
        w_copy(b).wait()
        product = jnp.dot(x[...], w[b], preferred_element_type=jnp.float32)
        part = slice(b % per_owner * width, (b % per_owner + 1) * width)
        if b < per_owner:
            own_ref[:, part] = product
        else:
            send_ref[b // per_owner - 1, :, part] = product


def early_work(place, table, lengths, queries, k_cache, v_cache, tokens, w_kv, tp, count, scale):
    seqs, stride, head_dim = queries.shape
    pool, kv_heads, page, _ = k_cache.shape
    per_head = stride // kv_heads
    rows, depth = tokens.shape
    columns = w_kv.shape[1] // tp
    width = min(256, columns)
    local_shape = jax.ShapeDtypeStruct((count, per_head * seqs, head_dim), jnp.float32)
    local = [local_shape, local_shape] if count else []
    return pl.pallas_call(
        functools.partial(early_kernel, tp=tp, scale=scale, count=count, per_head=per_head),
        in_specs=[smem(), vmem(), vmem()] + [hbm()] * 5,
        out_specs=[vmem()] * (len(local) + 2),
        out_shape=local + [
            jax.ShapeDtypeStruct((rows, columns), jnp.float32),
            jax.ShapeDtypeStruct((tp - 1, rows, columns), jnp.float32),
        ],
        scratch_shapes=[
            pltpu.VMEM((rows, depth), jnp.bfloat16),
            pltpu.VMEM((w_kv.shape[1] // width, depth, width), jnp.bfloat16),
            pltpu.SemaphoreType.DMA((1,)),
            pltpu.SemaphoreType.DMA((w_kv.shape[1] // width,)),
        ] + attend_scratch(count, pool, page, head_dim, seqs, per_head, stride),
        compiler_params=pltpu.CompilerParams(vmem_limit_bytes=VMEM_LIMIT),
        cost_estimate=pl.CostEstimate(
            flops=2 * tokens.size * w_kv.shape[1] + 8 * count * per_head * seqs * pool * page * head_dim,
            bytes_accessed=2 * w_kv.size + 4 * count * pool * page * head_dim,
            transcendentals=count * per_head * seqs * pool * page,
        ),
        name="early_heads_and_new_kv",
    )(place, table, lengths, queries.reshape(seqs * stride, head_dim), k_cache, v_cache, tokens, w_kv)


def late_kernel(
    table_ref, length_ref, own_ref, other_ref, q_hbm, k_hbm, v_hbm, *refs,
    scale, early, count, per_head, steps,
):
    ins = 2 if early else 0
    before, (state, state_lse, new_ref) = refs[:ins], refs[ins : ins + 3]
    (fresh, raw, query, bias, keys, values, s0, s1, t0, t1, packed, total,
     sems, q_sem) = refs[ins + 3 :]
    head_dim = keys.shape[3]
    seqs = bias.shape[1]
    stride = query.shape[0] // seqs
    copies = cache_copies(k_hbm, v_hbm, keys, values, sems, early)
    q_copy = pltpu.make_async_copy(q_hbm, raw, q_sem.at[0])
    q_copy.start()
    for h in range(count):
        for copy in copies(h):
            copy.start()
    make_bias(table_ref, length_ref, bias, keys.shape[2])
    q_copy.wait()
    query[...] = raw[...].astype(jnp.float32)
    new = own_ref[...]
    for k in range(other_ref.shape[0]):
        new = new + other_ref[k]
    new = new.astype(jnp.bfloat16)
    new_ref[...] = new
    for column in range(fresh.shape[0]):
        fresh[column] = new[:, column * head_dim : (column + 1) * head_dim].astype(jnp.float32)

    def join(head, part):
        new_keys, new_values = [], []
        for j in range(steps):
            every = pl.ds(j, seqs, stride=steps)
            new_keys.append(fresh[2 * head, every, :])
            new_values.append(fresh[2 * head + 1, every, :])
        for r in range(per_head):
            place = pl.ds(head * per_head + r, seqs, stride=stride)
            biggest, weight, summed = part(pl.ds(r * seqs, seqs))
            q = query[place, :]
            new_scores = [
                jnp.sum(q * new_keys[j], axis=1, keepdims=True) * scale
                for j in range(r % steps + 1)
            ]
            top = biggest
            for s in new_scores:
                top = jnp.maximum(top, s)
            factor = jnp.exp2(biggest - top)
            weight = factor * weight
            summed = factor * summed
            for j, s in enumerate(new_scores):
                w = jnp.exp2(s - top)
                weight = weight + w
                summed = summed + w * new_values[j]
            state[place, :] = summed / weight
            state_lse[place, :] = top + jnp.log2(weight)

    for h in range(early):
        join(h, lambda rows, h=h: (before[1][h, rows, :], 1.0, before[0][h, rows, :]))
    attend = Attend(query, bias, keys, values, (s0, s1), (t0, t1), packed, total, scale, per_head)

    def ready(h):
        for copy in copies(h):
            copy.wait()

    def take(h):
        top = attend.tops[h % 2]
        join(
            early + h,
            lambda rows: (top[rows, :] * scale, total[rows, head_dim:], total[rows, :head_dim]),
        )

    attend.run(early, count, ready, take)


def late_work(table, lengths, own, other, queries, k_cache, v_cache, before, steps, early, scale):
    seqs, stride, head_dim = queries.shape
    pool, kv_heads, page, _ = k_cache.shape
    per_head = stride // kv_heads
    count = kv_heads - early
    state = jax.ShapeDtypeStruct((seqs * stride, head_dim), jnp.float32)
    return pl.pallas_call(
        functools.partial(
            late_kernel, scale=scale, early=early, count=count, per_head=per_head, steps=steps
        ),
        in_specs=[vmem()] * 4 + [hbm()] * 3 + [vmem()] * len(before),
        out_specs=[vmem()] * 3,
        out_shape=[state, state, jax.ShapeDtypeStruct(own.shape, jnp.bfloat16)],
        scratch_shapes=[
            pltpu.VMEM((own.shape[1] // head_dim, own.shape[0], head_dim), jnp.float32)
        ] + attend_scratch(count, pool, page, head_dim, seqs, per_head, stride),
        compiler_params=pltpu.CompilerParams(vmem_limit_bytes=VMEM_LIMIT),
        cost_estimate=pl.CostEstimate(
            flops=8 * count * per_head * seqs * pool * page * head_dim,
            bytes_accessed=4 * count * pool * page * head_dim + 8 * seqs * stride * head_dim,
            transcendentals=count * per_head * seqs * pool * page,
        ),
        name="late_heads_and_new_keys",
    )(
        table, lengths, own, other, queries.reshape(seqs * stride, head_dim), k_cache, v_cache,
        *before,
    )


def moved_kernel(
    slot_ref, page_ref, me_ref, q_ref, k_hbm, v_hbm, out_ref, keys, values, sems, *, scale
):
    moves, kv_heads, page, head_dim = keys.shape
    rows = q_ref.shape[1]
    padding = out_ref.shape[1] - rows
    columns = kv_heads * page

    def copies(k):
        source = page_ref[me_ref[0] * moves + k]
        return (
            pltpu.make_async_copy(k_hbm.at[source], keys.at[k], sems.at[0, k]),
            pltpu.make_async_copy(v_hbm.at[source], values.at[k], sems.at[1, k]),
        )

    def start(k, _):
        for copy in copies(k):
            copy.start()
        return 0

    lax.fori_loop(0, moves, start, 0)
    out_ref[...] = jnp.zeros(out_ref.shape, jnp.bfloat16)
    row = lax.broadcasted_iota(jnp.int32, (rows, columns), 0)
    column = lax.broadcasted_iota(jnp.int32, (rows, columns), 1)
    other_head = jnp.where(row // (rows // kv_heads) == column // page, 0.0, NEGATIVE)
    tall = lax.broadcasted_iota(jnp.int32, (rows, LANES), 0)
    lane = lax.broadcasted_iota(jnp.int32, (rows, LANES), 1)
    spare = lax.broadcasted_iota(jnp.int32, (padding, LANES), 0)
    ones = jnp.ones((columns, head_dim), jnp.bfloat16)

    def one_move(k):
        s = lax.dot_general(
            q_ref[slot_ref[k]],
            keys[k].reshape(columns, head_dim),
            (((1,), (1,)), ((), ())),
            preferred_element_type=jnp.float32,
        )
        s = s + other_head
        biggest = jnp.max(s, axis=1, keepdims=True)
        weights = jnp.exp2((s - biggest) * scale).astype(jnp.bfloat16)
        both = jnp.concatenate([values[k].reshape(columns, head_dim), ones], axis=1)
        summed = jnp.dot(weights, both, preferred_element_type=jnp.float32)
        weight_sum = summed[:, head_dim:]
        lse = biggest * scale + jnp.log2(weight_sum)
        lse = jnp.sum(jnp.where(tall == lane, lse, 0.0), axis=0, keepdims=True)
        high = lse.astype(jnp.bfloat16).astype(jnp.float32)
        middle = (lse - high).astype(jnp.bfloat16).astype(jnp.float32)
        low = lse - high - middle
        pieces = jnp.where(spare == 0, high, jnp.where(spare == 1, middle, low))
        result = jnp.concatenate([summed[:, :head_dim] / weight_sum, pieces], axis=0)
        out_ref[slot_ref[k]] = result.astype(jnp.bfloat16)

    def wait(k, _):
        for copy in copies(k):
            copy.wait()
        return 0

    lax.fori_loop(0, moves, wait, 0)
    batch = min(8, moves)

    def some_moves(b, _):
        for k in range(batch):
            one_move(b * batch + k)
        return 0

    lax.fori_loop(0, moves // batch, some_moves, 0)


def moved_attention(slots, pages, me, received, k_cache, v_cache, scale):
    moves = slots.shape[0]
    _, kv_heads, page, head_dim = k_cache.shape
    count, rows, _ = received.shape
    return pl.pallas_call(
        functools.partial(moved_kernel, scale=scale),
        in_specs=[smem(), smem(), smem(), vmem(), hbm(), hbm()],
        out_specs=vmem(),
        out_shape=jax.ShapeDtypeStruct((count, answer_rows(rows), head_dim), jnp.bfloat16),
        scratch_shapes=[
            pltpu.VMEM((moves, kv_heads, page, head_dim), jnp.bfloat16),
            pltpu.VMEM((moves, kv_heads, page, head_dim), jnp.bfloat16),
            pltpu.SemaphoreType.DMA((2, moves)),
        ],
        compiler_params=pltpu.CompilerParams(vmem_limit_bytes=VMEM_LIMIT),
        cost_estimate=pl.CostEstimate(
            flops=4 * moves * rows * kv_heads * page * head_dim,
            bytes_accessed=4 * moves * kv_heads * page * head_dim + 4 * received.size,
            transcendentals=moves * rows * kv_heads * page,
        ),
        name="moved_attention",
    )(slots, pages, me, received, k_cache, v_cache)


def join_kernel(owner_ref, state_ref, lse_ref, slot_ref, out_ref, state, state_lse):
    rows = out_ref.shape[1]
    slot_size = slot_ref.shape[1]
    state[...] = state_ref[...]
    state_lse[...] = lse_ref[...]
    tall = lax.broadcasted_iota(jnp.int32, (rows, LANES), 0)
    lane = lax.broadcasted_iota(jnp.int32, (rows, LANES), 1)

    def one_slot(n, _):
        @pl.when(owner_ref[n] >= 0)
        def _():
            seq = owner_ref[n]
            block = slot_ref[n].astype(jnp.float32)
            packed = block[rows : rows + 1] + block[rows + 1 : rows + 2] + block[rows + 2 : rows + 3]
            come_lse = jnp.sum(jnp.where(tall == lane, packed, 0.0), axis=1, keepdims=True)
            lse = state_lse[seq]
            top = jnp.maximum(lse, come_lse)
            old = jnp.exp2(lse - top)
            come = jnp.exp2(come_lse - top)
            weight = old + come
            state[seq] = (old * state[seq] + come * block[:rows]) / weight
            state_lse[seq] = top + jnp.log2(weight)

        return 0

    lax.fori_loop(0, slot_ref.shape[0], one_slot, 0)
    out_ref[...] = state[...].astype(jnp.bfloat16)


def join_moved(owner, state, state_lse, answers, seqs):
    shape = (seqs, state.shape[0] // seqs, state.shape[1])
    return pl.pallas_call(
        join_kernel,
        in_specs=[smem()] + [vmem()] * 3,
        out_specs=vmem(),
        out_shape=jax.ShapeDtypeStruct(shape, jnp.bfloat16),
        scratch_shapes=[pltpu.VMEM(shape, jnp.float32), pltpu.VMEM(shape, jnp.float32)],
        compiler_params=pltpu.CompilerParams(vmem_limit_bytes=VMEM_LIMIT),
        cost_estimate=pl.CostEstimate(
            flops=10 * state.size, bytes_accessed=10 * state.size, transcendentals=0
        ),
        name="join_moved",
    )(owner, state.reshape(shape), state_lse.reshape(shape), answers)


def per_device(
    tokens_in, w_kv, queries, k_cache, v_cache, page_table, lengths, move_dest, move_page, move_seq
):
    groups = lax.axis_size("gen")
    me = lax.axis_index("gen").astype(jnp.int32).reshape(1)
    tp = lax.axis_size("tp")
    place = lax.axis_index("tp").astype(jnp.int32).reshape(1)
    seqs, steps, heads, head_dim = queries.shape
    kv_heads = k_cache.shape[1]
    scale = LOG2E / math.sqrt(head_dim)

    def exchange(array):
        return lax.all_to_all(array, "gen", split_axis=0, concat_axis=0, tiled=True)

    rows = queries.transpose(0, 2, 1, 3).reshape(seqs, heads * steps, head_dim)
    table = page_table.T
    lengths = lengths.reshape(1, seqs)
    owner, slots, to_send = gather(move_dest.reshape(-1), move_seq, me, rows, groups)
    early = kv_heads // 4
    early_rows, to_send = lax.optimization_barrier((rows, to_send))
    received = exchange(to_send)
    *before, own, partial = early_work(
        place, table, lengths, early_rows, k_cache, v_cache, tokens_in, w_kv, tp, early, scale
    )
    pieces = []
    for k in range(1, tp):
        pairs = [(i, (i + k) % tp) for i in range(tp)]
        pieces.append(lax.ppermute(partial[k - 1], "tp", pairs))
    other = jnp.stack(pieces)
    received, own = lax.optimization_barrier((received, own))
    answers = moved_attention(slots, move_page, me, received, k_cache, v_cache, scale)
    late_rows, answers = lax.optimization_barrier((rows, answers))
    returned = exchange(answers)
    state, state_lse, new_kv = late_work(
        table, lengths, own, other, late_rows, k_cache, v_cache, before, steps, early, scale
    )
    attended = join_moved(owner, state, state_lse, returned, seqs)
    attended = attended.reshape(seqs, heads, steps, head_dim).transpose(0, 2, 1, 3)
    return (attended, new_kv)


def solution(mesh):
    return jax.shard_map(
        per_device,
        mesh=mesh,
        in_specs=(
            P("gen", "tp"),
            P("tp", None),
            P("gen", None, "tp", None),
            P("gen", "tp", None, None),
            P("gen", "tp", None, None),
            P("gen", None),
            P("gen"),
            P(),
            P(),
            P(),
        ),
        out_specs=(P("gen", None, "tp", None), P("gen", "tp")),
        check_vma=False,
    )
```

time: 176 us -> 62.9 us (0.36)
  matrix products: 82.2 us -> 0 us
  Pallas kernels: 0 us -> 43.9 us
  other arithmetic: 36 us -> 0 us
  local copies, waits for them, and re-layouts: 28.4 us -> 2.29 us
  between operations: 14.4 us -> 0.71 us
    dot_general x10 -> x0, matrix products: 82.2 us -> none  [the longest x1 30.1 us: per_device(): jnp.einsum('scrd,pcqd->scrpq', query_rows, k_cache, preferred_element_typ...]
    pallas_call x0 -> x5, Pallas kernels: none -> 43.9 us  [the longest x1 16.3 us: late_work(): pl.pallas_call(functools.partial(late_kernel, scale=scale, early=early, c...]
    reduce_sum x6 -> x0, other arithmetic: 27.5 us -> none  [the longest x1 23.5 us: per_device(): local_total = jnp.sum(local_weights.astype(jnp.float32), axis=(3, 4))]
    gather x4 -> x0, local copies, waits for them, and re-layouts: 9.73 us -> none  [the longest x1 4.21 us: per_device(): k_cache[send_page]]
    select_n x4 -> x0, other arithmetic: 4.05 us -> none  [the longest x1 3.93 us: per_device(): jnp.where(sent_mask, v_cache[send_page], jnp.zeros((), v_cache.dtype))]
    reshape x5 -> x0, local copies, waits for them, and re-layouts: 3.43 us -> none  [the longest x1 1.83 us: per_device(): new_parts = new_kv.reshape(seq_dev, step_count, kv_dev, 2, head_dim)]
    convert_element_type x2 -> x0, local copies, waits for them, and re-layouts: 3.3 us -> none  [the longest x1 1.79 us: per_device(): new_kv = fresh_kv.astype(jnp.bfloat16)]
    gt x5 -> x0, local copies, waits for them, and re-layouts: 2.98 us -> none  [the longest x1 2.58 us: per_device(): visible = (usage_count > 0.5)[:, None, None]]
  transfers between devices with their start and end apart: 3 -> 3, of which waited for: 0 -> 1; matrix products, arithmetic and copies ran while one was open for 74% -> 0% of each run, Pallas kernels for 0% -> 55%
where the time goes in v2:
time: 62.9 us; the launch traced here: 63.1 us
  Pallas kernels  43.9 us (70%)
  starting transfers between devices  15 us (24%)
  local copies, waits for them, and re-layouts  2.29 us (4%)
  waiting for transfers between devices  1.3 us (2%)
  between operations  0.71 us (1%)
    pallas_call x1, Pallas kernels, late_work(): pl.pallas_call(functools.partial(late_kernel, scale=scale, early=early, c...  16.3 us
    all_to_all x2, starting transfers between devices, exchange(): return lax.all_to_all(array, 'gen', split_axis=0, concat_axis=0, tiled=True)  13.4 us
    pallas_call x1, Pallas kernels, early_work(): pl.pallas_call(functools.partial(early_kernel, tp=tp, scale=scale, count=...  13.4 us
    pallas_call x1, Pallas kernels, join_moved(): pl.pallas_call(join_kernel, in_specs=[smem()] + [vmem()] * 3, out_specs=v...  6.38 us
    pallas_call x1, Pallas kernels, moved_attention(): pl.pallas_call(functools.partial(moved_kernel, scale=scale), in_specs=[sm...  4.89 us
    pallas_call x1, Pallas kernels, gather(): pl.pallas_call(functools.partial(gather_kernel, groups=groups), in_specs=...  2.93 us
    unnamed x6, local copies, waits for them, and re-layouts  2.29 us
    ppermute x1, starting transfers between devices, per_device(): pieces.append(lax.ppermute(partial[k - 1], 'tp', pairs))  1.56 us
  transfers between devices with their start and end apart: 3, of which 1 were waited for; matrix products, arithmetic and copies ran while one was open for 0% of the time, Pallas kernels for 55%

profile of v2, /device:TPU:0, one launch (start us, length us, event | category | flops | bytes accessed | tf_op | source)
XLA Modules:
  0.0 63.1 jit_solution(4275266816630370464)
XLA Ops:
  0.6 2.9 %gather_queries.1 = (s32[33]{0:T(128)}, s32[16]{0:T(128)}, bf16[32,40,128]{2,1,0:T(8,128)(2,1)}) custom-call(s32[256]{0:T(256)} %bitcast.25, s32[256]{0:T(256)} %seq_ref.1, s32[1]{0:T(128)} %bitcast.1.me_ref, bf16[64,40,128]{2,1,0:T(8,128)(2,1)} %bitcast.17), custom_call_target="tpu_custom_call" | custom-call | bytes 1310720 | tf_op jit(solution)/shard_map/gather_queries/pallas_call | solution.py:74
  3.6 7.4 %all-to-all-start = ((bf16[32,40,128]{2,1,0:T(8,128)(2,1)}), bf16[32,40,128]{2,1,0:T(8,128)(2,1)S(1)}, u32[]{:S(2)}, u32[]{:S(2)}) async-start(bf16[32,40,128]{2,1,0:T(8,128)(2,1)} %get-tuple-element.20), calls=%async_computation | async-start | bytes 655360 | tf_op jit(solution)/shard_map/all_to_all | solution.py:555
  11.0 13.4 %early_heads_and_new_kv.1 = (f32[1,640,128]{2,1,0:T(8,128)}, f32[1,640,128]{2,1,0:T(8,128)}, f32[128,1024]{1,0:T(8,128)}, f32[1,128,1024]{2,1,0:T(8,128)}) custom-call(s32[1]{0:T(128)} %bitcast.7.place_ref, s32[32,64]{1,0:T(8,128)} %bitcast.23, s32[1,64]{1,0:T(1,128)} %bitcast.26, bf16[2560,128]{1,0:T(8,128)(2,1)} %bitcast.18, ...), custom_call_target="tpu_custom_call" | custom-call | flops 3690987520 | bytes 12320768 | tf_op jit(solution)/shard_map/early_heads_and_new_kv/pallas_call | solution.py:280
  24.4 1.6 %collective-permute-start = (f32[128,1024]{1,0:T(8,128)}, f32[128,1024]{1,0:T(8,128)S(1)}, u32[]{:S(2)}, u32[]{:S(2)}) collective-permute-start(f32[128,1024]{1,0:T(8,128)} %bitcast.29), channel_id=1, source_target_pairs={{0,1},{1,0},{2,3},{3,2},{4,5},{5,4},{6,7},{7,6},{8,9},{9,8},{10,11... | collective-permute-start | bytes 1572872 | tf_op jit(solution)/shard_map/ppermute | solution.py:570
  25.9 0.0 all-to-all-done.q_ref
  25.9 0.0 copy-start.1
  25.9 0.7 %copy-done.1 = bf16[32,40,128]{2,1,0:T(8,128)(2,1)} copy-done((bf16[32,40,128]{2,1,0:T(8,128)(2,1)}, bf16[32,40,128]{2,1,0:T(8,128)(2,1)S(1)}, u32[]{:S(2)}) %copy-start.1) | copy-done | bytes 327704
  26.7 4.9 %moved_attention.1 = bf16[32,48,128]{2,1,0:T(8,128)(2,1)} custom-call(s32[16]{0:T(128)} %get-tuple-element.25.slot_ref, s32[256]{0:T(256)} %page_ref.1, s32[1]{0:T(128)} %bitcast.1.me_ref, bf16[32,40,128]{2,1,0:T(8,128)(2,1)} %copy-done.1, bf16[56,4,64,128]{3,2,1,0:T(8,128)(2,1)} %k_hbm.5, bf16[56,4,64,128]{3,2,1,0:T(8,128)(2,1)} %v_hbm.5), custom_call_target="tpu_custom_call" | custom-call | flops 83886080 | bytes 2752512 | tf_op jit(solution)/shard_map/moved_attention/pallas_call | solution.py:478
  31.6 6.0 %all-to-all-start.1 = ((bf16[32,48,128]{2,1,0:T(8,128)(2,1)}), bf16[32,48,128]{2,1,0:T(8,128)(2,1)S(1)}, u32[]{:S(2)}, u32[]{:S(2)}) async-start(bf16[32,48,128]{2,1,0:T(8,128)(2,1)} %moved_attention.1), calls=%async_computation.1 | async-start | bytes 786432 | tf_op jit(solution)/shard_map/all_to_all | solution.py:555
  37.6 1.3 %collective-permute-done = f32[128,1024]{1,0:T(8,128)S(1)} collective-permute-done((f32[128,1024]{1,0:T(8,128)}, f32[128,1024]{1,0:T(8,128)S(1)}, u32[]{:S(2)}, u32[]{:S(2)}) %collective-permute-start) | collective-permute-done | bytes 524320 | tf_op jit(solution)/shard_map/ppermute | solution.py:570
  38.9 0.0 copy-start.2
  38.9 0.8 %copy-done.2 = f32[128,1024]{1,0:T(8,128)} copy-done((f32[128,1024]{1,0:T(8,128)}, f32[128,1024]{1,0:T(8,128)S(1)}, u32[]{:S(2)}) %copy-start.2) | copy-done | bytes 524312
  39.7 16.3 %late_heads_and_new_keys.1 = (f32[2560,128]{1,0:T(8,128)}, f32[2560,128]{1,0:T(8,128)}, bf16[128,1024]{1,0:T(8,128)(2,1)}) custom-call(s32[32,64]{1,0:T(8,128)} %bitcast.24, s32[1,64]{1,0:T(1,128)} %bitcast.27, f32[128,1024]{1,0:T(8,128)} %get-tuple-element.23.own_ref, f32[1,128,1024]{2,1,0:T(8,128)} %bitcast.28, bf16[2560,128]{1,0:T(8,128)(2,1)} %bitcast.19, ...), custom_call_target="tpu_custom_call" | custom-call | flops 7046430720 | bytes 8126464 | tf_op jit(solution)/shard_map/late_heads_and_new_keys/pallas_call | solution.py:383
  56.0 0.0 all-to-all-done.1.slot_ref
  56.0 0.0 copy-start
  56.0 0.7 %copy-done = bf16[32,48,128]{2,1,0:T(8,128)(2,1)} copy-done((bf16[32,48,128]{2,1,0:T(8,128)(2,1)}, bf16[32,48,128]{2,1,0:T(8,128)(2,1)S(1)}, u32[]{:S(2)}) %copy-start) | copy-done | bytes 393240
  56.8 6.4 %join_moved.1 = bf16[64,40,128]{2,1,0:T(8,128)(2,1)} custom-call(s32[33]{0:T(128)} %get-tuple-element.18.owner_ref, f32[64,40,128]{2,1,0:T(8,128)} %bitcast.20, f32[64,40,128]{2,1,0:T(8,128)} %bitcast.21, bf16[32,48,128]{2,1,0:T(8,128)(2,1)} %copy-done), custom_call_target="tpu_custom_call" | custom-call | flops 3276800 | bytes 3276800 | tf_op jit(solution)/shard_map/join_moved/pallas_call | solution.py:529
Async XLA Ops:
  3.6 22.4 %all-to-all-start = ((bf16[32,40,128]{2,1,0:T(8,128)(2,1)}), bf16[32,40,128]{2,1,0:T(8,128)(2,1)S(1)}, u32[]{:S(2)}, u32[]{:S(2)}) async-start(bf16[32,40,128]{2,1,0:T(8,128)(2,1)} %get-tuple-element.20), calls=%async_computation | async-start | bytes 655360 | tf_op jit(solution)/shard_map/all_to_all | solution.py:555
  24.4 14.5 %collective-permute-start = (f32[128,1024]{1,0:T(8,128)}, f32[128,1024]{1,0:T(8,128)S(1)}, u32[]{:S(2)}, u32[]{:S(2)}) collective-permute-start(f32[128,1024]{1,0:T(8,128)} %bitcast.29), channel_id=1, source_target_pairs={{0,1},{1,0},{2,3},{3,2},{4,5},{5,4},{6,7},{7,6},{8,9},{9,8},{10,11... | collective-permute-start | bytes 1572872 | tf_op jit(solution)/shard_map/ppermute | solution.py:570
  25.9 0.7 %copy-start.1 = (bf16[32,40,128]{2,1,0:T(8,128)(2,1)}, bf16[32,40,128]{2,1,0:T(8,128)(2,1)S(1)}, u32[]{:S(2)}) copy-start(bf16[32,40,128]{2,1,0:T(8,128)(2,1)S(1)} %all-to-all-done.q_ref) | copy-start | bytes 983044
  31.6 24.4 %all-to-all-start.1 = ((bf16[32,48,128]{2,1,0:T(8,128)(2,1)}), bf16[32,48,128]{2,1,0:T(8,128)(2,1)S(1)}, u32[]{:S(2)}, u32[]{:S(2)}) async-start(bf16[32,48,128]{2,1,0:T(8,128)(2,1)} %moved_attention.1), calls=%async_computation.1 | async-start | bytes 786432 | tf_op jit(solution)/shard_map/all_to_all | solution.py:555
  38.9 0.8 %copy-start.2 = (f32[128,1024]{1,0:T(8,128)}, f32[128,1024]{1,0:T(8,128)S(1)}, u32[]{:S(2)}) copy-start(f32[128,1024]{1,0:T(8,128)S(1)} %collective-permute-done) | copy-start | bytes 1572868
  56.0 0.8 %copy-start = (bf16[32,48,128]{2,1,0:T(8,128)(2,1)}, bf16[32,48,128]{2,1,0:T(8,128)(2,1)S(1)}, u32[]{:S(2)}) copy-start(bf16[32,48,128]{2,1,0:T(8,128)(2,1)S(1)} %all-to-all-done.1.slot_ref) | copy-start | bytes 1179652

commit v3 on v2

v3 whole, which is shorter than its diff:
```python
import functools
import math

import jax
import jax.numpy as jnp
from jax import lax
from jax.experimental import pallas as pl
from jax.experimental.pallas import tpu as pltpu
from jax.sharding import PartitionSpec as P

CAP = 2
NEGATIVE = -1e30
LOG2E = 1.4426950408889634
LANES = 128
MIB = 1024 * 1024


def smem():
    return pl.BlockSpec(memory_space=pltpu.SMEM)


def vmem():
    return pl.BlockSpec(memory_space=pltpu.VMEM)


def hbm():
    return pl.BlockSpec(memory_space=pltpu.HBM)


def stay(array):
    return pltpu.with_memory_space_constraint(array, pltpu.HBM)


def limit(mib):
    return pltpu.CompilerParams(vmem_limit_bytes=mib * MIB)


def padded(rows):
    return (rows + 7) // 8 * 8


def answer_rows(rows):
    return (rows + 3 + 15) // 16 * 16


def fill_owner(dest, seq, me, owner, per_source):
    groups = dest.shape[0] // per_source
    slots = groups * CAP

    def clear(n, _):
        owner[n] = -1
        return 0

    lax.fori_loop(0, slots, clear, 0, unroll=8)

    def one_source(source, _):
        count = jnp.int32(0)
        for k in range(per_source):
            row = source * per_source + k
            hit = dest[row] == me
            owner[jnp.where(hit, source * CAP + count, slots)] = seq[row]
            count = count + hit.astype(jnp.int32)
        return 0

    lax.fori_loop(0, groups, one_source, 0)


def first_slots(owner, first, seen):
    def unseen(n, _):
        seen[n] = -1
        return 0

    lax.fori_loop(0, seen.shape[0], unseen, 0, unroll=8)

    def first_slot(n, _):
        sequence = owner[n]
        place = jnp.maximum(sequence, 0)
        earlier = seen[place]
        mine = jnp.where(earlier < 0, n, earlier)
        seen[place] = jnp.where(sequence < 0, earlier, mine)
        first[n] = jnp.where(sequence < 0, -1, mine)
        return 0

    lax.fori_loop(0, first.shape[0], first_slot, 0)


def gather_kernel(
    dest_hbm, seq_hbm, q_hbm, out_ref, dest, seq, owner, queries, sems, *, per_source
):
    me = lax.axis_index("gen")
    copies = [
        pltpu.make_async_copy(dest_hbm, dest, sems.at[0]),
        pltpu.make_async_copy(seq_hbm, seq, sems.at[1]),
        pltpu.make_async_copy(q_hbm, queries, sems.at[2]),
    ]
    for copy in copies:
        copy.start()
    copies[0].wait()
    copies[1].wait()
    fill_owner(dest, seq, me, owner, per_source)
    copies[2].wait()

    def one_slot(n, _):
        out_ref[n] = queries[jnp.maximum(owner[n], 0)]
        return 0

    lax.fori_loop(0, out_ref.shape[0], one_slot, 0, unroll=8)


def gather(dest, seq, queries, groups):
    slots = groups * CAP
    _, rows, head_dim = queries.shape
    return pl.pallas_call(
        functools.partial(gather_kernel, per_source=dest.shape[0] // groups),
        in_specs=[hbm()] * 3,
        out_specs=vmem(),
        out_shape=jax.ShapeDtypeStruct((slots, rows, head_dim), jnp.bfloat16),
        scratch_shapes=[
            pltpu.SMEM(dest.shape, jnp.int32),
            pltpu.SMEM(seq.shape, jnp.int32),
            pltpu.SMEM((slots + 1,), jnp.int32),
            pltpu.VMEM(queries.shape, jnp.bfloat16),
            pltpu.SemaphoreType.DMA((3,)),
        ],
        compiler_params=limit(4),
        cost_estimate=pl.CostEstimate(flops=0, bytes_accessed=4 * queries.size, transcendentals=0),
        name="gather_queries",
    )(stay(dest), stay(seq), stay(queries))


def make_bias(table_ref, length_ref, bias, page):
    blocks, seqs, width = bias.shape
    pool = padded(blocks * width // page)
    lengths = length_ref[...].astype(jnp.float32)
    page_id = lax.broadcasted_iota(jnp.int32, (pool, seqs), 0)
    used = jnp.zeros((pool, seqs), jnp.float32)
    for j in range(table_ref.shape[0]):
        inside = jnp.clip(lengths - float(page * j), 0.0, float(page))
        used = used + jnp.where(table_ref[j : j + 1, :] == page_id, inside, 0.0)
    used = used.T.astype(jnp.bfloat16)

    def one_block(b, _):
        key = lax.broadcasted_iota(jnp.int32, (pool, width), 1) + b * width
        owner = lax.broadcasted_iota(jnp.int32, (pool, width), 0)
        expand = jnp.where(key // page == owner, 1.0, 0.0).astype(jnp.bfloat16)
        count = jnp.dot(used, expand, preferred_element_type=jnp.float32)
        position = lax.broadcasted_iota(jnp.int32, (seqs, width), 1) % page
        bias[b] = jnp.where(position.astype(jnp.float32) < count, 0.0, NEGATIVE)
        return 0

    lax.fori_loop(0, blocks, one_block, 0)


class Attend:
    def __init__(self, query, bias, keys, values, scores, tops, packed, total, scale, per_head):
        self.query, self.bias, self.keys, self.values = query, bias, keys, values
        self.scores, self.tops, self.packed, self.total = scores, tops, packed, total
        self.scale, self.per_head = scale, per_head
        self.blocks, self.seqs, self.width = bias.shape
        self.head_dim = query.shape[1]
        self.stride = query.shape[0] // self.seqs
        self.rows = per_head * self.seqs
        self.pages = self.width // keys.shape[2]

    def start_scores(self, h, head):
        for r in range(self.per_head):
            rows = self.query[pl.ds(head * self.per_head + r, self.seqs, stride=self.stride), :]
            self.packed[pl.ds(r * self.seqs, self.seqs), :] = rows.astype(jnp.bfloat16)
        self.tops[h % 2][...] = jnp.full(self.tops[0].shape, NEGATIVE, jnp.float32)

    def product(self, keys):
        return lax.dot_general(
            self.packed[...], keys, (((1,), (1,)), ((), ())), preferred_element_type=jnp.float32
        )

    def score_block(self, h, b):
        top = self.tops[h % 2]
        keys = self.keys[h, pl.ds(b * self.pages, self.pages)].reshape(self.width, self.head_dim)
        s = self.product(keys).reshape(self.per_head, self.seqs, self.width) + self.bias[b][None]
        s = s.reshape(self.rows, self.width)
        self.scores[h % 2][b] = s
        largest = s[:, :LANES]
        for t in range(1, self.width // LANES):
            largest = jnp.maximum(largest, s[:, t * LANES : (t + 1) * LANES])
        top[...] = jnp.maximum(top[...], largest)

    def start_values(self, h):
        top = self.tops[h % 2]
        top[...] = jnp.broadcast_to(jnp.max(top[...], axis=1, keepdims=True), top.shape)
        self.total[...] = jnp.zeros(self.total.shape, jnp.float32)

    def weigh(self, weights, values):
        return jnp.dot(
            weights,
            jnp.concatenate([values, jnp.ones(values.shape, jnp.bfloat16)], axis=1),
            preferred_element_type=jnp.float32,
        )

    def value_block(self, h, b):
        scores, biggest = self.scores[h % 2], self.tops[h % 2][...]
        values = self.values[h, pl.ds(b * self.pages, self.pages)]
        weights = []
        for t in range(self.width // LANES):
            s = scores[b, :, t * LANES : (t + 1) * LANES]
            weights.append(jnp.exp2((s - biggest) * self.scale).astype(jnp.bfloat16))
        self.total[...] += self.weigh(
            jnp.concatenate(weights, axis=1), values.reshape(self.width, self.head_dim)
        )

    def run(self, first, count, keys_ready, values_ready, take):
        for h in range(count + 1):
            if h < count:
                keys_ready(h)
                self.start_scores(h, first + h)
            if h > 0:
                values_ready(h - 1)
                self.start_values(h - 1)

            def one_block(b, _, h=h):
                if h < count:
                    self.score_block(h, b)
                if h > 0:
                    self.value_block(h - 1, b)
                return 0

            lax.fori_loop(0, self.blocks, one_block, 0)
            if h > 0:
                take(h - 1)


def attend_scratch(seqs, per_head, pool, page, head_dim, pairs):
    keys = pool * page
    width = keys // 2
    rows = per_head * seqs
    scores = [pltpu.VMEM((keys // width, rows, width), jnp.float32) for _ in range(pairs)]
    tops = [pltpu.VMEM((rows, LANES), jnp.float32) for _ in range(pairs)]
    return scores + tops + [
        pltpu.VMEM((rows, head_dim), jnp.bfloat16),
        pltpu.VMEM((rows, 2 * head_dim), jnp.float32),
    ]


def start_all(copies):
    for copy in copies:
        copy.start()


def wait_all(copies):
    for copy in copies:
        copy.wait()


def early_kernel(
    table_hbm, length_hbm, pages_hbm, q_hbm, x_hbm, dest_hbm, seq_hbm, k_hbm, v_hbm, w_hbm, *refs,
    tp, scale, count, per_head,
):
    outs = 2 if count else 0
    local_hbm = refs[:outs]
    own_hbm, owner_hbm, first_hbm, send_ref, move_keys, move_values = refs[outs : outs + 6]
    (table, lengths, pages, raw, query, bias, x, dest, seq, owner, first, seen, w, keys, values, own,
     small_sems, cache_sems, move_sems, w_sems, out_sems, *attend_refs) = refs[outs + 6 :]
    pairs = min(count, 2)
    scores, tops = attend_refs[:pairs], attend_refs[pairs : 2 * pairs]
    blocks, _, width = w.shape
    moves = move_keys.shape[0]
    head_dim = keys.shape[3]
    per_owner = blocks // tp
    me, place = lax.axis_index("gen"), lax.axis_index("tp")
    small = [
        pltpu.make_async_copy(source, target, small_sems.at[k])
        for k, (source, target) in enumerate(
            [(dest_hbm, dest), (seq_hbm, seq), (table_hbm, table), (length_hbm, lengths),
             (pages_hbm, pages), (q_hbm, raw), (x_hbm, x)]
        )
    ]
    own_copy = pltpu.make_async_copy(own, own_hbm, out_sems.at[2])
    table_copies = [
        pltpu.make_async_copy(owner, owner_hbm, out_sems.at[3]),
        pltpu.make_async_copy(first, first_hbm, out_sems.at[4]),
    ]

    def key_copy(h):
        return pltpu.make_async_copy(k_hbm.at[:, h], keys.at[h], cache_sems.at[0, h])

    def value_copy(h):
        return pltpu.make_async_copy(v_hbm.at[:, h], values.at[h], cache_sems.at[1, h])

    def w_copy(b):
        owner = lax.rem(place + b // per_owner, tp)
        start = pl.multiple_of((owner * per_owner + b % per_owner) * width, width)
        return pltpu.make_async_copy(w_hbm.at[:, pl.ds(start, width)], w.at[b], w_sems.at[b])

    def move_copies(k):
        page = pages[me * moves + k]
        return (
            pltpu.make_async_copy(k_hbm.at[page], move_keys.at[k], move_sems.at[0, k]),
            pltpu.make_async_copy(v_hbm.at[page], move_values.at[k], move_sems.at[1, k]),
        )

    def start_move(k, _):
        start_all(move_copies(k))
        return 0

    def wait_move(k, _):
        wait_all(move_copies(k))
        return 0

    def start_weights(first, last):
        for b in range(first, last):
            w_copy(b).start()

    start_all(small[:6])
    if count:
        key_copy(0).start()
    wait_all(small[:2])
    fill_owner(dest, seq, me, owner, moves)
    first_slots(owner, first, seen)
    start_all(table_copies)
    wait_all(small[2:6])
    if count:
        make_bias(table, lengths, bias, keys.shape[2])
        query[...] = raw[...].astype(jnp.float32)
        packed, total, out, out_lse = attend_refs[2 * pairs :]
        attend = Attend(query, bias, keys, values, scores, tops, packed, total, scale, per_head)
        local_copies = [
            pltpu.make_async_copy(out, local_hbm[0], out_sems.at[0]),
            pltpu.make_async_copy(out_lse, local_hbm[1], out_sems.at[1]),
        ]

        def keys_ready(h):
            key_copy(h).wait()
            value_copy(h).start()
            if h + 1 < count:
                key_copy(h + 1).start()
            if h == count - 1:
                small[6].start()
                start_weights(0, blocks // 2)

        def values_ready(h):
            value_copy(h).wait()
            if h == count - 1:
                start_weights(blocks // 2, blocks)
                lax.fori_loop(0, moves, start_move, 0)

        def take(h):
            weight_sum = total[:, head_dim:]
            out[h] = total[:, :head_dim] / weight_sum
            out_lse[h] = attend.tops[h % 2][...] * scale + jnp.log2(weight_sum)

        attend.run(0, count, keys_ready, values_ready, take)
        start_all(local_copies)
    else:
        small[6].start()
        start_weights(0, blocks)
        lax.fori_loop(0, moves, start_move, 0)
    small[6].wait()
    for b in range(blocks):
        w_copy(b).wait()
        product = jnp.dot(x[...], w[b], preferred_element_type=jnp.float32)
        part = slice(b % per_owner * width, (b % per_owner + 1) * width)
        if b < per_owner:
            own[:, part] = product
            if b == per_owner - 1:
                own_copy.start()
        else:
            send_ref[b // per_owner - 1, :, part] = product.astype(jnp.bfloat16)
    lax.fori_loop(0, moves, wait_move, 0)
    own_copy.wait()
    wait_all(table_copies)
    if count:
        wait_all(local_copies)


def early_work(
    table, lengths, pages, queries, tokens, dest, seq, k_cache, v_cache, w_kv, groups, tp, count, scale
):
    seqs, stride, head_dim = queries.shape
    pool, kv_heads, page, _ = k_cache.shape
    per_head = stride // kv_heads
    rows, depth = tokens.shape
    moves, slots = dest.shape[0] // groups, groups * CAP
    columns = w_kv.shape[1] // tp
    width = min(512, columns)
    blocks = w_kv.shape[1] // width
    keys = pool * page
    f32, bf16 = jnp.float32, jnp.bfloat16
    local_shape = (count, per_head * seqs, head_dim)
    local = [pltpu.HBM(local_shape, f32)] * 2 if count else []
    scratch = [
        pltpu.VMEM(table.shape, jnp.int32),
        pltpu.VMEM(lengths.shape, jnp.int32),
        pltpu.SMEM(pages.shape, jnp.int32),
        pltpu.VMEM((seqs * stride, head_dim), bf16),
        pltpu.VMEM((seqs * stride, head_dim), f32),
        pltpu.VMEM((2, seqs, keys // 2), f32),
        pltpu.VMEM((rows, depth), bf16),
        pltpu.SMEM(dest.shape, jnp.int32),
        pltpu.SMEM(seq.shape, jnp.int32),
        pltpu.SMEM((slots + 1,), jnp.int32),
        pltpu.SMEM((slots,), jnp.int32),
        pltpu.SMEM((seqs,), jnp.int32),
        pltpu.VMEM((blocks, depth, width), bf16),
        pltpu.VMEM((max(count, 1), pool, page, head_dim), bf16),
        pltpu.VMEM((max(count, 1), pool, page, head_dim), bf16),
        pltpu.VMEM((rows, columns), f32),
        pltpu.SemaphoreType.DMA((7,)),
        pltpu.SemaphoreType.DMA((2, max(count, 1))),
        pltpu.SemaphoreType.DMA((2, moves)),
        pltpu.SemaphoreType.DMA((blocks,)),
        pltpu.SemaphoreType.DMA((5,)),
    ]
    if count:
        scratch += attend_scratch(seqs, per_head, pool, page, head_dim, min(count, 2))
        scratch += [pltpu.VMEM(local_shape, f32)] * 2
    return pl.pallas_call(
        functools.partial(early_kernel, tp=tp, scale=scale, count=count, per_head=per_head),
        in_specs=[hbm()] * 10,
        out_specs=[hbm()] * (len(local) + 3) + [vmem()] * 3,
        out_shape=local + [
            pltpu.HBM((rows, columns), f32),
            pltpu.HBM((slots + 1,), jnp.int32),
            pltpu.HBM((slots,), jnp.int32),
            jax.ShapeDtypeStruct((tp - 1, rows, columns), bf16),
            jax.ShapeDtypeStruct((moves,) + k_cache.shape[1:], bf16),
            jax.ShapeDtypeStruct((moves,) + k_cache.shape[1:], bf16),
        ],
        scratch_shapes=scratch,
        compiler_params=limit(44),
        cost_estimate=pl.CostEstimate(
            flops=2 * tokens.size * w_kv.shape[1] + 8 * count * per_head * seqs * keys * head_dim,
            bytes_accessed=2 * w_kv.size + 4 * count * keys * head_dim,
            transcendentals=count * per_head * seqs * keys,
        ),
        name="early_heads_and_new_kv",
    )(
        stay(table), stay(lengths), stay(pages), stay(queries.reshape(seqs * stride, head_dim)),
        stay(tokens), stay(dest), stay(seq), stay(k_cache), stay(v_cache), stay(w_kv),
    )


def late_kernel(
    table_hbm, length_hbm, q_hbm, k_hbm, v_hbm, own_hbm, *refs, scale, early, count, per_head
):
    ins = 2 if early else 0
    before_hbm = refs[:ins]
    state, state_lse, query, own = refs[ins : ins + 4]
    table, lengths, raw, bias, keys, values, sems, cache_sems, *attend_refs = refs[ins + 4 :]
    pairs = min(count, 2)
    scores, tops = attend_refs[:pairs], attend_refs[pairs : 2 * pairs]
    packed, total = attend_refs[2 * pairs : 2 * pairs + 2]
    before = attend_refs[2 * pairs + 2 :]
    seqs, stride, head_dim = state.shape
    flat = (seqs * stride, head_dim)
    rows, rows_lse = state.reshape(flat), state_lse.reshape(flat)
    pairs_in = [(table_hbm, table), (length_hbm, lengths), (q_hbm, raw), (own_hbm, own)]
    pairs_in += list(zip(before_hbm, before))
    small = [
        pltpu.make_async_copy(source, target, sems.at[k])
        for k, (source, target) in enumerate(pairs_in)
    ]

    def key_copy(h):
        return pltpu.make_async_copy(k_hbm.at[:, early + h], keys.at[h], cache_sems.at[0, h])

    def value_copy(h):
        return pltpu.make_async_copy(v_hbm.at[:, early + h], values.at[h], cache_sems.at[1, h])

    start_all(small[:3])
    key_copy(0).start()
    wait_all(small[:2])
    make_bias(table, lengths, bias, keys.shape[2])
    small[2].wait()
    query[...] = raw[...].astype(jnp.float32)
    attend = Attend(query, bias, keys, values, scores, tops, packed, total, scale, per_head)

    def keys_ready(h):
        key_copy(h).wait()
        value_copy(h).start()
        if h + 1 < count:
            key_copy(h + 1).start()
        if h == count - 1:
            start_all(small[3:])

    def values_ready(h):
        value_copy(h).wait()

    def take(h):
        top = attend.tops[h % 2]
        for r in range(per_head):
            place = pl.ds((early + h) * per_head + r, seqs, stride=stride)
            part = pl.ds(r * seqs, seqs)
            weight_sum = total[part, head_dim:]
            rows[place, :] = total[part, :head_dim] / weight_sum
            rows_lse[place, :] = top[part, :] * scale + jnp.log2(weight_sum)

    attend.run(early, count, keys_ready, values_ready, take)
    wait_all(small[3:])
    for h in range(early):
        for r in range(per_head):
            place = pl.ds(h * per_head + r, seqs, stride=stride)
            part = pl.ds(r * seqs, seqs)
            rows[place, :] = before[0][h, part, :]
            rows_lse[place, :] = before[1][h, part, :]


def late_work(table, lengths, queries, k_cache, v_cache, own, before, early, scale):
    pool, kv_heads, page, head_dim = k_cache.shape
    seqs, stride, _ = queries.shape
    per_head = stride // kv_heads
    count = kv_heads - early
    rows = per_head * seqs
    keys = pool * page
    pairs = min(count, 2)
    f32, bf16 = jnp.float32, jnp.bfloat16
    state = jax.ShapeDtypeStruct((seqs, padded(stride), head_dim), f32)
    return pl.pallas_call(
        functools.partial(late_kernel, scale=scale, early=early, count=count, per_head=per_head),
        in_specs=[hbm()] * (6 + len(before)),
        out_specs=[vmem()] * 4,
        out_shape=[
            state,
            state,
            jax.ShapeDtypeStruct((seqs * stride, head_dim), f32),
            jax.ShapeDtypeStruct(own.shape, f32),
        ],
        scratch_shapes=[
            pltpu.VMEM(table.shape, jnp.int32),
            pltpu.VMEM(lengths.shape, jnp.int32),
            pltpu.VMEM((seqs * stride, head_dim), bf16),
            pltpu.VMEM((2, seqs, keys // 2), f32),
            pltpu.VMEM((count, pool, page, head_dim), bf16),
            pltpu.VMEM((count, pool, page, head_dim), bf16),
            pltpu.SemaphoreType.DMA((6,)),
            pltpu.SemaphoreType.DMA((2, count)),
        ] + attend_scratch(seqs, per_head, pool, page, head_dim, pairs) + [
            pltpu.VMEM(array.shape, f32) for array in before
        ],
        compiler_params=limit(40),
        cost_estimate=pl.CostEstimate(
            flops=8 * count * rows * keys * head_dim,
            bytes_accessed=4 * count * keys * head_dim,
            transcendentals=count * rows * keys,
        ),
        name="late_heads",
    )(
        stay(table), stay(lengths), stay(queries.reshape(seqs * stride, head_dim)), stay(k_cache),
        stay(v_cache), stay(own), *[stay(array) for array in before],
    )


def new_kernel(
    own_ref, other_ref, query, old_ref, old_lse_ref, new_hbm, state, state_lse, new, fresh, sem,
    *, per_head, steps, scale,
):
    seqs, stride, head_dim = state.shape
    flat = (seqs * stride, head_dim)
    rows, rows_lse = state.reshape(flat), state_lse.reshape(flat)
    old, old_lse = old_ref.reshape(flat), old_lse_ref.reshape(flat)
    real = query.shape[0] // seqs
    partial = own_ref[...]
    for k in range(other_ref.shape[0]):
        partial = partial + other_ref[k].astype(jnp.float32)
    new[...] = partial.astype(jnp.bfloat16)
    copy = pltpu.make_async_copy(new, new_hbm, sem.at[0])
    copy.start()
    for column in range(fresh.shape[0]):
        columns = slice(column * head_dim, (column + 1) * head_dim)
        fresh[column] = new[:, columns].astype(jnp.float32)
    for h in range(real // per_head):
        new_keys, new_values = [], []
        for j in range(steps):
            every = pl.ds(j, seqs, stride=steps)
            new_keys.append(fresh[2 * h, every, :])
            new_values.append(fresh[2 * h + 1, every, :])
        for r in range(per_head):
            place = pl.ds(h * per_head + r, seqs, stride=stride)
            q = query[pl.ds(h * per_head + r, seqs, stride=real), :]
            scores = [
                jnp.sum(q * new_keys[j], axis=1, keepdims=True) * scale
                for j in range(r % steps + 1)
            ]
            lse = old_lse[place, :]
            top = lse
            for s in scores:
                top = jnp.maximum(top, s)
            weight = jnp.exp2(lse - top)
            summed = weight * old[place, :]
            for j, s in enumerate(scores):
                w = jnp.exp2(s - top)
                weight = weight + w
                summed = summed + w * new_values[j]
            rows[place, :] = summed / weight
            rows_lse[place, :] = top + jnp.log2(weight)
    copy.wait()


def join_new(own, other, query, old, old_lse, per_head, steps, scale):
    head_dim = query.shape[1]
    return pl.pallas_call(
        functools.partial(new_kernel, per_head=per_head, steps=steps, scale=scale),
        in_specs=[vmem()] * 5,
        out_specs=[hbm(), vmem(), vmem()],
        out_shape=[
            jax.ShapeDtypeStruct(own.shape, jnp.bfloat16),
            jax.ShapeDtypeStruct(old.shape, jnp.float32),
            jax.ShapeDtypeStruct(old.shape, jnp.float32),
        ],
        scratch_shapes=[
            pltpu.VMEM(own.shape, jnp.bfloat16),
            pltpu.VMEM((own.shape[1] // head_dim, own.shape[0], head_dim), jnp.float32),
            pltpu.SemaphoreType.DMA((1,)),
        ],
        compiler_params=limit(8),
        cost_estimate=pl.CostEstimate(
            flops=20 * query.size, bytes_accessed=20 * query.size, transcendentals=4 * query.size
        ),
        name="join_new",
    )(own, other, query, old, old_lse)


def moved_kernel(dest_ref, q_ref, keys, values, out_ref, slot, *, scale):
    moves, kv_heads, page, head_dim = keys.shape
    rows = q_ref.shape[1]
    padding = out_ref.shape[1] - rows
    columns = kv_heads * page
    me = lax.axis_index("gen")
    for k in range(moves):
        mine = dest_ref[me * moves + k]
        rank = jnp.int32(0)
        for j in range(k):
            rank = rank + (dest_ref[me * moves + j] == mine).astype(jnp.int32)
        slot[k] = mine * CAP + rank
    out_ref[...] = jnp.zeros(out_ref.shape, jnp.bfloat16)
    row = lax.broadcasted_iota(jnp.int32, (rows, columns), 0)
    column = lax.broadcasted_iota(jnp.int32, (rows, columns), 1)
    other_head = jnp.where(row // (rows // kv_heads) == column // page, 0.0, NEGATIVE)
    tall = lax.broadcasted_iota(jnp.int32, (rows, LANES), 0)
    lane = lax.broadcasted_iota(jnp.int32, (rows, LANES), 1)
    spare = lax.broadcasted_iota(jnp.int32, (padding, LANES), 0)
    ones = jnp.ones((columns, head_dim), jnp.bfloat16)

    def one_move(k):
        s = lax.dot_general(
            q_ref[slot[k]],
            keys[k].reshape(columns, head_dim),
            (((1,), (1,)), ((), ())),
            preferred_element_type=jnp.float32,
        )
        s = s + other_head
        biggest = jnp.max(s, axis=1, keepdims=True)
        weights = jnp.exp2((s - biggest) * scale).astype(jnp.bfloat16)
        both = jnp.concatenate([values[k].reshape(columns, head_dim), ones], axis=1)
        summed = jnp.dot(weights, both, preferred_element_type=jnp.float32)
        weight_sum = summed[:, head_dim:]
        lse = biggest * scale + jnp.log2(weight_sum)
        lse = jnp.sum(jnp.where(tall == lane, lse, 0.0), axis=0, keepdims=True)
        high = lse.astype(jnp.bfloat16).astype(jnp.float32)
        middle = (lse - high).astype(jnp.bfloat16).astype(jnp.float32)
        low = lse - high - middle
        pieces = jnp.where(spare == 0, high, jnp.where(spare == 1, middle, low))
        result = jnp.concatenate([summed[:, :head_dim] / weight_sum, pieces], axis=0)
        return result.astype(jnp.bfloat16)

    batch = min(16, moves)

    def some_moves(b, _):
        results = [one_move(b * batch + k) for k in range(batch)]
        for k in range(batch):
            out_ref[slot[b * batch + k]] = results[k]
        return 0

    lax.fori_loop(0, moves // batch, some_moves, 0)


def moved_attention(dest, received, move_keys, move_values, scale):
    moves, kv_heads, page, head_dim = move_keys.shape
    count, rows, _ = received.shape
    return pl.pallas_call(
        functools.partial(moved_kernel, scale=scale),
        in_specs=[smem(), vmem(), vmem(), vmem()],
        out_specs=vmem(),
        out_shape=jax.ShapeDtypeStruct((count, answer_rows(rows), head_dim), jnp.bfloat16),
        scratch_shapes=[pltpu.SMEM((moves,), jnp.int32)],
        compiler_params=limit(4),
        cost_estimate=pl.CostEstimate(
            flops=4 * moves * rows * kv_heads * page * head_dim,
            bytes_accessed=4 * received.size,
            transcendentals=moves * rows * kv_heads * page,
        ),
        name="moved_attention",
    )(dest, received, move_keys, move_values)


def join_kernel(owner_ref, first_ref, state_ref, lse_ref, slot_ref, out_ref, states, states_lse):
    seqs, rows, head_dim = out_ref.shape
    count = slot_ref.shape[0]
    out_ref[...] = state_ref[:, :rows, :].astype(jnp.bfloat16)
    tall = lax.broadcasted_iota(jnp.int32, (rows, LANES), 0)
    lane = lax.broadcasted_iota(jnp.int32, (rows, LANES), 1)
    real = pl.ds(0, rows)

    def one_slot(n, _):
        first = first_ref[n]

        @pl.when(first == n)
        def _():
            states[n] = state_ref[owner_ref[n], real]
            states_lse[n] = lse_ref[owner_ref[n], real]

        @pl.when(first >= 0)
        def _():
            block = slot_ref[n].astype(jnp.float32)
            packed = block[rows : rows + 1] + block[rows + 1 : rows + 2] + block[rows + 2 : rows + 3]
            come_lse = jnp.sum(jnp.where(tall == lane, packed, 0.0), axis=1, keepdims=True)
            lse = states_lse[first]
            top = jnp.maximum(lse, come_lse)
            old = jnp.exp2(lse - top)
            come = jnp.exp2(come_lse - top)
            weight = old + come
            joined = (old * states[first] + come * block[:rows]) / weight
            states[first] = joined
            states_lse[first] = top + jnp.log2(weight)
            out_ref[owner_ref[n]] = joined.astype(jnp.bfloat16)

        return 0

    lax.fori_loop(0, count, one_slot, 0)


def join_moved(owner, first, state, state_lse, answers, shape):
    slots = first.shape[0]
    return pl.pallas_call(
        join_kernel,
        in_specs=[smem()] * 2 + [vmem()] * 3,
        out_specs=vmem(),
        out_shape=jax.ShapeDtypeStruct(shape, jnp.bfloat16),
        scratch_shapes=[pltpu.VMEM((slots,) + shape[1:], jnp.float32)] * 2,
        compiler_params=limit(8),
        cost_estimate=pl.CostEstimate(
            flops=10 * state.size, bytes_accessed=10 * state.size, transcendentals=0
        ),
        name="join_moved",
    )(owner, first, state, state_lse, answers)


def per_device(
    tokens_in, w_kv, queries, k_cache, v_cache, page_table, lengths, move_dest, move_page, move_seq
):
    groups = lax.axis_size("gen")
    tp = lax.axis_size("tp")
    seqs, steps, heads, head_dim = queries.shape
    kv_heads = k_cache.shape[1]
    scale = LOG2E / math.sqrt(head_dim)

    def exchange(array):
        return lax.all_to_all(array, "gen", split_axis=0, concat_axis=0, tiled=True)

    rows = queries.transpose(0, 2, 1, 3).reshape(seqs, heads * steps, head_dim)
    dest = move_dest.reshape(-1)
    to_send = gather(dest, move_seq, rows, groups)
    early = kv_heads // 2
    early_rows, to_send = lax.optimization_barrier((rows, to_send))
    received = exchange(to_send)
    table, lengths = page_table.T, lengths.reshape(1, seqs)
    *before, own, owner, first, partial, move_keys, move_values = early_work(
        table, lengths, move_page, early_rows, tokens_in, dest, move_seq, k_cache, v_cache, w_kv,
        groups, tp, early, scale,
    )
    pieces = []
    for k in range(1, tp):
        pairs = [(i, (i + k) % tp) for i in range(tp)]
        pieces.append(lax.ppermute(partial[k - 1], "tp", pairs))
    other = jnp.stack(pieces)
    answers = moved_attention(dest, received, move_keys, move_values, scale)
    late_rows, answers = lax.optimization_barrier((rows, answers))
    returned = exchange(answers)
    state, state_lse, query, own = late_work(
        table, lengths, late_rows, k_cache, v_cache, own, before, early, scale
    )
    new_kv, state, state_lse = join_new(
        own, other, query, state, state_lse, heads * steps // kv_heads, steps, scale
    )
    attended = join_moved(
        owner, first, state, state_lse, returned, (seqs, heads * steps, head_dim)
    )
    attended = attended.reshape(seqs, heads, steps, head_dim).transpose(0, 2, 1, 3)
    return (attended, new_kv)


def solution(mesh):
    return jax.shard_map(
        per_device,
        mesh=mesh,
        in_specs=(
            P("gen", "tp"),
            P("tp", None),
            P("gen", None, "tp", None),
            P("gen", "tp", None, None),
            P("gen", "tp", None, None),
            P("gen", None),
            P("gen"),
            P(),
            P(),
            P(),
        ),
        out_specs=(P("gen", None, "tp", None), P("gen", "tp")),
        check_vma=False,
    )
```

time: 62.9 us -> 47.2 us (0.75); the launches traced: 63.1 us -> 46.8 us
  Pallas kernels: 43.9 us -> 30.7 us
  local copies, waits for them, and re-layouts: 2.29 us -> 0.01 us
  waiting for transfers between devices: 1.3 us -> 0.39 us
    pallas_call x1, Pallas kernels: 16.3 us -> 8.52 us  [late_work(): pl.pallas_call(functools.partial(late_kernel, scale=scale, early=early, c...]
    pallas_call x1, Pallas kernels: 4.89 us -> 2.34 us  [moved_attention(): pl.pallas_call(functools.partial(moved_kernel, scale=scale), in_specs=[sm...]
    unnamed x6, local copies, waits for them, and re-layouts: 2.29 us -> 0.01 us
    pallas_call x2 -> x3, Pallas kernels: 9.31 us -> 7.72 us  [the longest x1 3.68 us: join_moved(): pl.pallas_call(join_kernel, in_specs=[smem()] * 2 + [vmem()] * 3, out_spe...]
    pallas_call x1, Pallas kernels: 13.4 us -> 12.1 us  [early_work(): pl.pallas_call(functools.partial(early_kernel, tp=tp, scale=scale, count=...]
    ppermute x1, waiting for transfers between devices: 1.3 us -> 0.01 us  [per_device(): pieces.append(lax.ppermute(partial[k - 1], 'tp', pairs))]
  transfers between devices with their start and end apart: 3 -> 3, of which waited for: 1 -> 1; matrix products, arithmetic and copies ran while one was open for 0% -> 0% of each run, Pallas kernels for 55% -> 48%
where the time goes in v3:
time: 47.2 us; the launch traced here: 46.8 us
  Pallas kernels  30.7 us (65%)
  starting transfers between devices  15 us (32%)
  between operations  0.73 us (2%)
    all_to_all x2, starting transfers between devices, exchange(): return lax.all_to_all(array, 'gen', split_axis=0, concat_axis=0, tiled=True)  13.4 us
    pallas_call x1, Pallas kernels, early_work(): pl.pallas_call(functools.partial(early_kernel, tp=tp, scale=scale, count=...  12.1 us
    pallas_call x1, Pallas kernels, late_work(): pl.pallas_call(functools.partial(late_kernel, scale=scale, early=early, c...  8.52 us
    pallas_call x1, Pallas kernels, join_moved(): pl.pallas_call(join_kernel, in_specs=[smem()] * 2 + [vmem()] * 3, out_spe...  3.68 us
    pallas_call x1, Pallas kernels, gather(): pl.pallas_call(functools.partial(gather_kernel, per_source=dest.shape[0]...  2.35 us
    pallas_call x1, Pallas kernels, moved_attention(): pl.pallas_call(functools.partial(moved_kernel, scale=scale), in_specs=[sm...  2.34 us
    pallas_call x1, Pallas kernels, join_new(): pl.pallas_call(functools.partial(new_kernel, per_head=per_head, steps=ste...  1.7 us
    ppermute x1, starting transfers between devices, per_device(): pieces.append(lax.ppermute(partial[k - 1], 'tp', pairs))  1.55 us
  transfers between devices with their start and end apart: 3, of which 1 were waited for; matrix products, arithmetic and copies ran while one was open for 0% of the time, Pallas kernels for 48%

profile of v3, /device:TPU:0, one launch (start us, length us, event | category | flops | bytes accessed | tf_op | source)
XLA Modules:
  0.0 46.8 jit_solution(6904685464276829064)
XLA Ops:
  0.6 2.3 %gather_queries.1 = bf16[32,40,128]{2,1,0:T(8,128)(2,1)} custom-call(s32[256]{0:T(256)} %bitcast.14, s32[256]{0:T(256)} %seq_hbm.3, bf16[64,40,128]{2,1,0:T(8,128)(2,1)} %bitcast.18), custom_call_target="tpu_custom_call" | custom-call | bytes 1310720 | tf_op jit(solution)/shard_map/gather_queries/pallas_call | solution.py:113
  3.0 7.4 %all-to-all-start = ((bf16[32,40,128]{2,1,0:T(8,128)(2,1)}), bf16[32,40,128]{2,1,0:T(8,128)(2,1)S(1)}, u32[]{:S(2)}, u32[]{:S(2)}) async-start(bf16[32,40,128]{2,1,0:T(8,128)(2,1)} %gather_queries.1), calls=%async_computation | async-start | bytes 655360 | tf_op jit(solution)/shard_map/all_to_all | solution.py:756
  10.4 0.0 copy-start
  10.4 12.1 %early_heads_and_new_kv.1 = (f32[2,640,128]{2,1,0:T(8,128)}, f32[2,640,128]{2,1,0:T(8,128)}, f32[128,1024]{1,0:T(8,128)}, s32[33]{0:T(128)}, s32[32]{0:T(128)}, ...) custom-call(s32[32,64]{1,0:T(8,128)} %bitcast.22, ...), custom_call_target="tpu_custom_call" | custom-call | flops 6039797760 | bytes 14155776 | tf_op jit(solution)/shard_map/early_heads_and_new_kv/pallas_call | solution.py:415
  22.5 0.0 all-to-all-done.q_ref
  22.5 0.0 copy-done
  22.5 2.3 %moved_attention.1 = bf16[32,48,128]{2,1,0:T(8,128)(2,1)} custom-call(s32[256]{0:T(256)S(1)} %bitcast.16, bf16[32,40,128]{2,1,0:T(8,128)(2,1)S(1)} %all-to-all-done.q_ref, bf16[16,4,64,128]{3,2,1,0:T(8,128)(2,1)S(1)} %get-tuple-element.25.keys, bf16[16,4,64,128]{3,2,1,0:T(8,128)(2,1)S(1)} %get-tuple-element.26.values), custom_call_target="tpu_custom_call" | custom-call | flops 83886080 | bytes 655360 | tf_op jit(solution)/shard_map/moved_attention/pallas_call | solution.py:678
  24.8 6.0 %all-to-all-start.1 = ((bf16[32,48,128]{2,1,0:T(8,128)(2,1)}), bf16[32,48,128]{2,1,0:T(8,128)(2,1)S(1)}, u32[]{:S(2)}, u32[]{:S(2)}) async-start(bf16[32,48,128]{2,1,0:T(8,128)(2,1)} %moved_attention.1), calls=%async_computation.1 | async-start | bytes 786432 | tf_op jit(solution)/shard_map/all_to_all | solution.py:756
  30.9 1.5 %collective-permute-start = (bf16[128,1024]{1,0:T(8,128)(2,1)S(1)}, bf16[128,1024]{1,0:T(8,128)(2,1)S(1)}, u32[]{:S(2)}, u32[]{:S(2)}) collective-permute-start(bf16[128,1024]{1,0:T(8,128)(2,1)S(1)} %bitcast.17), channel_id=1, source_target_pairs={{0,1},{1,0},{2,3},{3,2},{4,5},{5,4},{6,7},{7,6},{8,9},{9,8},{10,11... | collective-permute-start | bytes 786440 | tf_op jit(solution)/shard_map/ppermute | solution.py:772
  32.4 8.5 %late_heads.1 = (f32[64,40,128]{2,1,0:T(8,128)S(1)}, f32[64,40,128]{2,1,0:T(8,128)S(1)}, f32[2560,128]{1,0:T(8,128)S(1)}, f32[128,1024]{1,0:T(8,128)S(1)}) custom-call(s32[32,64]{1,0:T(8,128)} %bitcast.23, s32[1,64]{1,0:T(1,128)} %bitcast.25, bf16[2560,128]{1,0:T(8,128)(2,1)} %bitcast.20, bf16[56,4,64,128]{3,2,1,0:T(8,128)(2,1)} %k_hbm.3, ...), custom_call_target="tpu_custom_call" | custom-call | flops 4697620480 | bytes 3670016 | tf_op jit(solution)/shard_map/late_heads/pallas_call | solution.py:516
  40.9 0.0 collective-permute-done
  41.0 0.0 copy-start.1
  41.0 0.0 copy-start.2
  41.0 1.7 %join_new.1 = (bf16[128,1024]{1,0:T(8,128)(2,1)}, f32[64,40,128]{2,1,0:T(8,128)S(1)}, f32[64,40,128]{2,1,0:T(8,128)S(1)}) custom-call(f32[128,1024]{1,0:T(8,128)S(1)} %get-tuple-element.31.own_ref, bf16[1,128,1024]{2,1,0:T(8,128)(2,1)S(1)} %bitcast.13, f32[2560,128]{1,0:T(8,128)S(1)} %get-tuple-element.33.query, ...), custom_call_target="tpu_custom_call" | custom-call | flops 6553600 | bytes 6553600 | tf_op jit(solution)/shard_map/join_new/pallas_call | solution.py:599
  42.7 0.4 all-to-all-done.1.slot_ref
  43.1 0.0 copy-done.1
  43.1 0.0 copy-done.2
  43.1 3.7 %join_moved.1 = bf16[64,40,128]{2,1,0:T(8,128)(2,1)} custom-call(s32[33]{0:T(128)S(1)} %copy-done.1, s32[32]{0:T(128)S(1)} %copy-done.2, f32[64,40,128]{2,1,0:T(8,128)S(1)} %get-tuple-element.36.state_ref, f32[64,40,128]{2,1,0:T(8,128)S(1)} %get-tuple-element.37.lse_ref, bf16[32,48,128]{2,1,0:T(8,128)(2,1)S(1)} %all-to-all-done.1.slot_ref), custom_call_target="tpu_custom_call" | custom-call | flops 3276800 | bytes 3276800 | tf_op jit(solution)/shard_map/join_moved/pallas_call | solution.py:732
Async XLA Ops:
  3.0 19.5 %all-to-all-start = ((bf16[32,40,128]{2,1,0:T(8,128)(2,1)}), bf16[32,40,128]{2,1,0:T(8,128)(2,1)S(1)}, u32[]{:S(2)}, u32[]{:S(2)}) async-start(bf16[32,40,128]{2,1,0:T(8,128)(2,1)} %gather_queries.1), calls=%async_computation | async-start | bytes 655360 | tf_op jit(solution)/shard_map/all_to_all | solution.py:756
  10.4 12.1 %copy-start = (s32[256,1]{0,1:T(1,128)S(1)}, s32[256,1]{0,1:T(1,128)}, u32[]{:S(2)}) copy-start(s32[256,1]{0,1:T(1,128)} %param.17) | copy-start | bytes 3076
  24.8 18.2 %all-to-all-start.1 = ((bf16[32,48,128]{2,1,0:T(8,128)(2,1)}), bf16[32,48,128]{2,1,0:T(8,128)(2,1)S(1)}, u32[]{:S(2)}, u32[]{:S(2)}) async-start(bf16[32,48,128]{2,1,0:T(8,128)(2,1)} %moved_attention.1), calls=%async_computation.1 | async-start | bytes 786432 | tf_op jit(solution)/shard_map/all_to_all | solution.py:756
  30.9 10.1 %collective-permute-start = (bf16[128,1024]{1,0:T(8,128)(2,1)S(1)}, bf16[128,1024]{1,0:T(8,128)(2,1)S(1)}, u32[]{:S(2)}, u32[]{:S(2)}) collective-permute-start(bf16[128,1024]{1,0:T(8,128)(2,1)S(1)} %bitcast.17), channel_id=1, source_target_pairs={{0,1},{1,0},{2,3},{3,2},{4,5},{5,4},{6,7},{7,6},{8,9},{9,8},{10,11... | collective-permute-start | bytes 786440 | tf_op jit(solution)/shard_map/ppermute | solution.py:772
  41.0 2.1 %copy-start.1 = (s32[33]{0:T(128)S(1)}, s32[33]{0:T(128)}, u32[]{:S(2)}) copy-start(s32[33]{0:T(128)} %get-tuple-element.22.owner_ref) | copy-start | bytes 400
  41.0 2.1 %copy-start.2 = (s32[32]{0:T(128)S(1)}, s32[32]{0:T(128)}, u32[]{:S(2)}) copy-start(s32[32]{0:T(128)} %get-tuple-element.23.first_ref) | copy-start | bytes 388

commit v4 on v3

v4 whole, which is shorter than its diff:
```python
import functools
import math

import jax
import jax.numpy as jnp
from jax import lax
from jax.experimental import pallas as pl
from jax.experimental.pallas import tpu as pltpu
from jax.sharding import PartitionSpec as P

CAP = 2
NEGATIVE = -1e30
LOG2E = 1.4426950408889634
LANES = 128
MIB = 1024 * 1024


def vmem():
    return pl.BlockSpec(memory_space=pltpu.VMEM)


def hbm():
    return pl.BlockSpec(memory_space=pltpu.HBM)


def stay(array):
    return pltpu.with_memory_space_constraint(array, pltpu.HBM)


def limit(mib):
    return pltpu.CompilerParams(vmem_limit_bytes=mib * MIB)


def padded(rows):
    return (rows + 7) // 8 * 8


def answer_rows(rows):
    return (rows + 3 + 15) // 16 * 16


def fill_owner(dest, seq, me, owner, per_source):
    groups = dest.shape[0] // per_source
    slots = groups * CAP

    short = dest.shape[0] <= 256

    def clear(n, _):
        owner[n] = -1
        return 0

    def one_source(source, _):
        count = jnp.int32(0)
        for k in range(per_source):
            row = source * per_source + k
            hit = dest[row] == me
            owner[jnp.where(hit, source * CAP + count, slots)] = seq[row]
            count = count + hit.astype(jnp.int32)
        return 0

    repeat(slots, clear, short)
    repeat(groups, one_source, short)


def repeat(count, step, unrolled):
    if unrolled:
        for n in range(count):
            step(n, 0)
    else:
        lax.fori_loop(0, count, step, 0)


def first_slots(owner, first, seen):
    def unseen(n, _):
        seen[n] = -1
        return 0

    short = first.shape[0] <= 32
    repeat(seen.shape[0], unseen, short)

    def first_slot(n, _):
        sequence = owner[n]
        place = jnp.maximum(sequence, 0)
        earlier = seen[place]
        mine = jnp.where(earlier < 0, n, earlier)
        seen[place] = jnp.where(sequence < 0, earlier, mine)
        first[n] = jnp.where(sequence < 0, -1, mine)
        return 0

    repeat(first.shape[0], first_slot, short)


def gather_kernel(
    dest_hbm, seq_hbm, q_hbm, out_ref, dest, seq, owner, queries, sems, *, per_source
):
    me = lax.axis_index("gen")
    copies = [
        pltpu.make_async_copy(dest_hbm, dest, sems.at[0]),
        pltpu.make_async_copy(seq_hbm, seq, sems.at[1]),
        pltpu.make_async_copy(q_hbm, queries, sems.at[2]),
    ]
    for copy in copies:
        copy.start()
    copies[0].wait()
    copies[1].wait()
    fill_owner(dest, seq, me, owner, per_source)
    copies[2].wait()

    def one_slot(n, _):
        out_ref[n] = queries[jnp.maximum(owner[n], 0)]
        return 0

    lax.fori_loop(0, out_ref.shape[0], one_slot, 0, unroll=8)


def gather(dest, seq, queries, groups):
    slots = groups * CAP
    _, rows, head_dim = queries.shape
    return pl.pallas_call(
        functools.partial(gather_kernel, per_source=dest.shape[0] // groups),
        in_specs=[hbm()] * 3,
        out_specs=vmem(),
        out_shape=jax.ShapeDtypeStruct((slots, rows, head_dim), jnp.bfloat16),
        scratch_shapes=[
            pltpu.SMEM(dest.shape, jnp.int32),
            pltpu.SMEM(seq.shape, jnp.int32),
            pltpu.SMEM((slots + 1,), jnp.int32),
            pltpu.VMEM(queries.shape, jnp.bfloat16),
            pltpu.SemaphoreType.DMA((3,)),
        ],
        compiler_params=limit(4),
        cost_estimate=pl.CostEstimate(flops=0, bytes_accessed=4 * queries.size, transcendentals=0),
        name="gather_queries",
    )(stay(dest), stay(seq), stay(queries))


def make_bias(table_ref, length_ref, bias, page):
    blocks, seqs, width = bias.shape
    pool = padded(blocks * width // page)
    lengths = length_ref[...].astype(jnp.float32)
    page_id = lax.broadcasted_iota(jnp.int32, (pool, seqs), 0)
    used = jnp.zeros((pool, seqs), jnp.float32)
    for j in range(table_ref.shape[0]):
        inside = jnp.clip(lengths - float(page * j), 0.0, float(page))
        used = used + jnp.where(table_ref[j : j + 1, :] == page_id, inside, 0.0)
    used = used.T.astype(jnp.bfloat16)

    def one_block(b, _):
        key = lax.broadcasted_iota(jnp.int32, (pool, width), 1) + b * width
        owner = lax.broadcasted_iota(jnp.int32, (pool, width), 0)
        expand = jnp.where(key // page == owner, 1.0, 0.0).astype(jnp.bfloat16)
        count = jnp.dot(used, expand, preferred_element_type=jnp.float32)
        position = lax.broadcasted_iota(jnp.int32, (seqs, width), 1) % page
        bias[b] = jnp.where(position.astype(jnp.float32) < count, 0.0, NEGATIVE)
        return 0

    lax.fori_loop(0, blocks, one_block, 0)


class Attend:
    def __init__(self, packed, bias, keys, values, scores, tops, totals, scale, per_head):
        self.packed, self.bias, self.keys, self.values = packed, bias, keys, values
        self.scores, self.tops, self.totals = scores, tops, totals
        self.scale, self.per_head = scale, per_head
        self.blocks, self.seqs, self.width = bias.shape
        self.head_dim = packed.shape[2]
        self.rows = per_head * self.seqs
        self.pages = self.width // keys.shape[2]

    def start_scores(self, h):
        self.tops[h] = jnp.full((self.rows, LANES), NEGATIVE, jnp.float32)

    def score_block(self, h, b):
        keys = self.keys[h, pl.ds(b * self.pages, self.pages)].reshape(self.width, self.head_dim)
        s = lax.dot_general(
            self.packed[self.first + h], keys, (((1,), (1,)), ((), ())),
            preferred_element_type=jnp.float32,
        )
        s = s.reshape(self.per_head, self.seqs, self.width) + self.bias[b][None]
        s = s.reshape(self.rows, self.width)
        self.scores[h % 2][b] = s
        largest = s[:, :LANES]
        for t in range(1, self.width // LANES):
            largest = jnp.maximum(largest, s[:, t * LANES : (t + 1) * LANES])
        self.tops[h] = jnp.maximum(self.tops[h], largest)

    def start_values(self, h):
        top = jnp.max(self.tops[h], axis=1, keepdims=True)
        self.tops[h] = jnp.broadcast_to(top, (self.rows, LANES))
        self.totals[h] = jnp.zeros((self.rows, 2 * self.head_dim), jnp.float32)

    def weigh(self, weights, values):
        return jnp.dot(
            weights,
            jnp.concatenate([values, jnp.ones(values.shape, jnp.bfloat16)], axis=1),
            preferred_element_type=jnp.float32,
        )

    def value_block(self, h, b):
        scores, biggest = self.scores[h % 2], self.tops[h]
        values = self.values[h, pl.ds(b * self.pages, self.pages)]
        weights = []
        for t in range(self.width // LANES):
            s = scores[b, :, t * LANES : (t + 1) * LANES]
            weights.append(jnp.exp2((s - biggest) * self.scale).astype(jnp.bfloat16))
        self.totals[h] += self.weigh(
            jnp.concatenate(weights, axis=1), values.reshape(self.width, self.head_dim)
        )

    def run(self, first, count, keys_ready, values_ready, done):
        self.first = first
        for h in range(count + 1):
            if h < count:
                self.start_scores(h)
                keys_ready(h, 0)
            if h > 0:
                values_ready(h - 1)
                self.start_values(h - 1)

            def one_block(b, _, h=h):
                if h < count:
                    self.score_block(h, b)
                if h > 0:
                    self.value_block(h - 1, b)
                return 0

            if h == 0:
                self.score_block(0, 0)
                keys_ready(0, 1)
                self.score_block(0, 1)
            else:
                if h < count:
                    keys_ready(h, 1)
                lax.fori_loop(0, self.blocks, one_block, 0)
            if h > 0:
                done(h - 1)


def attend_scratch(seqs, per_head, pool, page, head_dim, pairs):
    keys = pool * page
    width = keys // 2
    rows = per_head * seqs
    scores = [pltpu.VMEM((keys // width, rows, width), jnp.float32) for _ in range(pairs)]
    return scores


def start_all(copies):
    for copy in copies:
        copy.start()


def wait_all(copies):
    for copy in copies:
        copy.wait()


def key_part(hbm_ref, head, target, sems, part):
    half = target.shape[0] // 2
    pages = pl.ds(part * half, half)
    return pltpu.make_async_copy(hbm_ref.at[pages, head], target.at[pages], sems.at[part])


def early_kernel(
    table_hbm, length_hbm, q_hbm, pages_hbm, dest_hbm, seq_hbm, x_hbm, k_hbm, v_hbm, w_hbm, *refs,
    tp, scale, count, per_head,
):
    outs = 2 if count else 0
    local_hbm = refs[:outs]
    owner_hbm, first_hbm, packed_hbm, send_ref, move_keys, move_values = refs[outs : outs + 6]
    (table, lengths, pages, raw, query, packed, bias, x, dest, seq, owner, first, seen, w, keys, values,
     small_sems, key_sems, value_sems, move_sems, w_sems, out_sems, *attend_refs) = refs[outs + 6 :]
    pairs = min(count, 2)
    blocks, _, width = w.shape
    moves = move_keys.shape[0]
    per_owner = blocks // (tp - 1)
    columns = per_owner * width
    me, place = lax.axis_index("gen"), lax.axis_index("tp")
    small = [
        pltpu.make_async_copy(source, target, small_sems.at[k])
        for k, (source, target) in enumerate(
            [(table_hbm, table), (length_hbm, lengths), (q_hbm, raw), (pages_hbm, pages),
             (dest_hbm, dest), (seq_hbm, seq), (x_hbm, x)]
        )
    ]
    owner_copy = pltpu.make_async_copy(owner, owner_hbm, out_sems.at[4, 0])
    first_copy = pltpu.make_async_copy(first, first_hbm, out_sems.at[0, 0])
    packed_copy = pltpu.make_async_copy(packed, packed_hbm, out_sems.at[3, 0])
    seqs = bias.shape[1]
    stride = query.shape[0] // seqs

    def pack(head):
        for r in range(per_head):
            rows = query[pl.ds(head * per_head + r, seqs, stride=stride), :]
            packed[head, pl.ds(r * seqs, seqs), :] = rows.astype(jnp.bfloat16)

    def key_copy(h, part):
        return key_part(k_hbm, h, keys.at[h], key_sems.at[h], part)

    def value_copy(h):
        return pltpu.make_async_copy(v_hbm.at[:, h], values.at[h], value_sems.at[h])

    def w_copy(b):
        target = lax.rem(place + 1 + b // per_owner, tp)
        start = pl.multiple_of(target * columns + b % per_owner * width, width)
        return pltpu.make_async_copy(w_hbm.at[:, pl.ds(start, width)], w.at[b], w_sems.at[b])

    def move_copies(k):
        page = pages[me * moves + k]
        return (
            pltpu.make_async_copy(k_hbm.at[page], move_keys.at[k], move_sems.at[0, k]),
            pltpu.make_async_copy(v_hbm.at[page], move_values.at[k], move_sems.at[1, k]),
        )

    def start_move(k, _):
        start_all(move_copies(k))
        return 0

    def wait_move(k, _):
        wait_all(move_copies(k))
        return 0

    def start_weights(start, stop):
        for b in range(start, stop):
            w_copy(b).start()

    start_all(small[:3])
    if count:
        key_copy(0, 0).start()
        key_copy(0, 1).start()
    start_all(small[3:6])
    wait_all(small[:2])
    if count:
        make_bias(table, lengths, bias, keys.shape[2])
    small[2].wait()
    query[...] = raw[...].astype(jnp.float32)
    for head in range(count):
        pack(head)
    if count:
        totals, tops = attend_refs[pairs:]
        attend = Attend(
            packed, bias, keys, values, attend_refs[:pairs], tops, totals, scale, per_head
        )

        def local_copies(h):
            return [
                pltpu.make_async_copy(totals.at[h], local_hbm[0].at[h], out_sems.at[1, h]),
                pltpu.make_async_copy(tops.at[h], local_hbm[1].at[h], out_sems.at[2, h]),
            ]

        def keys_ready(h, b):
            key_copy(h, b).wait()
            if b == 0:
                value_copy(h).start()
                if h + 1 < count:
                    key_copy(h + 1, 0).start()
                    key_copy(h + 1, 1).start()
                if h == count - 1:
                    small[6].start()
                    start_weights(0, (blocks + 1) // 2)

        def values_ready(h):
            value_copy(h).wait()
            if h == count - 1:
                start_weights((blocks + 1) // 2, blocks)
                small[3].wait()
                lax.fori_loop(0, moves, start_move, 0)

        attend.run(0, count, keys_ready, values_ready, lambda h: start_all(local_copies(h)))
    else:
        small[6].start()
        start_weights(0, blocks)
        small[3].wait()
        lax.fori_loop(0, moves, start_move, 0)
    for head in range(count, packed.shape[0]):
        pack(head)
    packed_copy.start()
    wait_all(small[4:])
    for b in range(blocks):
        w_copy(b).wait()
        product = jnp.dot(x[...], w[b], preferred_element_type=jnp.float32)
        part = slice(b % per_owner * width, (b % per_owner + 1) * width)
        send_ref[b // per_owner, :, part] = product.astype(jnp.bfloat16)
        if b == 0:
            fill_owner(dest, seq, me, owner, moves)
            first_slots(owner, first, seen)
            owner_copy.start()
            first_copy.start()
    lax.fori_loop(0, moves, wait_move, 0)
    owner_copy.wait()
    first_copy.wait()
    packed_copy.wait()
    for h in range(count):
        wait_all(local_copies(h))


def early_work(
    table, lengths, pages, queries, tokens, dest, seq, k_cache, v_cache, w_kv, groups, tp, count, scale
):
    seqs, stride, head_dim = queries.shape
    pool, kv_heads, page, _ = k_cache.shape
    per_head = stride // kv_heads
    rows, depth = tokens.shape
    moves, slots = pages.shape[0] // groups, groups * CAP
    columns = w_kv.shape[1] // tp
    width = min(512, columns)
    blocks = (tp - 1) * columns // width
    keys = pool * page
    held = max(count, 1)
    f32, bf16 = jnp.float32, jnp.bfloat16
    total_shape = (count, per_head * seqs, 2 * head_dim)
    top_shape = (count, per_head * seqs, LANES)
    local = [pltpu.HBM(total_shape, f32), pltpu.HBM(top_shape, f32)] if count else []
    scratch = [
        pltpu.VMEM(table.shape, jnp.int32),
        pltpu.VMEM(lengths.shape, jnp.int32),
        pltpu.SMEM(pages.shape, jnp.int32),
        pltpu.VMEM((seqs * stride, head_dim), bf16),
        pltpu.VMEM((seqs * stride, head_dim), f32),
        pltpu.VMEM((kv_heads, per_head * seqs, head_dim), bf16),
        pltpu.VMEM((2, seqs, keys // 2), f32),
        pltpu.VMEM((rows, depth), bf16),
        pltpu.SMEM(dest.shape, jnp.int32),
        pltpu.SMEM(seq.shape, jnp.int32),
        pltpu.SMEM((slots + 1,), jnp.int32),
        pltpu.SMEM((slots,), jnp.int32),
        pltpu.SMEM((seqs,), jnp.int32),
        pltpu.VMEM((blocks, depth, width), bf16),
        pltpu.VMEM((held, pool, page, head_dim), bf16),
        pltpu.VMEM((held, pool, page, head_dim), bf16),
        pltpu.SemaphoreType.DMA((7,)),
        pltpu.SemaphoreType.DMA((held, 2)),
        pltpu.SemaphoreType.DMA((held,)),
        pltpu.SemaphoreType.DMA((2, moves)),
        pltpu.SemaphoreType.DMA((blocks,)),
        pltpu.SemaphoreType.DMA((5, held)),
    ]
    if count:
        scratch += attend_scratch(seqs, per_head, pool, page, head_dim, min(count, 2))
        scratch += [pltpu.VMEM(total_shape, f32), pltpu.VMEM(top_shape, f32)]
    return pl.pallas_call(
        functools.partial(early_kernel, tp=tp, scale=scale, count=count, per_head=per_head),
        in_specs=[hbm()] * 10,
        out_specs=[hbm()] * (len(local) + 3) + [vmem()] * 3,
        out_shape=local + [
            pltpu.HBM((slots + 1,), jnp.int32),
            pltpu.HBM((slots,), jnp.int32),
            pltpu.HBM((kv_heads, per_head * seqs, head_dim), bf16),
            jax.ShapeDtypeStruct((tp - 1, rows, columns), bf16),
            jax.ShapeDtypeStruct((moves,) + k_cache.shape[1:], bf16),
            jax.ShapeDtypeStruct((moves,) + k_cache.shape[1:], bf16),
        ],
        scratch_shapes=scratch,
        compiler_params=limit(40),
        cost_estimate=pl.CostEstimate(
            flops=tokens.size * w_kv.shape[1] + 8 * count * per_head * seqs * keys * head_dim,
            bytes_accessed=w_kv.size + 4 * count * keys * head_dim,
            transcendentals=count * per_head * seqs * keys,
        ),
        name="early_heads_and_sent_kv",
    )(
        stay(table), stay(lengths), stay(queries.reshape(seqs * stride, head_dim)), stay(pages),
        stay(dest), stay(seq), stay(tokens), stay(k_cache), stay(v_cache), stay(w_kv),
    )


def late_kernel(
    table_hbm, length_hbm, q_hbm, k_hbm, v_hbm, x_hbm, w_hbm, *refs, scale, early, count, per_head
):
    ins = 2 if early else 0
    before_hbm = refs[:ins]
    totals, tops, packed, x, w = refs[ins : ins + 5]
    before = refs[ins + 5 : 2 * ins + 5]
    table, lengths, bias, keys, values, sems, key_sems, value_sems, *scores = refs[2 * ins + 5 :]
    columns = w.shape[1]
    start = pl.multiple_of(lax.axis_index("tp") * columns, columns)
    pairs_in = [
        (table_hbm, table), (length_hbm, lengths), (q_hbm, packed), (x_hbm, x),
        (w_hbm.at[:, pl.ds(start, columns)], w),
    ] + list(zip(before_hbm, before))
    small = [
        pltpu.make_async_copy(source, target, sems.at[k])
        for k, (source, target) in enumerate(pairs_in)
    ]

    def key_copy(h, part):
        return key_part(k_hbm, early + h, keys.at[h], key_sems.at[h], part)

    def value_copy(h):
        return pltpu.make_async_copy(v_hbm.at[:, early + h], values.at[h], value_sems.at[h])

    start_all(small[:3])
    key_copy(0, 0).start()
    key_copy(0, 1).start()
    wait_all(small[:2])
    make_bias(table, lengths, bias, keys.shape[2])
    small[2].wait()
    attend = Attend(packed, bias, keys, values, scores, tops, totals, scale, per_head)

    def keys_ready(h, b):
        key_copy(h, b).wait()
        if b == 0:
            value_copy(h).start()
            if h + 1 < count:
                key_copy(h + 1, 0).start()
                key_copy(h + 1, 1).start()
            if h == count - 1:
                start_all(small[3:])

    attend.run(early, count, keys_ready, lambda h: value_copy(h).wait(), lambda h: None)
    wait_all(small[3:])


def late_work(table, lengths, packed, k_cache, v_cache, tokens, w_kv, before, tp, early, scale):
    pool, kv_heads, page, head_dim = k_cache.shape
    _, rows, _ = packed.shape
    seqs = lengths.shape[1]
    per_head = rows // seqs
    count = kv_heads - early
    keys = pool * page
    f32, bf16 = jnp.float32, jnp.bfloat16
    return pl.pallas_call(
        functools.partial(late_kernel, scale=scale, early=early, count=count, per_head=per_head),
        in_specs=[hbm()] * (7 + len(before)),
        out_specs=[vmem()] * (5 + len(before)),
        out_shape=[
            jax.ShapeDtypeStruct((count, rows, 2 * head_dim), f32),
            jax.ShapeDtypeStruct((count, rows, LANES), f32),
            jax.ShapeDtypeStruct(packed.shape, bf16),
            jax.ShapeDtypeStruct(tokens.shape, bf16),
            jax.ShapeDtypeStruct((w_kv.shape[0], w_kv.shape[1] // tp), bf16),
        ] + [jax.ShapeDtypeStruct(array.shape, f32) for array in before],
        scratch_shapes=[
            pltpu.VMEM(table.shape, jnp.int32),
            pltpu.VMEM(lengths.shape, jnp.int32),
            pltpu.VMEM((2, seqs, keys // 2), f32),
            pltpu.VMEM((count, pool, page, head_dim), bf16),
            pltpu.VMEM((count, pool, page, head_dim), bf16),
            pltpu.SemaphoreType.DMA((7,)),
            pltpu.SemaphoreType.DMA((count, 2)),
            pltpu.SemaphoreType.DMA((count,)),
        ] + attend_scratch(seqs, per_head, pool, page, head_dim, min(count, 2)),
        compiler_params=limit(36),
        cost_estimate=pl.CostEstimate(
            flops=8 * count * rows * keys * head_dim,
            bytes_accessed=4 * count * keys * head_dim,
            transcendentals=count * rows * keys,
        ),
        name="late_heads",
    )(
        stay(table), stay(lengths), stay(packed), stay(k_cache), stay(v_cache), stay(tokens), stay(w_kv),
        *[stay(array) for array in before],
    )


def new_kernel(
    other_ref, packed, x, w, *refs, parts, per_head, steps, scale
):
    local = refs[: 2 * parts]
    new_hbm, state, state_lse, new, fresh, sem = refs[2 * parts :]
    seqs, stride, head_dim = state.shape
    flat = (seqs * stride, head_dim)
    rows, rows_lse = state.reshape(flat), state_lse.reshape(flat)
    width = 2 * head_dim
    head = 0
    for part in range(parts):
        totals, tops = local[2 * part], local[2 * part + 1]
        for h in range(totals.shape[0]):
            columns = slice(head * width, (head + 1) * width)
            if head % 2 == 0:
                both = jnp.dot(
                    x[...], w[:, head * width : (head + 2) * width], preferred_element_type=jnp.float32
                )
            partial = both[:, head % 2 * width : (head % 2 + 1) * width]
            for k in range(other_ref.shape[0]):
                partial = partial + other_ref[k, :, columns].astype(jnp.float32)
            rounded = partial.astype(jnp.bfloat16)
            new[:, columns] = rounded
            fresh[head, 0] = rounded[:, :head_dim].astype(jnp.float32)
            fresh[head, 1] = rounded[:, head_dim:].astype(jnp.float32)
            new_keys, new_values = [], []
            for j in range(steps):
                every = pl.ds(j, seqs, stride=steps)
                new_keys.append(fresh[head, 0, every, :])
                new_values.append(fresh[head, 1, every, :])
            for r in range(per_head):
                place = pl.ds(head * per_head + r, seqs, stride=stride)
                block = pl.ds(r * seqs, seqs)
                q = packed[head, block, :].astype(jnp.float32)
                scores = [
                    jnp.sum(q * new_keys[j], axis=1, keepdims=True) * scale
                    for j in range(r % steps + 1)
                ]
                biggest = tops[h, block, :] * scale
                top = biggest
                for s in scores:
                    top = jnp.maximum(top, s)
                factor = jnp.exp2(biggest - top)
                weight = factor * totals[h, block, head_dim:]
                summed = factor * totals[h, block, :head_dim]
                for j, s in enumerate(scores):
                    share = jnp.exp2(s - top)
                    weight = weight + share
                    summed = summed + share * new_values[j]
                rows[place, :] = summed / weight
                rows_lse[place, :] = top + jnp.log2(weight)
            head += 1
    copy = pltpu.make_async_copy(new, new_hbm, sem.at[0])
    copy.start()
    copy.wait()


def join_new(other, packed, x, w, local, seqs, per_head, steps, scale):
    kv_heads, rows, head_dim = packed.shape
    columns = w.shape[1]
    state = jax.ShapeDtypeStruct((seqs, padded(kv_heads * per_head), head_dim), jnp.float32)
    return pl.pallas_call(
        functools.partial(
            new_kernel, parts=len(local) // 2, per_head=per_head, steps=steps, scale=scale
        ),
        in_specs=[vmem()] * (4 + len(local)),
        out_specs=[hbm(), vmem(), vmem()],
        out_shape=[jax.ShapeDtypeStruct((x.shape[0], columns), jnp.bfloat16), state, state],
        scratch_shapes=[
            pltpu.VMEM((x.shape[0], columns), jnp.bfloat16),
            pltpu.VMEM((columns // (2 * head_dim), 2, x.shape[0], head_dim), jnp.float32),
            pltpu.SemaphoreType.DMA((1,)),
        ],
        compiler_params=limit(8),
        cost_estimate=pl.CostEstimate(
            flops=20 * packed.size + 2 * x.shape[0] * w.size,
            bytes_accessed=20 * packed.size,
            transcendentals=4 * packed.size,
        ),
        name="join_new",
    )(other, packed, x, w, *local)


def moved_kernel(dest_hbm, q_ref, keys, values, out_ref, dest_ref, slot, sem, *, scale):
    moves, kv_heads, page, head_dim = keys.shape
    rows = q_ref.shape[1]
    padding = out_ref.shape[1] - rows
    columns = kv_heads * page
    me = lax.axis_index("gen")
    dest_copy = pltpu.make_async_copy(dest_hbm, dest_ref, sem.at[0])
    dest_copy.start()
    out_ref[...] = jnp.zeros(out_ref.shape, jnp.bfloat16)
    row = lax.broadcasted_iota(jnp.int32, (rows, columns), 0)
    column = lax.broadcasted_iota(jnp.int32, (rows, columns), 1)
    other_head = jnp.where(row // (rows // kv_heads) == column // page, 0.0, NEGATIVE)
    tall = lax.broadcasted_iota(jnp.int32, (rows, LANES), 0)
    lane = lax.broadcasted_iota(jnp.int32, (rows, LANES), 1)
    spare = lax.broadcasted_iota(jnp.int32, (padding, LANES), 0)
    ones = jnp.ones((columns, head_dim), jnp.bfloat16)

    def one_move(k):
        s = lax.dot_general(
            q_ref[slot[k]],
            keys[k].reshape(columns, head_dim),
            (((1,), (1,)), ((), ())),
            preferred_element_type=jnp.float32,
        )
        s = s + other_head
        biggest = jnp.max(s, axis=1, keepdims=True)
        weights = jnp.exp2((s - biggest) * scale).astype(jnp.bfloat16)
        both = jnp.concatenate([values[k].reshape(columns, head_dim), ones], axis=1)
        summed = jnp.dot(weights, both, preferred_element_type=jnp.float32)
        weight_sum = summed[:, head_dim:]
        lse = biggest * scale + jnp.log2(weight_sum)
        lse = jnp.sum(jnp.where(tall == lane, lse, 0.0), axis=0, keepdims=True)
        high = lse.astype(jnp.bfloat16).astype(jnp.float32)
        middle = (lse - high).astype(jnp.bfloat16).astype(jnp.float32)
        low = lse - high - middle
        pieces = jnp.where(spare == 0, high, jnp.where(spare == 1, middle, low))
        result = jnp.concatenate([summed[:, :head_dim] / weight_sum, pieces], axis=0)
        return result.astype(jnp.bfloat16)

    dest_copy.wait()
    for k in range(moves):
        mine = dest_ref[me * moves + k]
        rank = jnp.int32(0)
        for j in range(k):
            rank = rank + (dest_ref[me * moves + j] == mine).astype(jnp.int32)
        slot[k] = mine * CAP + rank
    batch = min(16, moves)

    def some_moves(b, _):
        results = [one_move(b * batch + k) for k in range(batch)]
        for k in range(batch):
            out_ref[slot[b * batch + k]] = results[k]
        return 0

    lax.fori_loop(0, moves // batch, some_moves, 0)


def moved_attention(dest, received, move_keys, move_values, scale):
    moves, kv_heads, page, head_dim = move_keys.shape
    count, rows, _ = received.shape
    return pl.pallas_call(
        functools.partial(moved_kernel, scale=scale),
        in_specs=[hbm(), vmem(), vmem(), vmem()],
        out_specs=vmem(),
        out_shape=jax.ShapeDtypeStruct((count, answer_rows(rows), head_dim), jnp.bfloat16),
        scratch_shapes=[
            pltpu.SMEM(dest.shape, jnp.int32),
            pltpu.SMEM((moves,), jnp.int32),
            pltpu.SemaphoreType.DMA((1,)),
        ],
        compiler_params=limit(4),
        cost_estimate=pl.CostEstimate(
            flops=4 * moves * rows * kv_heads * page * head_dim,
            bytes_accessed=4 * received.size,
            transcendentals=moves * rows * kv_heads * page,
        ),
        name="moved_attention",
    )(stay(dest), received, move_keys, move_values)


def join_kernel(
    owner_hbm, first_hbm, state_ref, lse_ref, slot_ref, out_ref, owner_ref, first_ref, states,
    states_lse, come_lses, sems,
):
    seqs, rows, head_dim = out_ref.shape
    count = slot_ref.shape[0]
    copies = [
        pltpu.make_async_copy(owner_hbm, owner_ref, sems.at[0]),
        pltpu.make_async_copy(first_hbm, first_ref, sems.at[1]),
    ]
    start_all(copies)
    real = pl.ds(0, rows)
    tall = lax.broadcasted_iota(jnp.int32, (rows, LANES), 0)
    lane = lax.broadcasted_iota(jnp.int32, (rows, LANES), 1)
    out_ref[...] = state_ref[:, :rows, :].astype(jnp.bfloat16)

    def answer_lse(n, _):
        pieces = slot_ref[n, pl.ds(rows // 8 * 8, slot_ref.shape[1] - rows // 8 * 8)]
        pieces = pieces.astype(jnp.float32)[rows % 8 :]
        packed = pieces[0:1] + pieces[1:2] + pieces[2:3]
        lse = jnp.sum(jnp.where(tall == lane, packed, 0.0), axis=1, keepdims=True)
        come_lses[n] = jnp.broadcast_to(lse, (rows, LANES))
        return 0

    lax.fori_loop(0, count, answer_lse, 0, unroll=8)
    wait_all(copies)

    def join(n, old_sum, old_lse):
        come_lse = come_lses[n]
        top = jnp.maximum(old_lse, come_lse)
        old = jnp.exp2(old_lse - top)
        come = jnp.exp2(come_lse - top)
        weight = old + come
        come_sum = slot_ref[n].astype(jnp.float32)[:rows]
        return (old * old_sum + come * come_sum) / weight, top + jnp.log2(weight)

    def every_slot(n, _):
        seq = jnp.maximum(owner_ref[n], 0)
        states[n], states_lse[n] = join(n, state_ref[seq, real], lse_ref[seq, real])
        return 0

    def later_slot(n, _):
        first = first_ref[n]

        @pl.when((first >= 0) & (first < n))
        def _():
            states[first], states_lse[first] = join(n, states[first], states_lse[first])

        return 0

    def store_slot(n, _):
        @pl.when(first_ref[n] == n)
        def _():
            out_ref[owner_ref[n]] = states[n].astype(jnp.bfloat16)

        return 0

    lax.fori_loop(0, count, every_slot, 0, unroll=8)
    lax.fori_loop(0, count, later_slot, 0)
    lax.fori_loop(0, count, store_slot, 0)


def join_moved(owner, first, state, state_lse, answers, shape):
    slots = first.shape[0]
    block = pltpu.VMEM((slots,) + shape[1:], jnp.float32)
    return pl.pallas_call(
        join_kernel,
        in_specs=[hbm()] * 2 + [vmem()] * 3,
        out_specs=vmem(),
        out_shape=jax.ShapeDtypeStruct(shape, jnp.bfloat16),
        scratch_shapes=[
            pltpu.SMEM(owner.shape, jnp.int32),
            pltpu.SMEM(first.shape, jnp.int32),
            block, block, block,
            pltpu.SemaphoreType.DMA((2,)),
        ],
        compiler_params=limit(8),
        cost_estimate=pl.CostEstimate(
            flops=10 * state.size, bytes_accessed=10 * state.size, transcendentals=0
        ),
        name="join_moved",
    )(stay(owner), stay(first), state, state_lse, answers)


def per_device(
    tokens_in, w_kv, queries, k_cache, v_cache, page_table, lengths, move_dest, move_page, move_seq
):
    groups = lax.axis_size("gen")
    tp = lax.axis_size("tp")
    seqs, steps, heads, head_dim = queries.shape
    kv_heads = k_cache.shape[1]
    scale = LOG2E / math.sqrt(head_dim)

    def exchange(array):
        return lax.all_to_all(array, "gen", split_axis=0, concat_axis=0, tiled=True)

    rows = queries.transpose(0, 2, 1, 3).reshape(seqs, heads * steps, head_dim)
    dest = move_dest.reshape(-1)
    to_send = gather(dest, move_seq, rows, groups)
    early = kv_heads // 2
    early_rows, to_send = lax.optimization_barrier((rows, to_send))
    received = exchange(to_send)
    table, lengths = page_table.T, lengths.reshape(1, seqs)
    *before, owner, first, packed, partial, move_keys, move_values = early_work(
        table, lengths, move_page, early_rows, tokens_in, dest, move_seq, k_cache, v_cache, w_kv,
        groups, tp, early, scale,
    )
    pieces = []
    for k in range(1, tp):
        pairs = [(i, (i + k) % tp) for i in range(tp)]
        pieces.append(lax.ppermute(partial[k - 1], "tp", pairs))
    other = jnp.stack(pieces)
    answers = moved_attention(dest, received, move_keys, move_values, scale)
    packed, answers = lax.optimization_barrier((packed, answers))
    returned = exchange(answers)
    totals, tops, packed, x, w, *before = late_work(
        table, lengths, packed, k_cache, v_cache, tokens_in, w_kv, before, tp, early, scale
    )
    new_kv, state, state_lse = join_new(
        other, packed, x, w, before + [totals, tops], seqs, heads * steps // kv_heads, steps, scale
    )
    attended = join_moved(
        owner, first, state, state_lse, returned, (seqs, heads * steps, head_dim)
    )
    attended = attended.reshape(seqs, heads, steps, head_dim).transpose(0, 2, 1, 3)
    return (attended, new_kv)


def solution(mesh):
    return jax.shard_map(
        per_device,
        mesh=mesh,
        in_specs=(
            P("gen", "tp"),
            P("tp", None),
            P("gen", None, "tp", None),
            P("gen", "tp", None, None),
            P("gen", "tp", None, None),
            P("gen", None),
            P("gen"),
            P(),
            P(),
            P(),
        ),
        out_specs=(P("gen", None, "tp", None), P("gen", "tp")),
        check_vma=False,
    )
```

time: 47.2 us -> 44.8 us (0.949)
  Pallas kernels: 30.7 us -> 27.9 us
  waiting for transfers between devices: 0.39 us -> 1.46 us
  starting transfers between devices: 15 us -> 14.1 us
    pallas_call x1, Pallas kernels: 12.1 us -> 10.2 us  [early_work(): pl.pallas_call(functools.partial(early_kernel, tp=tp, scale=scale, count=...]
    all_to_all x2, waiting for transfers between devices: 0.38 us -> 1.46 us  [exchange(): return lax.all_to_all(array, 'gen', split_axis=0, concat_axis=0, tiled=True)]
    all_to_all x2, starting transfers between devices: 13.4 us -> 12.6 us  [exchange(): return lax.all_to_all(array, 'gen', split_axis=0, concat_axis=0, tiled=True)]
    pallas_call x1, Pallas kernels: 8.52 us -> 8.04 us  [late_work(): pl.pallas_call(functools.partial(late_kernel, scale=scale, early=early, c...]
  transfers between devices with their start and end apart: 3 -> 3, of which waited for: 1 -> 2; matrix products, arithmetic and copies ran while one was open for 0% -> 0% of each run, Pallas kernels for 48% -> 46%
where the time goes in v4:
time: 44.8 us; the launch traced here: 44.3 us
  Pallas kernels  27.9 us (62%)
  starting transfers between devices  14.1 us (31%)
  waiting for transfers between devices  1.46 us (3%)
  between operations  0.85 us (2%)
    all_to_all x2, starting transfers between devices, exchange(): return lax.all_to_all(array, 'gen', split_axis=0, concat_axis=0, tiled=True)  12.6 us
    pallas_call x1, Pallas kernels, early_work(): pl.pallas_call(functools.partial(early_kernel, tp=tp, scale=scale, count=...  10.2 us
    pallas_call x1, Pallas kernels, late_work(): pl.pallas_call(functools.partial(late_kernel, scale=scale, early=early, c...  8.04 us
    pallas_call x1, Pallas kernels, join_moved(): pl.pallas_call(join_kernel, in_specs=[hbm()] * 2 + [vmem()] * 3, out_spec...  2.93 us
    pallas_call x1, Pallas kernels, moved_attention(): pl.pallas_call(functools.partial(moved_kernel, scale=scale), in_specs=[hb...  2.46 us
    pallas_call x1, Pallas kernels, gather(): pl.pallas_call(functools.partial(gather_kernel, per_source=dest.shape[0]...  2.24 us
    pallas_call x1, Pallas kernels, join_new(): pl.pallas_call(functools.partial(new_kernel, parts=len(local) // 2, per_h...  1.94 us
    ppermute x1, starting transfers between devices, per_device(): pieces.append(lax.ppermute(partial[k - 1], 'tp', pairs))  1.56 us
  transfers between devices with their start and end apart: 3, of which 2 were waited for; matrix products, arithmetic and copies ran while one was open for 0% of the time, Pallas kernels for 46%

profile of v4, /device:TPU:0, one launch (start us, length us, event | category | flops | bytes accessed | tf_op | source)
XLA Modules:
  0.0 44.3 jit_solution(8529407612211473907)
XLA Ops:
  0.6 2.2 %gather_queries.1 = bf16[32,40,128]{2,1,0:T(8,128)(2,1)} custom-call(s32[256]{0:T(256)} %bitcast.19, s32[256]{0:T(256)} %seq_hbm.3, bf16[64,40,128]{2,1,0:T(8,128)(2,1)} %bitcast.14), custom_call_target="tpu_custom_call" | custom-call | bytes 1310720 | tf_op jit(solution)/shard_map/gather_queries/pallas_call | solution.py:119
  2.9 7.4 %all-to-all-start = ((bf16[32,40,128]{2,1,0:T(8,128)(2,1)}), bf16[32,40,128]{2,1,0:T(8,128)(2,1)S(1)}, u32[]{:S(2)}, u32[]{:S(2)}) async-start(bf16[32,40,128]{2,1,0:T(8,128)(2,1)} %gather_queries.1), calls=%async_computation | async-start | bytes 655360 | tf_op jit(solution)/shard_map/all_to_all | solution.py:812
  10.3 10.2 %early_heads_and_sent_kv.1 = (f32[2,640,256]{2,1,0:T(8,128)}, f32[2,640,128]{2,1,0:T(8,128)}, s32[33]{0:T(128)}, s32[32]{0:T(128)}, bf16[4,640,128]{2,1,0:T(8,12...) custom-call(s32[32,64]{1,0:T(8,128)} %bitcast.17, ...), custom_call_target="tpu_custom_call" | custom-call | flops 5368709120 | bytes 8912896 | tf_op jit(solution)/shard_map/early_heads_and_sent_kv/pallas_call | solution.py:440
  20.5 0.8 %all-to-all-done.q_ref = bf16[32,40,128]{2,1,0:T(8,128)(2,1)S(1)} async-done(((bf16[32,40,128]{2,1,0:T(8,128)(2,1)}), bf16[32,40,128]{2,1,0:T(8,128)(2,1)S(1)}, u32[]{:S(2)}, u32[]{:S(2)}) %all-to-all-start) | async-done | bytes 327712 | tf_op jit(solution)/shard_map/all_to_all | solution.py:812
  21.4 2.5 %moved_attention.1 = bf16[32,48,128]{2,1,0:T(8,128)(2,1)} custom-call(s32[256]{0:T(256)} %bitcast.21, bf16[32,40,128]{2,1,0:T(8,128)(2,1)S(1)} %all-to-all-done.q_ref, bf16[16,4,64,128]{3,2,1,0:T(8,128)(2,1)S(1)} %get-tuple-element.30.keys, bf16[16,4,64,128]{3,2,1,0:T(8,128)(2,1)S(1)} %get-tuple-element.31.values), custom_call_target="tpu_custom_call" | custom-call | flops 83886080 | bytes 655360 | tf_op jit(solution)/shard_map/moved_attention/pallas_call | solution.py:698
  23.8 5.2 %all-to-all-start.1 = ((bf16[32,48,128]{2,1,0:T(8,128)(2,1)}), bf16[32,48,128]{2,1,0:T(8,128)(2,1)S(1)}, u32[]{:S(2)}, u32[]{:S(2)}) async-start(bf16[32,48,128]{2,1,0:T(8,128)(2,1)} %moved_attention.1), calls=%async_computation.1 | async-start | bytes 786432 | tf_op jit(solution)/shard_map/all_to_all | solution.py:812
  29.0 1.6 %collective-permute-start = (bf16[128,1024]{1,0:T(8,128)(2,1)S(1)}, bf16[128,1024]{1,0:T(8,128)(2,1)S(1)}, u32[]{:S(2)}, u32[]{:S(2)}) collective-permute-start(bf16[128,1024]{1,0:T(8,128)(2,1)S(1)} %bitcast.13), channel_id=1, source_target_pairs={{0,1},{1,0},{2,3},{3,2},{4,5},{5,4},{6,7},{7,6},{8,9},{9,8},{10,11... | collective-permute-start | bytes 786440 | tf_op jit(solution)/shard_map/ppermute | solution.py:828
  30.6 8.0 %late_heads.1 = (f32[2,640,256]{2,1,0:T(8,128)S(1)}, f32[2,640,128]{2,1,0:T(8,128)S(1)}, bf16[4,640,128]{2,1,0:T(8,128)(2,1)S(1)}, bf16[128,2560]{1,0:T(8,128)(2...) custom-call(s32[32,64]{1,0:T(8,128)} %bitcast.18, ...), custom_call_target="tpu_custom_call" | custom-call | flops 4697620480 | bytes 3670016 | tf_op jit(solution)/shard_map/late_heads/pallas_call | solution.py:521
  38.7 0.0 collective-permute-done
  38.7 1.9 %join_new.1 = (bf16[128,1024]{1,0:T(8,128)(2,1)}, f32[64,40,128]{2,1,0:T(8,128)S(1)}, f32[64,40,128]{2,1,0:T(8,128)S(1)}) custom-call(bf16[1,128,1024]{2,1,0:T(8,128)(2,1)S(1)} %bitcast.12, bf16[4,640,128]{2,1,0:T(8,128)(2,1)S(1)} %get-tuple-element.35.packed, bf16[128,2560]{1,0:T(8,128)(2,1)S(1)} %get-tuple-element.36.x, ...), custom_call_target="tpu_custom_call" | custom-call | flops 677642240 | bytes 6553600 | tf_op jit(solution)/shard_map/join_new/pallas_call | solution.py:616
  40.6 0.6 %all-to-all-done.1.slot_ref = bf16[32,48,128]{2,1,0:T(8,128)(2,1)S(1)} async-done(((bf16[32,48,128]{2,1,0:T(8,128)(2,1)}), bf16[32,48,128]{2,1,0:T(8,128)(2,1)S(1)}, u32[]{:S(2)}, u32[]{:S(2)}) %all-to-all-start.1) | async-done | bytes 393248 | tf_op jit(solution)/shard_map/all_to_all | solution.py:812
  41.2 2.9 %join_moved.1 = bf16[64,40,128]{2,1,0:T(8,128)(2,1)} custom-call(s32[33]{0:T(128)} %get-tuple-element.25.owner_hbm, s32[32]{0:T(128)} %get-tuple-element.26.first_hbm, f32[64,40,128]{2,1,0:T(8,128)S(1)} %get-tuple-element.42.state_ref, f32[64,40,128]{2,1,0:T(8,128)S(1)} %get-tuple-element.43.lse_ref, bf16[32,48,128]{2,1,0:T(8,128)(2,1)S(1)} %all-to-all-done.1.slot_ref), custom_call_target="tpu_custom_call" | custom-call | flops 3276800 | bytes 3276800 | tf_op jit(solution)/shard_map/join_moved/pallas_call | solution.py:783
Async XLA Ops:
  2.9 18.5 %all-to-all-start = ((bf16[32,40,128]{2,1,0:T(8,128)(2,1)}), bf16[32,40,128]{2,1,0:T(8,128)(2,1)S(1)}, u32[]{:S(2)}, u32[]{:S(2)}) async-start(bf16[32,40,128]{2,1,0:T(8,128)(2,1)} %gather_queries.1), calls=%async_computation | async-start | bytes 655360 | tf_op jit(solution)/shard_map/all_to_all | solution.py:812
  23.8 17.4 %all-to-all-start.1 = ((bf16[32,48,128]{2,1,0:T(8,128)(2,1)}), bf16[32,48,128]{2,1,0:T(8,128)(2,1)S(1)}, u32[]{:S(2)}, u32[]{:S(2)}) async-start(bf16[32,48,128]{2,1,0:T(8,128)(2,1)} %moved_attention.1), calls=%async_computation.1 | async-start | bytes 786432 | tf_op jit(solution)/shard_map/all_to_all | solution.py:812
  29.0 9.6 %collective-permute-start = (bf16[128,1024]{1,0:T(8,128)(2,1)S(1)}, bf16[128,1024]{1,0:T(8,128)(2,1)S(1)}, u32[]{:S(2)}, u32[]{:S(2)}) collective-permute-start(bf16[128,1024]{1,0:T(8,128)(2,1)S(1)} %bitcast.13), channel_id=1, source_target_pairs={{0,1},{1,0},{2,3},{3,2},{4,5},{5,4},{6,7},{7,6},{8,9},{9,8},{10,11... | collective-permute-start | bytes 786440 | tf_op jit(solution)/shard_map/ppermute | solution.py:828

commit v5 on v4

--- a/solution.py
+++ b/solution.py
@@ -62,32 +62,45 @@
     repeat(groups, one_source, short)
 
 
-def repeat(count, step, unrolled):
-    if unrolled:
-        for n in range(count):
-            step(n, 0)
-    else:
-        lax.fori_loop(0, count, step, 0)
-
-
-def first_slots(owner, first, seen):
+def repeat(count, step, unrolled, carry=0):
+    if not unrolled:
+        return lax.fori_loop(0, count, step, carry)
+    for n in range(count):
+        carry = step(n, carry)
+    return carry
+
+
+def plan_size(slots):
+    return 3 * slots + 3
+
+
+def plan_joins(owner, plan, seen, slots):
+    short = slots <= 32
+    spare = 3 * slots + 2
+
     def unseen(n, _):
         seen[n] = -1
         return 0
 
-    short = first.shape[0] <= 32
-    repeat(seen.shape[0], unseen, short)
-
-    def first_slot(n, _):
+    def one_slot(n, counts):
+        firsts, laters = counts
         sequence = owner[n]
         place = jnp.maximum(sequence, 0)
         earlier = seen[place]
+        landed = sequence >= 0
+        is_first = landed & (earlier < 0)
+        is_later = landed & (earlier >= 0)
         mine = jnp.where(earlier < 0, n, earlier)
-        seen[place] = jnp.where(sequence < 0, earlier, mine)
-        first[n] = jnp.where(sequence < 0, -1, mine)
-        return 0
-
-    repeat(first.shape[0], first_slot, short)
+        seen[place] = jnp.where(landed, mine, earlier)
+        plan[n] = mine
+        plan[jnp.where(is_first, slots + firsts, spare)] = n
+        plan[jnp.where(is_later, 2 * slots + laters, spare)] = n
+        return firsts + is_first.astype(jnp.int32), laters + is_later.astype(jnp.int32)
+
+    repeat(seen.shape[0], unseen, short)
+    firsts, laters = repeat(slots, one_slot, short, (jnp.int32(0), jnp.int32(0)))
+    plan[3 * slots] = firsts
+    plan[3 * slots + 1] = laters
 
 
 def gather_kernel(
@@ -224,14 +237,9 @@
                     self.value_block(h - 1, b)
                 return 0
 
-            if h == 0:
-                self.score_block(0, 0)
-                keys_ready(0, 1)
-                self.score_block(0, 1)
-            else:
-                if h < count:
-                    keys_ready(h, 1)
-                lax.fori_loop(0, self.blocks, one_block, 0)
+            if h < count:
+                keys_ready(h, 1)
+            lax.fori_loop(0, self.blocks, one_block, 0)
             if h > 0:
                 done(h - 1)
 
@@ -266,8 +274,8 @@
 ):
     outs = 2 if count else 0
     local_hbm = refs[:outs]
-    owner_hbm, first_hbm, packed_hbm, send_ref, move_keys, move_values = refs[outs : outs + 6]
-    (table, lengths, pages, raw, query, packed, bias, x, dest, seq, owner, first, seen, w, keys, values,
+    owner_hbm, plan_hbm, packed_hbm, send_ref, move_keys, move_values = refs[outs : outs + 6]
+    (table, lengths, pages, raw, query, packed, bias, x, dest, seq, owner, plan, seen, w, keys, values,
      small_sems, key_sems, value_sems, move_sems, w_sems, out_sems, *attend_refs) = refs[outs + 6 :]
     pairs = min(count, 2)
     blocks, _, width = w.shape
@@ -283,7 +291,7 @@
         )
     ]
     owner_copy = pltpu.make_async_copy(owner, owner_hbm, out_sems.at[4, 0])
-    first_copy = pltpu.make_async_copy(first, first_hbm, out_sems.at[0, 0])
+    plan_copy = pltpu.make_async_copy(plan, plan_hbm, out_sems.at[0, 0])
     packed_copy = pltpu.make_async_copy(packed, packed_hbm, out_sems.at[3, 0])
     seqs = bias.shape[1]
     stride = query.shape[0] // seqs
@@ -382,12 +390,12 @@
         send_ref[b // per_owner, :, part] = product.astype(jnp.bfloat16)
         if b == 0:
             fill_owner(dest, seq, me, owner, moves)
-            first_slots(owner, first, seen)
+            plan_joins(owner, plan, seen, owner.shape[0] - 1)
             owner_copy.start()
-            first_copy.start()
+            plan_copy.start()
     lax.fori_loop(0, moves, wait_move, 0)
     owner_copy.wait()
-    first_copy.wait()
+    plan_copy.wait()
     packed_copy.wait()
     for h in range(count):
         wait_all(local_copies(h))
@@ -422,7 +430,7 @@
         pltpu.SMEM(dest.shape, jnp.int32),
         pltpu.SMEM(seq.shape, jnp.int32),
         pltpu.SMEM((slots + 1,), jnp.int32),
-        pltpu.SMEM((slots,), jnp.int32),
+        pltpu.SMEM((plan_size(slots),), jnp.int32),
         pltpu.SMEM((seqs,), jnp.int32),
         pltpu.VMEM((blocks, depth, width), bf16),
         pltpu.VMEM((held, pool, page, head_dim), bf16),
@@ -443,7 +451,7 @@
         out_specs=[hbm()] * (len(local) + 3) + [vmem()] * 3,
         out_shape=local + [
             pltpu.HBM((slots + 1,), jnp.int32),
-            pltpu.HBM((slots,), jnp.int32),
+            pltpu.HBM((plan_size(slots),), jnp.int32),
             pltpu.HBM((kv_heads, per_head * seqs, head_dim), bf16),
             jax.ShapeDtypeStruct((tp - 1, rows, columns), bf16),
             jax.ShapeDtypeStruct((moves,) + k_cache.shape[1:], bf16),
@@ -712,18 +720,18 @@
             transcendentals=moves * rows * kv_heads * page,
         ),
         name="moved_attention",
-    )(stay(dest), received, move_keys, move_values)
+    )(dest, received, move_keys, move_values)
 
 
 def join_kernel(
-    owner_hbm, first_hbm, state_ref, lse_ref, slot_ref, out_ref, owner_ref, first_ref, states,
+    owner_hbm, plan_hbm, state_ref, lse_ref, slot_ref, out_ref, owner_ref, plan, states,
     states_lse, come_lses, sems,
 ):
     seqs, rows, head_dim = out_ref.shape
     count = slot_ref.shape[0]
     copies = [
         pltpu.make_async_copy(owner_hbm, owner_ref, sems.at[0]),
-        pltpu.make_async_copy(first_hbm, first_ref, sems.at[1]),
+        pltpu.make_async_copy(plan_hbm, plan, sems.at[1]),
     ]
     start_all(copies)
     real = pl.ds(0, rows)
@@ -756,29 +764,24 @@
         states[n], states_lse[n] = join(n, state_ref[seq, real], lse_ref[seq, real])
         return 0
 
-    def later_slot(n, _):
-        first = first_ref[n]
-
-        @pl.when((first >= 0) & (first < n))
-        def _():
-            states[first], states_lse[first] = join(n, states[first], states_lse[first])
-
-        return 0
-
-    def store_slot(n, _):
-        @pl.when(first_ref[n] == n)
-        def _():
-            out_ref[owner_ref[n]] = states[n].astype(jnp.bfloat16)
-
+    def later_slot(k, _):
+        n = plan[2 * count + k]
+        first = plan[n]
+        states[first], states_lse[first] = join(n, states[first], states_lse[first])
+        return 0
+
+    def store_slot(k, _):
+        n = plan[count + k]
+        out_ref[owner_ref[n]] = states[n].astype(jnp.bfloat16)
         return 0
 
     lax.fori_loop(0, count, every_slot, 0, unroll=8)
-    lax.fori_loop(0, count, later_slot, 0)
-    lax.fori_loop(0, count, store_slot, 0)
-
-
-def join_moved(owner, first, state, state_lse, answers, shape):
-    slots = first.shape[0]
+    lax.fori_loop(0, plan[3 * count + 1], later_slot, 0)
+    lax.fori_loop(0, plan[3 * count], store_slot, 0)
+
+
+def join_moved(owner, plan, state, state_lse, answers, shape):
+    slots = answers.shape[0]
     block = pltpu.VMEM((slots,) + shape[1:], jnp.float32)
     return pl.pallas_call(
         join_kernel,
@@ -787,7 +790,7 @@
         out_shape=jax.ShapeDtypeStruct(shape, jnp.bfloat16),
         scratch_shapes=[
             pltpu.SMEM(owner.shape, jnp.int32),
-            pltpu.SMEM(first.shape, jnp.int32),
+            pltpu.SMEM(plan.shape, jnp.int32),
             block, block, block,
             pltpu.SemaphoreType.DMA((2,)),
         ],
@@ -796,7 +799,7 @@
             flops=10 * state.size, bytes_accessed=10 * state.size, transcendentals=0
         ),
         name="join_moved",
-    )(stay(owner), stay(first), state, state_lse, answers)
+    )(stay(owner), stay(plan), state, state_lse, answers)
 
 
 def per_device(
@@ -818,7 +821,7 @@
     early_rows, to_send = lax.optimization_barrier((rows, to_send))
     received = exchange(to_send)
     table, lengths = page_table.T, lengths.reshape(1, seqs)
-    *before, owner, first, packed, partial, move_keys, move_values = early_work(
+    *before, owner, plan, packed, partial, move_keys, move_values = early_work(
         table, lengths, move_page, early_rows, tokens_in, dest, move_seq, k_cache, v_cache, w_kv,
         groups, tp, early, scale,
     )
@@ -837,7 +840,7 @@
         other, packed, x, w, before + [totals, tops], seqs, heads * steps // kv_heads, steps, scale
     )
     attended = join_moved(
-        owner, first, state, state_lse, returned, (seqs, heads * steps, head_dim)
+        owner, plan, state, state_lse, returned, (seqs, heads * steps, head_dim)
     )
     attended = attended.reshape(seqs, heads, steps, head_dim).transpose(0, 2, 1, 3)
     return (attended, new_kv)

time: 44.8 us -> 43.7 us (0.975)
  Pallas kernels: 27.9 us -> 26.7 us
    pallas_call x1, Pallas kernels: 2.93 us -> 2.1 us  [join_moved(): pl.pallas_call(join_kernel, in_specs=[hbm()] * 2 + [vmem()] * 3, out_spec...]
where the time goes in v5:
time: 43.7 us; the launch traced here: 43.3 us
  Pallas kernels  26.7 us (61%)
  starting transfers between devices  14.1 us (32%)
  waiting for transfers between devices  1.64 us (4%)
  between operations  0.86 us (2%)
    all_to_all x2, starting transfers between devices, exchange(): return lax.all_to_all(array, 'gen', split_axis=0, concat_axis=0, tiled=True)  12.5 us
    pallas_call x1, Pallas kernels, early_work(): pl.pallas_call(functools.partial(early_kernel, tp=tp, scale=scale, count=...  10.2 us
    pallas_call x1, Pallas kernels, late_work(): pl.pallas_call(functools.partial(late_kernel, scale=scale, early=early, c...  7.94 us
    pallas_call x1, Pallas kernels, moved_attention(): pl.pallas_call(functools.partial(moved_kernel, scale=scale), in_specs=[hb...  2.32 us
    pallas_call x1, Pallas kernels, gather(): pl.pallas_call(functools.partial(gather_kernel, per_source=dest.shape[0]...  2.23 us
    pallas_call x1, Pallas kernels, join_moved(): pl.pallas_call(join_kernel, in_specs=[hbm()] * 2 + [vmem()] * 3, out_spec...  2.1 us
    pallas_call x1, Pallas kernels, join_new(): pl.pallas_call(functools.partial(new_kernel, parts=len(local) // 2, per_h...  1.94 us
    all_to_all x2, waiting for transfers between devices, exchange(): return lax.all_to_all(array, 'gen', split_axis=0, concat_axis=0, tiled=True)  1.64 us
  transfers between devices with their start and end apart: 3, of which 2 were waited for; matrix products, arithmetic and copies ran while one was open for 0% of the time, Pallas kernels for 46%

profile of v5, /device:TPU:0, one launch (start us, length us, event | category | flops | bytes accessed | tf_op | source)
XLA Modules:
  0.0 43.3 jit_solution(13227304397644957592)
XLA Ops:
  0.6 2.2 %gather_queries.1 = bf16[32,40,128]{2,1,0:T(8,128)(2,1)} custom-call(s32[256]{0:T(256)} %bitcast.13, s32[256]{0:T(256)} %seq_hbm.3, bf16[64,40,128]{2,1,0:T(8,128)(2,1)} %bitcast.17), custom_call_target="tpu_custom_call" | custom-call | bytes 1310720 | tf_op jit(solution)/shard_map/gather_queries/pallas_call | solution.py:132
  2.9 7.4 %all-to-all-start = ((bf16[32,40,128]{2,1,0:T(8,128)(2,1)}), bf16[32,40,128]{2,1,0:T(8,128)(2,1)S(1)}, u32[]{:S(2)}, u32[]{:S(2)}) async-start(bf16[32,40,128]{2,1,0:T(8,128)(2,1)} %gather_queries.1), calls=%async_computation | async-start | bytes 655360 | tf_op jit(solution)/shard_map/all_to_all | solution.py:815
  10.3 0.0 copy-start
  10.3 10.2 %early_heads_and_sent_kv.1 = (f32[2,640,256]{2,1,0:T(8,128)}, f32[2,640,128]{2,1,0:T(8,128)}, s32[33]{0:T(128)}, s32[99]{0:T(128)}, bf16[4,640,128]{2,1,0:T(8,12...) custom-call(s32[32,64]{1,0:T(8,128)} %bitcast.20, ...), custom_call_target="tpu_custom_call" | custom-call | flops 5368709120 | bytes 8912896 | tf_op jit(solution)/shard_map/early_heads_and_sent_kv/pallas_call | solution.py:448
  20.5 0.9 %all-to-all-done.q_ref = bf16[32,40,128]{2,1,0:T(8,128)(2,1)S(1)} async-done(((bf16[32,40,128]{2,1,0:T(8,128)(2,1)}), bf16[32,40,128]{2,1,0:T(8,128)(2,1)S(1)}, u32[]{:S(2)}, u32[]{:S(2)}) %all-to-all-start) | async-done | bytes 327712 | tf_op jit(solution)/shard_map/all_to_all | solution.py:815
  21.4 0.0 copy-done
  21.4 2.3 %moved_attention.1 = bf16[32,48,128]{2,1,0:T(8,128)(2,1)} custom-call(s32[256]{0:T(256)S(1)} %bitcast.15, bf16[32,40,128]{2,1,0:T(8,128)(2,1)S(1)} %all-to-all-done.q_ref, bf16[16,4,64,128]{3,2,1,0:T(8,128)(2,1)S(1)} %get-tuple-element.30.keys, bf16[16,4,64,128]{3,2,1,0:T(8,128)(2,1)S(1)} %get-tuple-element.31.values), custom_call_target="tpu_custom_call" | custom-call | flops 83886080 | bytes 655360 | tf_op jit(solution)/shard_map/moved_attention/pallas_call | solution.py:706
  23.7 5.1 %all-to-all-start.1 = ((bf16[32,48,128]{2,1,0:T(8,128)(2,1)}), bf16[32,48,128]{2,1,0:T(8,128)(2,1)S(1)}, u32[]{:S(2)}, u32[]{:S(2)}) async-start(bf16[32,48,128]{2,1,0:T(8,128)(2,1)} %moved_attention.1), calls=%async_computation.1 | async-start | bytes 786432 | tf_op jit(solution)/shard_map/all_to_all | solution.py:815
  28.9 1.6 %collective-permute-start = (bf16[128,1024]{1,0:T(8,128)(2,1)S(1)}, bf16[128,1024]{1,0:T(8,128)(2,1)S(1)}, u32[]{:S(2)}, u32[]{:S(2)}) collective-permute-start(bf16[128,1024]{1,0:T(8,128)(2,1)S(1)} %bitcast.16), channel_id=1, source_target_pairs={{0,1},{1,0},{2,3},{3,2},{4,5},{5,4},{6,7},{7,6},{8,9},{9,8},{10,11... | collective-permute-start | bytes 786440 | tf_op jit(solution)/shard_map/ppermute | solution.py:831
  30.4 7.9 %late_heads.1 = (f32[2,640,256]{2,1,0:T(8,128)S(1)}, f32[2,640,128]{2,1,0:T(8,128)S(1)}, bf16[4,640,128]{2,1,0:T(8,128)(2,1)S(1)}, bf16[128,2560]{1,0:T(8,128)(2...) custom-call(s32[32,64]{1,0:T(8,128)} %bitcast.21, ...), custom_call_target="tpu_custom_call" | custom-call | flops 4697620480 | bytes 3670016 | tf_op jit(solution)/shard_map/late_heads/pallas_call | solution.py:529
  38.4 0.0 collective-permute-done
  38.4 1.9 %join_new.1 = (bf16[128,1024]{1,0:T(8,128)(2,1)}, f32[64,40,128]{2,1,0:T(8,128)S(1)}, f32[64,40,128]{2,1,0:T(8,128)S(1)}) custom-call(bf16[1,128,1024]{2,1,0:T(8,128)(2,1)S(1)} %bitcast.12, bf16[4,640,128]{2,1,0:T(8,128)(2,1)S(1)} %get-tuple-element.35.packed, bf16[128,2560]{1,0:T(8,128)(2,1)S(1)} %get-tuple-element.36.x, ...), custom_call_target="tpu_custom_call" | custom-call | flops 677642240 | bytes 6553600 | tf_op jit(solution)/shard_map/join_new/pallas_call | solution.py:624
  40.3 0.7 %all-to-all-done.1.slot_ref = bf16[32,48,128]{2,1,0:T(8,128)(2,1)S(1)} async-done(((bf16[32,48,128]{2,1,0:T(8,128)(2,1)}), bf16[32,48,128]{2,1,0:T(8,128)(2,1)S(1)}, u32[]{:S(2)}, u32[]{:S(2)}) %all-to-all-start.1) | async-done | bytes 393248 | tf_op jit(solution)/shard_map/all_to_all | solution.py:815
  41.0 2.1 %join_moved.1 = bf16[64,40,128]{2,1,0:T(8,128)(2,1)} custom-call(s32[33]{0:T(128)} %get-tuple-element.25.owner_hbm, s32[99]{0:T(128)} %get-tuple-element.26.plan_hbm, f32[64,40,128]{2,1,0:T(8,128)S(1)} %get-tuple-element.42.state_ref, f32[64,40,128]{2,1,0:T(8,128)S(1)} %get-tuple-element.43.lse_ref, bf16[32,48,128]{2,1,0:T(8,128)(2,1)S(1)} %all-to-all-done.1.slot_ref), custom_call_target="tpu_custom_call" | custom-call | flops 3276800 | bytes 3276800 | tf_op jit(solution)/shard_map/join_moved/pallas_call | solution.py:786
Async XLA Ops:
  2.9 18.5 %all-to-all-start = ((bf16[32,40,128]{2,1,0:T(8,128)(2,1)}), bf16[32,40,128]{2,1,0:T(8,128)(2,1)S(1)}, u32[]{:S(2)}, u32[]{:S(2)}) async-start(bf16[32,40,128]{2,1,0:T(8,128)(2,1)} %gather_queries.1), calls=%async_computation | async-start | bytes 655360 | tf_op jit(solution)/shard_map/all_to_all | solution.py:815
  10.3 11.1 %copy-start = (s32[256,1]{0,1:T(1,128)S(1)}, s32[256,1]{0,1:T(1,128)}, u32[]{:S(2)}) copy-start(s32[256,1]{0,1:T(1,128)} %param.17) | copy-start | bytes 3076
  23.7 17.3 %all-to-all-start.1 = ((bf16[32,48,128]{2,1,0:T(8,128)(2,1)}), bf16[32,48,128]{2,1,0:T(8,128)(2,1)S(1)}, u32[]{:S(2)}, u32[]{:S(2)}) async-start(bf16[32,48,128]{2,1,0:T(8,128)(2,1)} %moved_attention.1), calls=%async_computation.1 | async-start | bytes 786432 | tf_op jit(solution)/shard_map/all_to_all | solution.py:815
  28.9 9.5 %collective-permute-start = (bf16[128,1024]{1,0:T(8,128)(2,1)S(1)}, bf16[128,1024]{1,0:T(8,128)(2,1)S(1)}, u32[]{:S(2)}, u32[]{:S(2)}) collective-permute-start(bf16[128,1024]{1,0:T(8,128)(2,1)S(1)} %bitcast.16), channel_id=1, source_target_pairs={{0,1},{1,0},{2,3},{3,2},{4,5},{5,4},{6,7},{7,6},{8,9},{9,8},{10,11... | collective-permute-start | bytes 786440 | tf_op jit(solution)/shard_map/ppermute | solution.py:831

commit v6 on v5

--- a/solution.py
+++ b/solution.py
@@ -36,7 +36,13 @@
 
 
 def answer_rows(rows):
-    return (rows + 3 + 15) // 16 * 16
+    return CAP * padded(rows) + 8
+
+
+def piece_mask(rows):
+    tall = lax.broadcasted_iota(jnp.int32, (rows, LANES), 0)
+    lane = lax.broadcasted_iota(jnp.int32, (rows, LANES), 1)
+    return (lane == tall) | (lane == tall + rows) | (lane == tall + 2 * rows)
 
 
 def fill_owner(dest, seq, me, owner, per_source):
@@ -643,21 +649,21 @@
     )(other, packed, x, w, *local)
 
 
-def moved_kernel(dest_hbm, q_ref, keys, values, out_ref, dest_ref, slot, sem, *, scale):
+def moved_kernel(
+    dest_hbm, q_ref, keys, values, out_ref, dest_ref, slot, place, lse_place, flat, sem, *, scale
+):
     moves, kv_heads, page, head_dim = keys.shape
     rows = q_ref.shape[1]
-    padding = out_ref.shape[1] - rows
     columns = kv_heads * page
     me = lax.axis_index("gen")
     dest_copy = pltpu.make_async_copy(dest_hbm, dest_ref, sem.at[0])
     dest_copy.start()
-    out_ref[...] = jnp.zeros(out_ref.shape, jnp.bfloat16)
+    flat[...] = jnp.zeros(flat.shape, jnp.float32)
     row = lax.broadcasted_iota(jnp.int32, (rows, columns), 0)
     column = lax.broadcasted_iota(jnp.int32, (rows, columns), 1)
     other_head = jnp.where(row // (rows // kv_heads) == column // page, 0.0, NEGATIVE)
-    tall = lax.broadcasted_iota(jnp.int32, (rows, LANES), 0)
     lane = lax.broadcasted_iota(jnp.int32, (rows, LANES), 1)
-    spare = lax.broadcasted_iota(jnp.int32, (padding, LANES), 0)
+    mask = piece_mask(rows)
     ones = jnp.ones((columns, head_dim), jnp.bfloat16)
 
     def one_move(k):
@@ -674,13 +680,14 @@
         summed = jnp.dot(weights, both, preferred_element_type=jnp.float32)
         weight_sum = summed[:, head_dim:]
         lse = biggest * scale + jnp.log2(weight_sum)
-        lse = jnp.sum(jnp.where(tall == lane, lse, 0.0), axis=0, keepdims=True)
         high = lse.astype(jnp.bfloat16).astype(jnp.float32)
         middle = (lse - high).astype(jnp.bfloat16).astype(jnp.float32)
         low = lse - high - middle
-        pieces = jnp.where(spare == 0, high, jnp.where(spare == 1, middle, low))
-        result = jnp.concatenate([summed[:, :head_dim] / weight_sum, pieces], axis=0)
-        return result.astype(jnp.bfloat16)
+        piece = jnp.where(lane < rows, high, jnp.where(lane < 2 * rows, middle, low))
+        return (
+            summed[:, :head_dim] / weight_sum,
+            jnp.sum(jnp.where(mask, piece, 0.0), axis=0, keepdims=True),
+        )
 
     dest_copy.wait()
     for k in range(moves):
@@ -689,28 +696,38 @@
         for j in range(k):
             rank = rank + (dest_ref[me * moves + j] == mine).astype(jnp.int32)
         slot[k] = mine * CAP + rank
+        first = mine * answer_rows(rows)
+        place[k] = first + rank * padded(rows)
+        lse_place[k] = first + CAP * padded(rows) + rank
     batch = min(16, moves)
 
     def some_moves(b, _):
         results = [one_move(b * batch + k) for k in range(batch)]
-        for k in range(batch):
-            out_ref[slot[b * batch + k]] = results[k]
+        for k, (result, lse) in enumerate(results):
+            move = b * batch + k
+            flat[pl.ds(pl.multiple_of(place[move], 8), rows), :] = result
+            flat[pl.ds(lse_place[move], 1), :] = lse
         return 0
 
     lax.fori_loop(0, moves // batch, some_moves, 0)
+    out_ref[...] = flat[...].astype(jnp.bfloat16)
 
 
 def moved_attention(dest, received, move_keys, move_values, scale):
     moves, kv_heads, page, head_dim = move_keys.shape
     count, rows, _ = received.shape
+    shape = (count // CAP * answer_rows(rows), head_dim)
     return pl.pallas_call(
         functools.partial(moved_kernel, scale=scale),
         in_specs=[hbm(), vmem(), vmem(), vmem()],
         out_specs=vmem(),
-        out_shape=jax.ShapeDtypeStruct((count, answer_rows(rows), head_dim), jnp.bfloat16),
+        out_shape=jax.ShapeDtypeStruct(shape, jnp.bfloat16),
         scratch_shapes=[
             pltpu.SMEM(dest.shape, jnp.int32),
             pltpu.SMEM((moves,), jnp.int32),
+            pltpu.SMEM((moves,), jnp.int32),
+            pltpu.SMEM((moves,), jnp.int32),
+            pltpu.VMEM(shape, jnp.float32),
             pltpu.SemaphoreType.DMA((1,)),
         ],
         compiler_params=limit(4),
@@ -725,25 +742,23 @@
 
 def join_kernel(
     owner_hbm, plan_hbm, state_ref, lse_ref, slot_ref, out_ref, owner_ref, plan, states,
-    states_lse, come_lses, sems,
+    states_lse, come_lses, flat, sems,
 ):
     seqs, rows, head_dim = out_ref.shape
-    count = slot_ref.shape[0]
+    count = states.shape[0]
     copies = [
         pltpu.make_async_copy(owner_hbm, owner_ref, sems.at[0]),
         pltpu.make_async_copy(plan_hbm, plan, sems.at[1]),
     ]
     start_all(copies)
     real = pl.ds(0, rows)
-    tall = lax.broadcasted_iota(jnp.int32, (rows, LANES), 0)
-    lane = lax.broadcasted_iota(jnp.int32, (rows, LANES), 1)
+    mask = piece_mask(rows)
     out_ref[...] = state_ref[:, :rows, :].astype(jnp.bfloat16)
+    flat[...] = slot_ref[...].astype(jnp.float32)
 
     def answer_lse(n, _):
-        pieces = slot_ref[n, pl.ds(rows // 8 * 8, slot_ref.shape[1] - rows // 8 * 8)]
-        pieces = pieces.astype(jnp.float32)[rows % 8 :]
-        packed = pieces[0:1] + pieces[1:2] + pieces[2:3]
-        lse = jnp.sum(jnp.where(tall == lane, packed, 0.0), axis=1, keepdims=True)
+        row = n // CAP * answer_rows(rows) + CAP * padded(rows) + n % CAP
+        lse = jnp.sum(jnp.where(mask, flat[pl.ds(row, 1), :], 0.0), axis=1, keepdims=True)
         come_lses[n] = jnp.broadcast_to(lse, (rows, LANES))
         return 0
 
@@ -756,7 +771,8 @@
         old = jnp.exp2(old_lse - top)
         come = jnp.exp2(come_lse - top)
         weight = old + come
-        come_sum = slot_ref[n].astype(jnp.float32)[:rows]
+        place = n // CAP * answer_rows(rows) + n % CAP * padded(rows)
+        come_sum = flat[pl.ds(pl.multiple_of(place, 8), rows), :]
         return (old * old_sum + come * come_sum) / weight, top + jnp.log2(weight)
 
     def every_slot(n, _):
@@ -781,7 +797,7 @@
 
 
 def join_moved(owner, plan, state, state_lse, answers, shape):
-    slots = answers.shape[0]
+    slots = answers.shape[0] // answer_rows(shape[1]) * CAP
     block = pltpu.VMEM((slots,) + shape[1:], jnp.float32)
     return pl.pallas_call(
         join_kernel,
@@ -792,6 +808,7 @@
             pltpu.SMEM(owner.shape, jnp.int32),
             pltpu.SMEM(plan.shape, jnp.int32),
             block, block, block,
+            pltpu.VMEM(answers.shape, jnp.float32),
             pltpu.SemaphoreType.DMA((2,)),
         ],
         compiler_params=limit(8),

time: 43.7 us -> 43.2 us (0.989)
  waiting for transfers between devices: 1.64 us -> 1.11 us
    all_to_all x2, waiting for transfers between devices: 1.64 us -> 1.11 us  [exchange(): return lax.all_to_all(array, 'gen', split_axis=0, concat_axis=0, tiled=True)]
  transfers between devices with their start and end apart: 3 -> 3, of which waited for: 2 -> 2; matrix products, arithmetic and copies ran while one was open for 0% -> 0% of each run, Pallas kernels for 46% -> 47%
where the time goes in v6:
time: 43.2 us; the launch traced here: 42.8 us
  Pallas kernels  26.8 us (62%)
  starting transfers between devices  14.1 us (33%)
  waiting for transfers between devices  1.11 us (3%)
  between operations  0.86 us (2%)
    all_to_all x2, starting transfers between devices, exchange(): return lax.all_to_all(array, 'gen', split_axis=0, concat_axis=0, tiled=True)  12.5 us
    pallas_call x1, Pallas kernels, early_work(): pl.pallas_call(functools.partial(early_kernel, tp=tp, scale=scale, count=...  10.2 us
    pallas_call x1, Pallas kernels, late_work(): pl.pallas_call(functools.partial(late_kernel, scale=scale, early=early, c...  7.94 us
    pallas_call x1, Pallas kernels, moved_attention(): pl.pallas_call(functools.partial(moved_kernel, scale=scale), in_specs=[hb...  2.36 us
    pallas_call x1, Pallas kernels, gather(): pl.pallas_call(functools.partial(gather_kernel, per_source=dest.shape[0]...  2.23 us
    pallas_call x1, Pallas kernels, join_moved(): pl.pallas_call(join_kernel, in_specs=[hbm()] * 2 + [vmem()] * 3, out_spec...  2.12 us
    pallas_call x1, Pallas kernels, join_new(): pl.pallas_call(functools.partial(new_kernel, parts=len(local) // 2, per_h...  1.94 us
    ppermute x1, starting transfers between devices, per_device(): pieces.append(lax.ppermute(partial[k - 1], 'tp', pairs))  1.55 us
  transfers between devices with their start and end apart: 3, of which 2 were waited for; matrix products, arithmetic and copies ran while one was open for 0% of the time, Pallas kernels for 47%

profile of v6, /device:TPU:0, one launch (start us, length us, event | category | flops | bytes accessed | tf_op | source)
XLA Modules:
  0.0 42.8 jit_solution(13461254574892294904)
XLA Ops:
  0.6 2.2 %gather_queries.1 = bf16[32,40,128]{2,1,0:T(8,128)(2,1)} custom-call(s32[256]{0:T(256)} %bitcast.16, s32[256]{0:T(256)} %seq_hbm.3, bf16[64,40,128]{2,1,0:T(8,128)(2,1)} %bitcast.20), custom_call_target="tpu_custom_call" | custom-call | bytes 1310720 | tf_op jit(solution)/shard_map/gather_queries/pallas_call | solution.py:138
  2.9 7.4 %all-to-all-start = ((bf16[32,40,128]{2,1,0:T(8,128)(2,1)}), bf16[32,40,128]{2,1,0:T(8,128)(2,1)S(1)}, u32[]{:S(2)}, u32[]{:S(2)}) async-start(bf16[32,40,128]{2,1,0:T(8,128)(2,1)} %gather_queries.1), calls=%async_computation | async-start | bytes 655360 | tf_op jit(solution)/shard_map/all_to_all | solution.py:832
  10.3 0.0 copy-start
  10.3 10.2 %early_heads_and_sent_kv.1 = (f32[2,640,256]{2,1,0:T(8,128)}, f32[2,640,128]{2,1,0:T(8,128)}, s32[33]{0:T(128)}, s32[99]{0:T(128)}, bf16[4,640,128]{2,1,0:T(8,12...) custom-call(s32[32,64]{1,0:T(8,128)} %bitcast.23, ...), custom_call_target="tpu_custom_call" | custom-call | flops 5368709120 | bytes 8912896 | tf_op jit(solution)/shard_map/early_heads_and_sent_kv/pallas_call | solution.py:454
  20.5 0.9 %all-to-all-done.q_ref = bf16[32,40,128]{2,1,0:T(8,128)(2,1)S(1)} async-done(((bf16[32,40,128]{2,1,0:T(8,128)(2,1)}), bf16[32,40,128]{2,1,0:T(8,128)(2,1)S(1)}, u32[]{:S(2)}, u32[]{:S(2)}) %all-to-all-start) | async-done | bytes 327712 | tf_op jit(solution)/shard_map/all_to_all | solution.py:832
  21.4 0.0 copy-done
  21.4 2.4 %moved_attention.1 = bf16[1408,128]{1,0:T(8,128)(2,1)} custom-call(s32[256]{0:T(256)S(1)} %bitcast.18, bf16[32,40,128]{2,1,0:T(8,128)(2,1)S(1)} %all-to-all-done.q_ref, bf16[16,4,64,128]{3,2,1,0:T(8,128)(2,1)S(1)} %get-tuple-element.30.keys, bf16[16,4,64,128]{3,2,1,0:T(8,128)(2,1)S(1)} %get-tuple-element.31.values), custom_call_target="tpu_custom_call" | custom-call | flops 83886080 | bytes 655360 | tf_op jit(solution)/shard_map/moved_attention/pallas_call | solution.py:720
  23.7 5.1 %all-to-all-start.1 = ((bf16[16,88,128]{2,1,0:T(8,128)(2,1)}), bf16[16,88,128]{2,1,0:T(8,128)(2,1)S(1)}, u32[]{:S(2)}, u32[]{:S(2)}) async-start(bf16[16,88,128]{2,1,0:T(8,128)(2,1)} %bitcast.9), calls=%async_computation.1 | async-start | bytes 720896 | tf_op jit(solution)/shard_map/all_to_all | solution.py:832
  28.9 1.6 %collective-permute-start = (bf16[128,1024]{1,0:T(8,128)(2,1)S(1)}, bf16[128,1024]{1,0:T(8,128)(2,1)S(1)}, u32[]{:S(2)}, u32[]{:S(2)}) collective-permute-start(bf16[128,1024]{1,0:T(8,128)(2,1)S(1)} %bitcast.19), channel_id=1, source_target_pairs={{0,1},{1,0},{2,3},{3,2},{4,5},{5,4},{6,7},{7,6},{8,9},{9,8},{10,11... | collective-permute-start | bytes 786440 | tf_op jit(solution)/shard_map/ppermute | solution.py:848
  30.5 7.9 %late_heads.1 = (f32[2,640,256]{2,1,0:T(8,128)S(1)}, f32[2,640,128]{2,1,0:T(8,128)S(1)}, bf16[4,640,128]{2,1,0:T(8,128)(2,1)S(1)}, bf16[128,2560]{1,0:T(8,128)(2...) custom-call(s32[32,64]{1,0:T(8,128)} %bitcast.24, ...), custom_call_target="tpu_custom_call" | custom-call | flops 4697620480 | bytes 3670016 | tf_op jit(solution)/shard_map/late_heads/pallas_call | solution.py:535
  38.4 0.0 collective-permute-done
  38.4 1.9 %join_new.1 = (bf16[128,1024]{1,0:T(8,128)(2,1)}, f32[64,40,128]{2,1,0:T(8,128)S(1)}, f32[64,40,128]{2,1,0:T(8,128)S(1)}) custom-call(bf16[1,128,1024]{2,1,0:T(8,128)(2,1)S(1)} %bitcast.15, bf16[4,640,128]{2,1,0:T(8,128)(2,1)S(1)} %get-tuple-element.35.packed, bf16[128,2560]{1,0:T(8,128)(2,1)S(1)} %get-tuple-element.36.x, ...), custom_call_target="tpu_custom_call" | custom-call | flops 677642240 | bytes 6553600 | tf_op jit(solution)/shard_map/join_new/pallas_call | solution.py:630
  40.4 0.2 all-to-all-done.1
  40.6 2.1 %join_moved.1 = bf16[64,40,128]{2,1,0:T(8,128)(2,1)} custom-call(s32[33]{0:T(128)} %get-tuple-element.25.owner_hbm, s32[99]{0:T(128)} %get-tuple-element.26.plan_hbm, f32[64,40,128]{2,1,0:T(8,128)S(1)} %get-tuple-element.42.state_ref, f32[64,40,128]{2,1,0:T(8,128)S(1)} %get-tuple-element.43.lse_ref, bf16[1408,128]{1,0:T(8,128)(2,1)S(1)} %bitcast.14), custom_call_target="tpu_custom_call" | custom-call | flops 3276800 | bytes 3276800 | tf_op jit(solution)/shard_map/join_moved/pallas_call | solution.py:802
Async XLA Ops:
  2.9 18.5 %all-to-all-start = ((bf16[32,40,128]{2,1,0:T(8,128)(2,1)}), bf16[32,40,128]{2,1,0:T(8,128)(2,1)S(1)}, u32[]{:S(2)}, u32[]{:S(2)}) async-start(bf16[32,40,128]{2,1,0:T(8,128)(2,1)} %gather_queries.1), calls=%async_computation | async-start | bytes 655360 | tf_op jit(solution)/shard_map/all_to_all | solution.py:832
  10.3 11.1 %copy-start = (s32[256,1]{0,1:T(1,128)S(1)}, s32[256,1]{0,1:T(1,128)}, u32[]{:S(2)}) copy-start(s32[256,1]{0,1:T(1,128)} %param.17) | copy-start | bytes 3076
  23.7 16.8 %all-to-all-start.1 = ((bf16[16,88,128]{2,1,0:T(8,128)(2,1)}), bf16[16,88,128]{2,1,0:T(8,128)(2,1)S(1)}, u32[]{:S(2)}, u32[]{:S(2)}) async-start(bf16[16,88,128]{2,1,0:T(8,128)(2,1)} %bitcast.9), calls=%async_computation.1 | async-start | bytes 720896 | tf_op jit(solution)/shard_map/all_to_all | solution.py:832
  28.9 9.5 %collective-permute-start = (bf16[128,1024]{1,0:T(8,128)(2,1)S(1)}, bf16[128,1024]{1,0:T(8,128)(2,1)S(1)}, u32[]{:S(2)}, u32[]{:S(2)}) collective-permute-start(bf16[128,1024]{1,0:T(8,128)(2,1)S(1)} %bitcast.19), channel_id=1, source_target_pairs={{0,1},{1,0},{2,3},{3,2},{4,5},{5,4},{6,7},{7,6},{8,9},{9,8},{10,11... | collective-permute-start | bytes 786440 | tf_op jit(solution)/shard_map/ppermute | solution.py:848

commit v7 on v6

--- a/solution.py
+++ b/solution.py
@@ -576,19 +576,25 @@
     rows, rows_lse = state.reshape(flat), state_lse.reshape(flat)
     width = 2 * head_dim
     head = 0
+    copies = []
     for part in range(parts):
         totals, tops = local[2 * part], local[2 * part + 1]
         for h in range(totals.shape[0]):
-            columns = slice(head * width, (head + 1) * width)
             if head % 2 == 0:
-                both = jnp.dot(
-                    x[...], w[:, head * width : (head + 2) * width], preferred_element_type=jnp.float32
+                pair = slice(head * width, min((head + 2) * width, w.shape[1]))
+                partial = jnp.dot(x[...], w[:, pair], preferred_element_type=jnp.float32)
+                for k in range(other_ref.shape[0]):
+                    partial = partial + other_ref[k, :, pair].astype(jnp.float32)
+                both = partial.astype(jnp.bfloat16)
+                new[:, pair] = both
+                part = pl.ds(pair.start, pair.stop - pair.start)
+                copies.append(
+                    pltpu.make_async_copy(
+                        new.at[:, part], new_hbm.at[:, part], sem.at[len(copies)]
+                    )
                 )
-            partial = both[:, head % 2 * width : (head % 2 + 1) * width]
-            for k in range(other_ref.shape[0]):
-                partial = partial + other_ref[k, :, columns].astype(jnp.float32)
-            rounded = partial.astype(jnp.bfloat16)
-            new[:, columns] = rounded
+                copies[-1].start()
+            rounded = both[:, head % 2 * width : (head % 2 + 1) * width]
             fresh[head, 0] = rounded[:, :head_dim].astype(jnp.float32)
             fresh[head, 1] = rounded[:, head_dim:].astype(jnp.float32)
             new_keys, new_values = [], []
@@ -618,9 +624,7 @@
                 rows[place, :] = summed / weight
                 rows_lse[place, :] = top + jnp.log2(weight)
             head += 1
-    copy = pltpu.make_async_copy(new, new_hbm, sem.at[0])
-    copy.start()
-    copy.wait()
+    wait_all(copies)
 
 
 def join_new(other, packed, x, w, local, seqs, per_head, steps, scale):
@@ -637,7 +641,7 @@
         scratch_shapes=[
             pltpu.VMEM((x.shape[0], columns), jnp.bfloat16),
             pltpu.VMEM((columns // (2 * head_dim), 2, x.shape[0], head_dim), jnp.float32),
-            pltpu.SemaphoreType.DMA((1,)),
+            pltpu.SemaphoreType.DMA(((kv_heads + 1) // 2,)),
         ],
         compiler_params=limit(8),
         cost_estimate=pl.CostEstimate(

time: 43.2 us -> 43.2 us (level)
  no operation moved by 1% of the time
where the time goes in v7:
time: 43.2 us; the launch traced here: 42.8 us
  Pallas kernels  26.7 us (62%)
  starting transfers between devices  14.1 us (33%)
  waiting for transfers between devices  1.14 us (3%)
  between operations  0.86 us (2%)
    all_to_all x2, starting transfers between devices, exchange(): return lax.all_to_all(array, 'gen', split_axis=0, concat_axis=0, tiled=True)  12.5 us
    pallas_call x1, Pallas kernels, early_work(): pl.pallas_call(functools.partial(early_kernel, tp=tp, scale=scale, count=...  10.2 us
    pallas_call x1, Pallas kernels, late_work(): pl.pallas_call(functools.partial(late_kernel, scale=scale, early=early, c...  7.94 us
    pallas_call x1, Pallas kernels, moved_attention(): pl.pallas_call(functools.partial(moved_kernel, scale=scale), in_specs=[hb...  2.36 us
    pallas_call x1, Pallas kernels, gather(): pl.pallas_call(functools.partial(gather_kernel, per_source=dest.shape[0]...  2.23 us
    pallas_call x1, Pallas kernels, join_moved(): pl.pallas_call(join_kernel, in_specs=[hbm()] * 2 + [vmem()] * 3, out_spec...  2.1 us
    pallas_call x1, Pallas kernels, join_new(): pl.pallas_call(functools.partial(new_kernel, parts=len(local) // 2, per_h...  1.91 us
    ppermute x1, starting transfers between devices, per_device(): pieces.append(lax.ppermute(partial[k - 1], 'tp', pairs))  1.55 us
  transfers between devices with their start and end apart: 3, of which 2 were waited for; matrix products, arithmetic and copies ran while one was open for 0% of the time, Pallas kernels for 47%

profile of v7, /device:TPU:0, one launch (start us, length us, event | category | flops | bytes accessed | tf_op | source)
XLA Modules:
  0.0 42.8 jit_solution(429206346321605303)
XLA Ops:
  0.6 2.2 %gather_queries.1 = bf16[32,40,128]{2,1,0:T(8,128)(2,1)} custom-call(s32[256]{0:T(256)} %bitcast.16, s32[256]{0:T(256)} %seq_hbm.3, bf16[64,40,128]{2,1,0:T(8,128)(2,1)} %bitcast.20), custom_call_target="tpu_custom_call" | custom-call | bytes 1310720 | tf_op jit(solution)/shard_map/gather_queries/pallas_call | solution.py:138
  2.9 7.4 %all-to-all-start = ((bf16[32,40,128]{2,1,0:T(8,128)(2,1)}), bf16[32,40,128]{2,1,0:T(8,128)(2,1)S(1)}, u32[]{:S(2)}, u32[]{:S(2)}) async-start(bf16[32,40,128]{2,1,0:T(8,128)(2,1)} %gather_queries.1), calls=%async_computation | async-start | bytes 655360 | tf_op jit(solution)/shard_map/all_to_all | solution.py:836
  10.3 0.0 copy-start
  10.3 10.2 %early_heads_and_sent_kv.1 = (f32[2,640,256]{2,1,0:T(8,128)}, f32[2,640,128]{2,1,0:T(8,128)}, s32[33]{0:T(128)}, s32[99]{0:T(128)}, bf16[4,640,128]{2,1,0:T(8,12...) custom-call(s32[32,64]{1,0:T(8,128)} %bitcast.23, ...), custom_call_target="tpu_custom_call" | custom-call | flops 5368709120 | bytes 8912896 | tf_op jit(solution)/shard_map/early_heads_and_sent_kv/pallas_call | solution.py:454
  20.5 0.9 %all-to-all-done.q_ref = bf16[32,40,128]{2,1,0:T(8,128)(2,1)S(1)} async-done(((bf16[32,40,128]{2,1,0:T(8,128)(2,1)}), bf16[32,40,128]{2,1,0:T(8,128)(2,1)S(1)}, u32[]{:S(2)}, u32[]{:S(2)}) %all-to-all-start) | async-done | bytes 327712 | tf_op jit(solution)/shard_map/all_to_all | solution.py:836
  21.4 0.0 copy-done
  21.4 2.4 %moved_attention.1 = bf16[1408,128]{1,0:T(8,128)(2,1)} custom-call(s32[256]{0:T(256)S(1)} %bitcast.18, bf16[32,40,128]{2,1,0:T(8,128)(2,1)S(1)} %all-to-all-done.q_ref, bf16[16,4,64,128]{3,2,1,0:T(8,128)(2,1)S(1)} %get-tuple-element.30.keys, bf16[16,4,64,128]{3,2,1,0:T(8,128)(2,1)S(1)} %get-tuple-element.31.values), custom_call_target="tpu_custom_call" | custom-call | flops 83886080 | bytes 655360 | tf_op jit(solution)/shard_map/moved_attention/pallas_call | solution.py:724
  23.7 5.1 %all-to-all-start.1 = ((bf16[16,88,128]{2,1,0:T(8,128)(2,1)}), bf16[16,88,128]{2,1,0:T(8,128)(2,1)S(1)}, u32[]{:S(2)}, u32[]{:S(2)}) async-start(bf16[16,88,128]{2,1,0:T(8,128)(2,1)} %bitcast.9), calls=%async_computation.1 | async-start | bytes 720896 | tf_op jit(solution)/shard_map/all_to_all | solution.py:836
  28.9 1.6 %collective-permute-start = (bf16[128,1024]{1,0:T(8,128)(2,1)S(1)}, bf16[128,1024]{1,0:T(8,128)(2,1)S(1)}, u32[]{:S(2)}, u32[]{:S(2)}) collective-permute-start(bf16[128,1024]{1,0:T(8,128)(2,1)S(1)} %bitcast.19), channel_id=1, source_target_pairs={{0,1},{1,0},{2,3},{3,2},{4,5},{5,4},{6,7},{7,6},{8,9},{9,8},{10,11... | collective-permute-start | bytes 786440 | tf_op jit(solution)/shard_map/ppermute | solution.py:852
  30.4 7.9 %late_heads.1 = (f32[2,640,256]{2,1,0:T(8,128)S(1)}, f32[2,640,128]{2,1,0:T(8,128)S(1)}, bf16[4,640,128]{2,1,0:T(8,128)(2,1)S(1)}, bf16[128,2560]{1,0:T(8,128)(2...) custom-call(s32[32,64]{1,0:T(8,128)} %bitcast.24, ...), custom_call_target="tpu_custom_call" | custom-call | flops 4697620480 | bytes 3670016 | tf_op jit(solution)/shard_map/late_heads/pallas_call | solution.py:535
  38.4 0.0 collective-permute-done
  38.4 1.9 %join_new.1 = (bf16[128,1024]{1,0:T(8,128)(2,1)}, f32[64,40,128]{2,1,0:T(8,128)S(1)}, f32[64,40,128]{2,1,0:T(8,128)S(1)}) custom-call(bf16[1,128,1024]{2,1,0:T(8,128)(2,1)S(1)} %bitcast.15, bf16[4,640,128]{2,1,0:T(8,128)(2,1)S(1)} %get-tuple-element.35.packed, bf16[128,2560]{1,0:T(8,128)(2,1)S(1)} %get-tuple-element.36.x, ...), custom_call_target="tpu_custom_call" | custom-call | flops 677642240 | bytes 6553600 | tf_op jit(solution)/shard_map/join_new/pallas_call | solution.py:634
  40.3 0.2 all-to-all-done.1
  40.6 2.1 %join_moved.1 = bf16[64,40,128]{2,1,0:T(8,128)(2,1)} custom-call(s32[33]{0:T(128)} %get-tuple-element.25.owner_hbm, s32[99]{0:T(128)} %get-tuple-element.26.plan_hbm, f32[64,40,128]{2,1,0:T(8,128)S(1)} %get-tuple-element.42.state_ref, f32[64,40,128]{2,1,0:T(8,128)S(1)} %get-tuple-element.43.lse_ref, bf16[1408,128]{1,0:T(8,128)(2,1)S(1)} %bitcast.14), custom_call_target="tpu_custom_call" | custom-call | flops 3276800 | bytes 3276800 | tf_op jit(solution)/shard_map/join_moved/pallas_call | solution.py:806
Async XLA Ops:
  2.9 18.5 %all-to-all-start = ((bf16[32,40,128]{2,1,0:T(8,128)(2,1)}), bf16[32,40,128]{2,1,0:T(8,128)(2,1)S(1)}, u32[]{:S(2)}, u32[]{:S(2)}) async-start(bf16[32,40,128]{2,1,0:T(8,128)(2,1)} %gather_queries.1), calls=%async_computation | async-start | bytes 655360 | tf_op jit(solution)/shard_map/all_to_all | solution.py:836
  10.3 11.1 %copy-start = (s32[256,1]{0,1:T(1,128)S(1)}, s32[256,1]{0,1:T(1,128)}, u32[]{:S(2)}) copy-start(s32[256,1]{0,1:T(1,128)} %param.17) | copy-start | bytes 3076
  23.7 16.8 %all-to-all-start.1 = ((bf16[16,88,128]{2,1,0:T(8,128)(2,1)}), bf16[16,88,128]{2,1,0:T(8,128)(2,1)S(1)}, u32[]{:S(2)}, u32[]{:S(2)}) async-start(bf16[16,88,128]{2,1,0:T(8,128)(2,1)} %bitcast.9), calls=%async_computation.1 | async-start | bytes 720896 | tf_op jit(solution)/shard_map/all_to_all | solution.py:836
  28.9 9.5 %collective-permute-start = (bf16[128,1024]{1,0:T(8,128)(2,1)S(1)}, bf16[128,1024]{1,0:T(8,128)(2,1)S(1)}, u32[]{:S(2)}, u32[]{:S(2)}) collective-permute-start(bf16[128,1024]{1,0:T(8,128)(2,1)S(1)} %bitcast.19), channel_id=1, source_target_pairs={{0,1},{1,0},{2,3},{3,2},{4,5},{5,4},{6,7},{7,6},{8,9},{9,8},{10,11... | collective-permute-start | bytes 786440 | tf_op jit(solution)/shard_map/ppermute | solution.py:852
